TPU v7x, 256 devices: a whole 4x4x8 slice. The times are simulated.
256 devices in a mesh: gr: 32 (over x_lo, z, core), gc: 8 (over y, x_hi).
Axes of the slice: x: 4 (x_hi: 2, x_lo: 2; x = x_hi * 2 + x_lo), y: 4, z: 8, core: 2. Of those that a mesh axis runs over, the one named last changes fastest.
Arguments:
- tile_counts: int32 [32, 8, 1024, 1024], P('gr', 'gc'), may hold values from 0 to 4095, as said below
- row_slot: int32 [32, 8, 1024], P('gr', 'gc'), may hold values from 0 to 1023, each once within a row
- col_slot: int32 [32, 8, 1024], P('gr', 'gc'), may hold values from 0 to 1023, each once within a row
- row_embed: float32 [32, 1024, 256], P('gr', 'gc'), may hold values from -2 to 2
- col_embed: float32 [8, 1024, 256], P('gc', 'gr'), may hold values from -2 to 2
- row_marginal: int32 [32, 1024], P('gr', 'gc'), may hold values from 30 to 2999
- col_marginal: int32 [8, 1024], P('gc', 'gr'), may hold values from 30 to 2999
- total_count: int32 [1], replicated, may hold values from 1048576 to 16777215
Outputs:
- new_rows: float32 [32, 1024, 256], P('gr', 'gc')
- new_cols: float32 [8, 1024, 256], P('gc', 'gr')
Inputs may be any that keep to these rules, and one draw needn't show every extreme that they name: `tile_counts`: each tile's counts, 0 for pairs never seen. `row_slot`: each tile's row slots name every block row once. `col_slot`: each tile's column slots name every block column once.
All inputs are finite; a program needn't handle non-finite values.
Results may differ from a plain program's by a relative error of at most 0.0003.
Values sent between devices are 32-bit elements; how exact they have to be, the bound alone decides.
No kernel may reach another device: no remote copies, remote signals or barrier semaphores. Data moves between devices by JAX's collectives and lax.ppermute only.
A program may use at most 64 MiB of HBM per device.

v0:
```python
import jax
import jax.numpy as jnp
from jax import lax
from jax.sharding import PartitionSpec as P


def cell_gradient(score, counts, base):
    weight = counts.astype(jnp.float32)
    pmi = base + jnp.log(jnp.maximum(weight, 1.0))
    diff = score - pmi
    return jnp.where(counts > 0, (0.1 + 0.25 * jnp.sqrt(weight)) * diff, jax.nn.sigmoid(diff))


def shards(
    tile_counts, row_slot, col_slot, row_embed, col_embed, row_marginal, col_marginal, total_count
):
    log_total = jnp.log(total_count.astype(jnp.float32))[0]
    row_logs = jnp.log(row_marginal.astype(jnp.float32))
    col_logs = jnp.log(col_marginal.astype(jnp.float32))
    gathered, left_logs = (
        lax.all_gather(row_embed, "gc", axis=1, tiled=True),
        lax.all_gather(row_logs, "gc", axis=1, tiled=True),
    )
    row_slots = row_slot[0, 0]
    col_slots = col_slot[0, 0]
    num_rows = row_slots.shape[0]
    num_cols = col_slots.shape[0]
    left_tile = gathered[0][row_slots]
    left_logs_tile = left_logs[0][row_slots]
    inv_rows = (
        jnp.zeros((num_rows,), jnp.int32).at[row_slots].set(jnp.arange(num_rows, dtype=jnp.int32))
    )
    inv_cols = (
        jnp.zeros((num_cols,), jnp.int32).at[col_slots].set(jnp.arange(num_cols, dtype=jnp.int32))
    )
    counts = tile_counts[0, 0]
    col_whole, right_logs = (
        lax.all_gather(col_embed, "gr", axis=1, tiled=True),
        lax.all_gather(col_logs, "gr", axis=1, tiled=True),
    )
    right_tile = col_whole[0][col_slots]
    right_logs_tile = right_logs[0][col_slots]
    base = log_total - left_logs_tile[:, None] - right_logs_tile[None, :]
    score = jnp.dot(left_tile, right_tile.T, precision=lax.Precision.HIGHEST)
    grads = cell_gradient(score, counts, base)
    row_block = jnp.dot(grads, right_tile, precision=lax.Precision.HIGHEST)[inv_rows]
    col_block = jnp.dot(grads.T, left_tile, precision=lax.Precision.HIGHEST)[inv_cols]
    row_grad = lax.psum_scatter(row_block, "gc", scatter_dimension=0, tiled=True)
    col_grad = lax.psum_scatter(col_block, "gr", scatter_dimension=0, tiled=True)
    new_rows = row_embed[0] - 0.001 * row_grad
    new_cols = col_embed[0] - 0.001 * col_grad
    return (new_rows[None], new_cols[None])


def solution(mesh):
    return jax.shard_map(
        shards,
        mesh=mesh,
        in_specs=(
            P("gr", "gc", None, None),
            P("gr", "gc", None),
            P("gr", "gc", None),
            P("gr", "gc", None),
            P("gc", "gr", None),
            P("gr", "gc"),
            P("gc", "gr"),
            P(),
        ),
        out_specs=(P("gr", "gc", None), P("gc", "gr", None)),
        check_vma=False,
    )
```

profile of v0, /device:TPU:32, one launch (start us, length us, event | category | flops | bytes accessed | tf_op | source)
XLA Modules:
  0.0 358.5 jit_solution(3422485646069348638)
XLA Ops:
  7.2 0.0 copy-start.4
  7.2 0.0 copy-start.3
  7.2 0.0 all-gather.3.cloned.1.call-start
  7.2 0.7 all-gather.3.cloned.1.call-update
  7.9 0.0 all-gather.5.cloned.1.call-start
  8.0 0.7 all-gather.5.cloned.1.call-update
  8.7 0.0 reduce-scatter.5.cloned.1.call-start
  9.4 1.3 dynamic-slice
  11.3 0.7 convert_log_fusion
  12.0 23.5 %all_gather.14 = f32[1,1024]{1,0:T(1,128)S(1)} all-gather(f32[1,128]{1,0:T(1,128)S(1)} %convert_log_fusion), channel_id=1, replica_groups=mesh['gr'=32,'gc'=8] {'gc'}, dimensions={1}, use_global_device_ids=true | all-gather | bytes 4608 | tf_op jit(solution)/shard_map/all_gather | solution.py:22
  35.4 0.7 compare_select_fusion.1
  36.1 4.5 %gather_fusion.2 = f32[1024]{0:T(1024)S(1)} fusion(f32[1024]{0:T(1024)S(1)} %bitcast.45, s32[1024]{0:T(1024)S(1)} %broadcast_clamp_fusion.1), kind=kCustom, calls=%fused_computation.2 | custom fusion | bytes 12288 | tf_op jit(solution)/shard_map/gather | solution.py:29
  40.7 0.0 copy-done.4
  40.7 0.1 bitcast_dynamic-update-slice_fusion
  40.8 50.6 %all-reduce = f32[1024]{0:T(1024)S(1)} all-reduce(f32[1024]{0:T(1024)S(1)} %bitcast_dynamic-update-slice_fusion), channel_id=1, replica_groups=mesh['gr'=32,'gc'=8] {'gr'}, use_global_device_ids=true, to_apply=%add | all-reduce | flops 1024 | bytes 8192 | tf_op jit(solution)/shard_map/squeeze | solution.py:42
  91.5 0.0 copy-done.3
  91.5 4.5 %gather_fusion.3 = f32[1024]{0:T(1024)S(1)} fusion(f32[1024]{0:T(1024)S(1)} %all-reduce, s32[1024]{0:T(1024)S(1)} %broadcast_clamp_fusion), kind=kCustom, calls=%fused_computation.3 | custom fusion | bytes 12288 | tf_op jit(solution)/shard_map/gather | solution.py:42
  96.0 4.5 %scatter_custom_fusion.1 = s32[1024]{0:T(1024)S(1)} fusion(s32[1024]{0:T(1024)S(1)} %bitcast.51, s32[1024]{0:T(1024)S(1)} %iota.7, s32[]{:T(128)} %constant.6.clone.1), kind=kCustom, calls=%fused_computation.24 | custom fusion | bytes 4100 | tf_op jit(solution)/shard_map/scatter | solution.py:34
  100.6 0.0 all-gather.3.cloned.1.call-done
  100.6 4.7 %gather_fusion = f32[1024,256]{1,0:T(8,128)S(1)} fusion(f32[1024,256]{1,0:T(8,128)} %bitcast.46, s32[1024]{0:T(1024)S(1)} %broadcast_clamp_fusion.1), kind=kCustom, calls=%fused_computation | custom fusion | bytes 2101248 | tf_op jit(solution)/shard_map/gather | solution.py:28
  105.3 22.9 %all-gather.5.cloned.1.call-done = f32[1,1024,256]{2,1,0:T(8,128)} async-done(((f32[1,32,256]{2,1,0:T(8,128)}), f32[1,1024,256]{2,1,0:T(8,128)}) %all-gather.5.cloned.1.call-update) | async-done | bytes 1048592 | tf_op jit(solution)/shard_map/all_gather | solution.py:38
  128.2 4.7 %gather_fusion.1 = f32[1024,256]{1,0:T(8,128)S(1)} fusion(f32[1024,256]{1,0:T(8,128)} %bitcast.47, s32[1024]{0:T(1024)S(1)} %broadcast_clamp_fusion), kind=kCustom, calls=%fused_computation.1 | custom fusion | bytes 2101248 | tf_op jit(solution)/shard_map/gather | solution.py:41
  132.9 9.9 %fusion.1 = f32[1024,1024]{1,0:T(8,128)S(1)} fusion(s32[1,1,1024,1024]{3,2,1,0:T(8,128)} %param.8, f32[1024,256]{1,0:T(8,128)S(1)} %gather_fusion, f32[1024,256]{1,0:T(8,128)S(1)} %gather_fusion.1, f32[1024]{0:T(1024)S(1)} %gather_fusion.3, f32[1024]{0:T(1024)S(1)} %broadcast_subtract_fusion), kind=kOutput, calls=%fused_computation.11 | convolution fusion | flops 3234856960 | bytes 10493952 | tf_op jit(solution)/shard_map/dot_general | solution.py:44
  142.8 0.0 copy-start
  142.8 1.9 copy-done
  144.8 6.8 %fusion.11 = f32[1024,256]{1,0:T(8,128)S(1)} fusion(f32[1024,1024]{1,0:T(8,128)S(1)} %fusion.1, f32[1024,256]{1,0:T(8,128)S(1)} %gather_fusion), kind=kOutput, calls=%fused_computation.32 | convolution fusion | flops 3221225472 | bytes 6291456 | tf_op jit(solution)/shard_map/dot_general | solution.py:47
  151.6 4.7 %gather_fusion.5 = f32[1024,256]{1,0:T(8,128)} fusion(f32[1024,256]{1,0:T(8,128)S(1)} %fusion.11, s32[1024]{0:T(1024)S(1)} %fusion.5), kind=kCustom, calls=%fused_computation.5 | custom fusion | bytes 2101248 | tf_op jit(solution)/shard_map/gather | solution.py:47
  156.3 0.0 reduce-scatter.5.cloned.1.call-update
  156.3 0.3 reduce-scatter.3.cloned.1.call-start
  156.6 4.3 %scatter_custom_fusion = s32[1024]{0:T(1024)S(1)} fusion(s32[1024]{0:T(1024)S(1)} %bitcast.49, s32[1024]{0:T(1024)S(1)} %iota.6, s32[]{:T(128)} %constant.6.clone.1), kind=kCustom, calls=%fused_computation.26 | custom fusion | bytes 4100 | tf_op jit(solution)/shard_map/scatter | solution.py:31
  161.0 5.2 %fusion.10 = f32[1024,256]{1,0:T(8,128)S(1)} fusion(f32[1024,1024]{1,0:T(8,128)} %copy-done, f32[1024,256]{1,0:T(8,128)S(1)} %gather_fusion.1), kind=kOutput, calls=%fused_computation.31 | convolution fusion | flops 3221225472 | bytes 6291456 | tf_op jit(solution)/shard_map/dot_general | solution.py:46
  166.2 0.0 copy-start.2
  166.2 0.0 copy-start.1
  166.2 4.7 %gather_fusion.4 = f32[1024,256]{1,0:T(8,128)} fusion(f32[1024,256]{1,0:T(8,128)S(1)} %fusion.10, s32[1024]{0:T(1024)S(1)} %fusion.4), kind=kCustom, calls=%fused_computation.4 | custom fusion | bytes 2101248 | tf_op jit(solution)/shard_map/gather | solution.py:46
  170.9 0.0 reduce-scatter.3.cloned.1.call-update
  170.9 98.7 %reduce-scatter.5.cloned.1.call-done = f32[32,256]{1,0:T(8,128)} async-done(((f32[1024,256]{1,0:T(8,128)}), f32[32,256]{1,0:T(8,128)}) %reduce-scatter.5.cloned.1.call-update) | async-done | bytes 32784 | tf_op jit(solution)/shard_map/reduce_scatter | solution.py:49
  269.7 0.0 copy-done.2
  269.7 1.4 fusion.3
  271.0 79.4 %reduce-scatter.3.cloned.1.call-done = f32[128,256]{1,0:T(8,128)} async-done(((f32[1024,256]{1,0:T(8,128)}), f32[128,256]{1,0:T(8,128)}) %reduce-scatter.3.cloned.1.call-update) | async-done | bytes 131088 | tf_op jit(solution)/shard_map/reduce_scatter | solution.py:48
  350.4 0.0 copy-done.1
  350.4 1.6 fusion.2
  (9 shorter events, 0.0 us)
Async XLA Ops:
  7.2 33.5 %copy-start.4 = (s32[1,32]{1,0:T(1,128)S(1)}, s32[1,32]{1,0:T(1,128)}, u32[]{:S(2)}) copy-start(s32[1,32]{1,0:T(1,128)} %param.14) | copy-start | bytes 388
  7.2 84.3 %copy-start.3 = (s32[1,1,1024]{2,1,0:T(1,128)S(1)}, s32[1,1,1024]{2,1,0:T(1,128)}, u32[]{:S(2)}) copy-start(s32[1,1,1024]{2,1,0:T(1,128)} %param.10) | copy-start | bytes 12292
  7.2 93.4 %all-gather.3.cloned.1.call-start = ((), (), s32[]{:S(2)}) async-start(), calls=%async_computation.2 | async-start | bytes 1179648 | tf_op jit(solution)/shard_map/all_gather | solution.py:21
  7.9 120.3 %all-gather.5.cloned.1.call-start = ((), (), s32[]{:S(2)}) async-start(), calls=%async_computation.3 | async-start | bytes 1081344 | tf_op jit(solution)/shard_map/all_gather | solution.py:38
  8.7 261.0 %reduce-scatter.5.cloned.1.call-start = ((), (), s32[]{:S(2)}) async-start(), calls=%async_computation.5 | async-start | bytes 1081344 | tf_op jit(solution)/shard_map/reduce_scatter | solution.py:49
  142.8 1.9 copy-start
  156.3 194.1 %reduce-scatter.3.cloned.1.call-start = ((), (), s32[]{:S(2)}) async-start(), calls=%async_computation.4 | async-start | bytes 1179648 | tf_op jit(solution)/shard_map/reduce_scatter | solution.py:48
  166.2 103.5 %copy-start.2 = (f32[1,32,256]{2,1,0:T(8,128)S(1)}, f32[1,32,256]{2,1,0:T(8,128)}, u32[]{:S(2)}) copy-start(f32[1,32,256]{2,1,0:T(8,128)} %param.12) | copy-start | bytes 98308
  166.2 184.2 %copy-start.1 = (f32[1,128,256]{2,1,0:T(8,128)S(1)}, f32[1,128,256]{2,1,0:T(8,128)}, u32[]{:S(2)}) copy-start(f32[1,128,256]{2,1,0:T(8,128)} %param.11) | copy-start | bytes 393220
Sparse Core Ops, SparseCore 0:
  10.7 53.9 all-gather.2
  66.5 61.6 all-gather.4
  156.5 113.1 reduce-scatter.4
  273.9 76.4 reduce-scatter.2
where the time goes:
time: 359 us
  waiting for transfers between devices  202 us (56%)
  blocking collectives  74.1 us (21%)
  local copies, waits for them, and re-layouts  39.9 us (11%)
  matrix products  22 us (6%)
  between operations  15.3 us (4%)
  other arithmetic  4.46 us (1%)
    reduce_scatter x1, waiting for transfers between devices, shards(): lax.psum_scatter(col_block, 'gr', scatter_dimension=0, tiled=True)  98.7 us
    reduce_scatter x1, waiting for transfers between devices, shards(): lax.psum_scatter(row_block, 'gc', scatter_dimension=0, tiled=True)  79.4 us
    squeeze x1, blocking collectives, shards(): right_logs_tile = right_logs[0][col_slots]  50.6 us
    all_gather x1, blocking collectives, shards(): lax.all_gather(row_logs, 'gc', axis=1, tiled=True)  23.5 us
    all_gather x1, waiting for transfers between devices, shards(): lax.all_gather(col_embed, 'gr', axis=1, tiled=True)  22.9 us
    dot_general x1, matrix products, shards(): score = jnp.dot(left_tile, right_tile.T, precision=lax.Precision.HIGHEST)  9.94 us
  transfers between devices with their start and end apart: 4, of which 3 were waited for; matrix products, arithmetic and copies ran while one was open for 10% of the time, Pallas kernels for 0%

commit v1 on v0

v1 whole, which is shorter than its diff:
```python
import functools

import jax
import jax.numpy as jnp
from jax import lax
from jax.experimental import pallas as pl
from jax.experimental.pallas import tpu as pltpu
from jax.sharding import PartitionSpec as P

F32 = jnp.float32
BF16 = jnp.bfloat16
N = 1024
D = 256
NN = ((1,), (0,))
NT = ((1,), (1,))
VMEM = pl.BlockSpec(memory_space=pltpu.VMEM)
SMEM = pl.BlockSpec(memory_space=pltpu.SMEM)


def dot(a, b, dims):
    return lax.dot_general(a, b, (dims, ((), ())), preferred_element_type=F32)


def split(v):
    hi = v.astype(BF16)
    return hi, (v - hi.astype(F32)).astype(BF16)


def shift(x, axis, k):
    if axis == "gc":
        pairs = [(i, (i + k) % 8) for i in range(8)]
        return lax.ppermute(x, "gc", pairs)
    pairs = [(i, (i & 17) | (((((i >> 1) & 7) + k) % 8) << 1)) for i in range(32)]
    return lax.ppermute(x, "gr", pairs)


def swap(x, mask):
    return lax.ppermute(x, "gr", [(i, i ^ mask) for i in range(32)])


def prep_body(pos, cnt, rs, cs, w, lx, chi, clo, bt):
    gc, gr = pos[0], pos[1]
    rows = rs[...]
    rows = (((gc - (rows >> 7)) & 7) << 7) | (rows & 127)
    cols = cs[...]
    owner = cols >> 5
    cols = (
        (((owner ^ gr) & 1) << 9)
        | ((((gr >> 1) - (owner >> 1)) & 7) << 6)
        | (((owner ^ gr) & 16) << 1)
        | (cols & 31)
    )
    T = 256

    def load(t, _):
        s = pl.ds(pl.multiple_of(t * T, T), T)
        c = cnt[s, :]
        hi = c >> 6
        chi[s, :] = hi.astype(F32).astype(BF16)
        clo[s, :] = (c & 63).astype(F32).astype(BF16)
        j = lax.broadcasted_iota(jnp.int32, (T, N), 0) + t * T
        bt[s, :] = jnp.where(j == cols, 1.0, 0.0).astype(BF16)
        return 0

    lax.fori_loop(0, N // T, load, 0)

    def step(t, _):
        s = pl.ds(pl.multiple_of(t * T, T), T)
        i = lax.broadcasted_iota(jnp.int32, (T, N), 0) + t * T
        a = jnp.where(i == rows, 1.0, 0.0).astype(BF16)
        hi = dot(a, chi[...], NN).astype(BF16)
        lo = dot(a, clo[...], NN).astype(BF16)
        x = dot(hi, bt[...], NT) * 64.0 + dot(lo, bt[...], NT)
        w[s, :] = jnp.where(x > 0, 0.1 + 0.25 * jnp.sqrt(x), 0.0)
        lx[s, :] = jnp.log(jnp.maximum(x, 1.0))
        return 0

    lax.fori_loop(0, N // T, step, 0)


def prep(pos, cnt, rs, cs):
    return pl.pallas_call(
        prep_body,
        out_shape=[jax.ShapeDtypeStruct((N, N), F32)] * 2,
        in_specs=[SMEM, VMEM, VMEM, VMEM],
        out_specs=[VMEM, VMEM],
        scratch_shapes=[pltpu.VMEM((N, N), BF16)] * 3,
        compiler_params=pltpu.CompilerParams(vmem_limit_bytes=48 << 20),
        name="prep",
    )(pos, cnt, rs, cs)


def main_body(*refs):
    lt, w, lx = refs[:3]
    left = refs[3:11]
    right = refs[11:13]
    row_out = refs[13:21]
    col_out = refs[21:23]
    rcat, bc, colt = refs[23:]
    for c in range(2):
        for z in range(8):
            at = c * 512 + z * 64
            hi, lo = split(right[c][z * 72 : z * 72 + 64, :])
            rcat[at : at + 64, :D] = hi
            rcat[at : at + 64, D:] = lo
            bc[:, at : at + 64] = right[c][z * 72 + 64 : z * 72 + 65, :64] - lt[0]
    br = jnp.concatenate([left[k][128:129, :128] for k in range(8)], 0).T
    for k in range(4):
        s = slice(256 * k, 256 * (k + 1))
        lv = jnp.concatenate([left[2 * k][:128, :], left[2 * k + 1][:128, :]], 0)
        bv = jnp.concatenate([br[:, 2 * k : 2 * k + 1], br[:, 2 * k + 1 : 2 * k + 2]], 0)
        lh, ll = split(lv)
        score = dot(lh, rcat[:, :D], NT) + dot(lh, rcat[:, D:], NT) + dot(ll, rcat[:, :D], NT)
        d = score + bv + bc[...] - lx[s, :]
        wv = w[s, :]
        g = jnp.where(wv > 0, wv * d, 0.5 * jnp.tanh(0.5 * d) + 0.5)
        gh, gl = split(g)
        rr = dot(gh, rcat[...], NN)
        rr = rr[:, :D] + rr[:, D:] + dot(gl, rcat[:, :D], NN)
        row_out[2 * k][...] = rr[:128]
        row_out[2 * k + 1][...] = rr[128:]
        lt_ = jnp.concatenate([lh, ll], 1).T
        cc = dot(lt_, gh, NN)
        cc = cc[:D] + cc[D:] + dot(lt_[:D], gl, NN)
        if k == 0:
            colt[...] = cc
        else:
            colt[...] += cc
    col = colt[...].T
    col_out[0][...] = col[:512]
    col_out[1][...] = col[512:]


def main(lt, w, lx, left, right):
    return pl.pallas_call(
        main_body,
        out_shape=[jax.ShapeDtypeStruct((128, D), F32)] * 8
        + [jax.ShapeDtypeStruct((512, D), F32)] * 2,
        in_specs=[SMEM] + [VMEM] * 12,
        out_specs=[VMEM] * 10,
        scratch_shapes=[
            pltpu.VMEM((N, 2 * D), BF16),
            pltpu.VMEM((1, N), F32),
            pltpu.VMEM((D, N), F32),
        ],
        compiler_params=pltpu.CompilerParams(vmem_limit_bytes=48 << 20),
        name="main",
    )(lt, w, lx, *left, *right)


def halves_body(own, got, *outs):
    for z in range(8):
        s = slice(64 * z, 64 * z + 64)
        outs[z][...] = own[s, :] + got[s, :]


def halves(own, got):
    return pl.pallas_call(
        halves_body,
        out_shape=[jax.ShapeDtypeStruct((64, D), F32)] * 8,
        in_specs=[VMEM] * 2,
        out_specs=[VMEM] * 8,
        name="halves",
    )(own, got)


def with_logs(embed, marginal):
    logs = jnp.log(marginal.astype(F32))
    return jnp.concatenate([embed, jnp.pad(logs[None], ((0, 7), (0, D - logs.shape[0])))], 0)


def shards(
    tile_counts, row_slot, col_slot, row_embed, col_embed, row_marginal, col_marginal, total_count
):
    log_total = jnp.log(total_count.astype(F32))
    pos = jnp.stack([lax.axis_index("gc"), lax.axis_index("gr")]).astype(jnp.int32)
    own = with_logs(col_embed[0], col_marginal[0])
    other = swap(own, 16)
    pair = jnp.concatenate(
        [own[:32], other[:32], own[32:] + jnp.roll(other[32:], 32, 1)], 0
    )
    rows = with_logs(row_embed[0], row_marginal[0])
    left = [rows] + [shift(rows, "gc", k) for k in range(1, 8)]
    along = jnp.concatenate([pair] + [shift(pair, "gr", k) for k in range(1, 8)], 0)
    right = [along, swap(along, 1)]
    w, lx = prep(pos, tile_counts[0, 0], row_slot[0], col_slot[0])
    outs = main(log_total, w, lx, left, right)
    row_grad = outs[0]
    back = [shift(outs[k], "gc", -k) for k in range(1, 8)]
    pieces = halves(outs[8], swap(outs[9], 1))
    col_pair = pieces[0]
    for k in range(1, 8):
        col_pair = col_pair + shift(pieces[k], "gr", -k)
    for b in back:
        row_grad = row_grad + b
    col_grad = col_pair[:32] + swap(col_pair[32:], 16)
    new_rows = row_embed[0] - 0.001 * row_grad
    new_cols = col_embed[0] - 0.001 * col_grad
    return (new_rows[None], new_cols[None])


def solution(mesh):
    return jax.shard_map(
        shards,
        mesh=mesh,
        in_specs=(
            P("gr", "gc", None, None),
            P("gr", "gc", None),
            P("gr", "gc", None),
            P("gr", "gc", None),
            P("gc", "gr", None),
            P("gr", "gc"),
            P("gc", "gr"),
            P(),
        ),
        out_specs=(P("gr", "gc", None), P("gc", "gr", None)),
        check_vma=False,
    )
```

time: 359 us -> 128 us (0.36)
  waiting for transfers between devices: 202 us -> 29.2 us
  blocking collectives: 74.1 us -> 0 us
  starting transfers between devices: 0.38 us -> 57.6 us
  local copies, waits for them, and re-layouts: 39.9 us -> 5.91 us
  Pallas kernels: 0 us -> 26.8 us
  matrix products: 22 us -> 0 us
  between operations: 15.3 us -> 1.51 us
    reduce_scatter x2 -> x0, waiting for transfers between devices: 178 us -> none  [the longest x1 98.7 us: shards(): lax.psum_scatter(col_block, 'gr', scatter_dimension=0, tiled=True)]
    ppermute x0 -> x32, starting transfers between devices: none -> 57.6 us  [the longest x14 28.1 us: shift(): return lax.ppermute(x, 'gr', pairs)]
    squeeze x1 -> x0, blocking collectives: 50.6 us -> none  [shards(): right_logs_tile = right_logs[0][col_slots]]
    ppermute x0 -> x32, waiting for transfers between devices: none -> 29.2 us  [the longest x14 16.6 us: shift(): return lax.ppermute(x, 'gr', pairs)]
    gather x6 -> x0, local copies, waits for them, and re-layouts: 27.8 us -> none  [the longest x1 4.71 us: shards(): jnp.dot(grads.T, left_tile, precision=lax.Precision.HIGHEST)[inv_cols]]
    pallas_call x0 -> x3, Pallas kernels: none -> 26.8 us  [the longest x1 15.5 us: prep(): pl.pallas_call(prep_body, out_shape=[jax.ShapeDtypeStruct((N, N), F32)] *...]
    all_gather x1 -> x0, blocking collectives: 23.5 us -> none  [shards(): lax.all_gather(row_logs, 'gc', axis=1, tiled=True)]
    all_gather x2 -> x0, waiting for transfers between devices: 22.9 us -> none  [the longest x1 22.9 us: shards(): lax.all_gather(col_embed, 'gr', axis=1, tiled=True)]
  transfers between devices with their start and end apart: 4 -> 32, of which waited for: 3 -> 9; matrix products, arithmetic and copies ran while one was open for 10% -> 3% of each run, Pallas kernels for 0% -> 14%
where the time goes in v1:
time: 128 us; the launch traced here: 127 us
  starting transfers between devices  57.6 us (45%)
  waiting for transfers between devices  29.2 us (23%)
  Pallas kernels  26.8 us (21%)
  other arithmetic  6.15 us (5%)
  local copies, waits for them, and re-layouts  5.91 us (5%)
  between operations  1.51 us (1%)
    ppermute x14, starting transfers between devices, shift(): return lax.ppermute(x, 'gr', pairs)  28.1 us
    ppermute x14, starting transfers between devices, shift(): return lax.ppermute(x, 'gc', pairs)  26.3 us
    ppermute x14, waiting for transfers between devices, shift(): return lax.ppermute(x, 'gr', pairs)  16.6 us
    pallas_call x1, Pallas kernels, prep(): pl.pallas_call(prep_body, out_shape=[jax.ShapeDtypeStruct((N, N), F32)] *...  15.5 us
    ppermute x14, waiting for transfers between devices, shift(): return lax.ppermute(x, 'gc', pairs)  10.8 us
    pallas_call x1, Pallas kernels, main(): pl.pallas_call(main_body, out_shape=[jax.ShapeDtypeStruct((128, D), F32)]...  9.28 us
    unnamed x21, local copies, waits for them, and re-layouts  5.81 us
    ppermute x4, starting transfers between devices, swap(): return lax.ppermute(x, 'gr', [(i, i ^ mask) for i in range(32)])  3.17 us
  transfers between devices with their start and end apart: 32, of which 9 were waited for; matrix products, arithmetic and copies ran while one was open for 3% of the time, Pallas kernels for 14%

profile of v1, /device:TPU:32, one launch (start us, length us, event | category | flops | bytes accessed | tf_op | source)
XLA Modules:
  0.0 127.1 jit_solution(13811818055578453378)
XLA Ops:
  0.6 0.7 convert_log_fusion
  1.3 0.8 pad_maximum_fusion.1
  2.1 1.5 %collective-permute-start.7 = (f32[40,256]{1,0:T(8,128)S(1)}, f32[40,256]{1,0:T(8,128)S(1)}, u32[]{:S(2)}, u32[]{:S(2)}) collective-permute-start(f32[40,256]{1,0:T(8,128)S(1)} %pad_maximum_fusion.1), channel_id=1, source_target_pairs={{0,128},{8,136},{16,144},{24,152},{32,160},{40,168},{48,176},{56,1... | collective-permute-start | bytes 122888 | tf_op jit(solution)/shard_map/ppermute | solution.py:38
  3.6 0.8 constant_dynamic-update-slice_fusion.9
  4.3 1.8 %collective-permute-done.7 = f32[40,256]{1,0:T(8,128)S(1)} collective-permute-done((f32[40,256]{1,0:T(8,128)S(1)}, f32[40,256]{1,0:T(8,128)S(1)}, u32[]{:S(2)}, u32[]{:S(2)}) %collective-permute-start.7) | collective-permute-done | bytes 40992 | tf_op jit(solution)/shard_map/ppermute | solution.py:38
  6.2 0.8 pad_maximum_fusion
  7.0 1.9 %collective-permute-start.8 = (f32[72,256]{1,0:T(8,128)S(1)}, f32[72,256]{1,0:T(8,128)S(1)}, u32[]{:S(2)}, u32[]{:S(2)}) collective-permute-start(f32[72,256]{1,0:T(8,128)S(1)} %pad_maximum_fusion), channel_id=1, source_target_pairs={{0,16},{8,24},{16,32},{24,40},{32,48},{40,56},{48,64},{56,72},{64,... | collective-permute-start | bytes 221192 | tf_op jit(solution)/shard_map/ppermute | solution.py:34
  9.0 5.4 %collective-permute-start.13 = (f32[72,256]{1,0:T(8,128)S(1)}, f32[72,256]{1,0:T(8,128)S(1)}, u32[]{:S(2)}, u32[]{:S(2)}) collective-permute-start(f32[72,256]{1,0:T(8,128)S(1)} %pad_maximum_fusion), channel_id=1, source_target_pairs={{0,96},{8,104},{16,112},{24,120},{32,0},{40,8},{48,16},{56,24},{64... | collective-permute-start | bytes 221192 | tf_op jit(solution)/shard_map/ppermute | solution.py:34
  14.4 3.1 %collective-permute-start.12 = (f32[72,256]{1,0:T(8,128)S(1)}, f32[72,256]{1,0:T(8,128)S(1)}, u32[]{:S(2)}, u32[]{:S(2)}) collective-permute-start(f32[72,256]{1,0:T(8,128)S(1)} %pad_maximum_fusion), channel_id=1, source_target_pairs={{0,80},{8,88},{16,96},{24,104},{32,112},{40,120},{48,0},{56,8},{64... | collective-permute-start | bytes 221192 | tf_op jit(solution)/shard_map/ppermute | solution.py:34
  17.5 1.4 %collective-permute-start.11 = (f32[72,256]{1,0:T(8,128)S(1)}, f32[72,256]{1,0:T(8,128)S(1)}, u32[]{:S(2)}, u32[]{:S(2)}) collective-permute-start(f32[72,256]{1,0:T(8,128)S(1)} %pad_maximum_fusion), channel_id=1, source_target_pairs={{0,64},{8,72},{16,80},{24,88},{32,96},{40,104},{48,112},{56,120},{... | collective-permute-start | bytes 221192 | tf_op jit(solution)/shard_map/ppermute | solution.py:34
  19.0 0.9 collective-permute-start.9
  19.9 7.3 %collective-permute-done.9 = f32[72,256]{1,0:T(8,128)S(1)} collective-permute-done((f32[72,256]{1,0:T(8,128)S(1)}, f32[72,256]{1,0:T(8,128)S(1)}, u32[]{:S(2)}, u32[]{:S(2)}) %collective-permute-start.9) | collective-permute-done | bytes 73760 | tf_op jit(solution)/shard_map/ppermute | solution.py:34
  27.2 1.3 %collective-permute-start.10 = (f32[72,256]{1,0:T(8,128)S(1)}, f32[72,256]{1,0:T(8,128)S(1)}, u32[]{:S(2)}, u32[]{:S(2)}) collective-permute-start(f32[72,256]{1,0:T(8,128)S(1)} %pad_maximum_fusion), channel_id=1, source_target_pairs={{0,48},{8,56},{16,64},{24,72},{32,80},{40,88},{48,96},{56,104},{64... | collective-permute-start | bytes 221192 | tf_op jit(solution)/shard_map/ppermute | solution.py:34
  28.5 6.1 %collective-permute-done.10 = f32[72,256]{1,0:T(8,128)S(1)} collective-permute-done((f32[72,256]{1,0:T(8,128)S(1)}, f32[72,256]{1,0:T(8,128)S(1)}, u32[]{:S(2)}, u32[]{:S(2)}) %collective-permute-start.10) | collective-permute-done | bytes 73760 | tf_op jit(solution)/shard_map/ppermute | solution.py:34
  34.8 0.7 convert_log_fusion.1
  35.4 0.9 select_maximum_fusion.refs_3_
  36.4 5.6 %collective-permute-start.6 = (f32[136,256]{1,0:T(8,128)S(1)}, f32[136,256]{1,0:T(8,128)S(1)}, u32[]{:S(2)}, u32[]{:S(2)}) collective-permute-start(f32[136,256]{1,0:T(8,128)S(1)} %select_maximum_fusion.refs_3_), channel_id=1, source_target_pairs={{0,7},{1,0},{2,1},{3,2},{4,3},{5,4},{6,5},{7,6},{8,15},{9,8},{10,9... | collective-permute-start | bytes 417800 | tf_op jit(solution)/shard_map/ppermute | solution.py:32
  41.9 0.7 collective-permute-start.5
  43.1 2.9 %collective-permute-start.3 = (f32[136,256]{1,0:T(8,128)S(1)}, f32[136,256]{1,0:T(8,128)S(1)}, u32[]{:S(2)}, u32[]{:S(2)}) collective-permute-start(f32[136,256]{1,0:T(8,128)S(1)} %select_maximum_fusion.refs_3_), channel_id=1, source_target_pairs={{0,4},{1,5},{2,6},{3,7},{4,0},{5,1},{6,2},{7,3},{8,12},{9,13},{10,... | collective-permute-start | bytes 417800 | tf_op jit(solution)/shard_map/ppermute | solution.py:32
  46.0 3.1 %collective-permute-start.2 = (f32[136,256]{1,0:T(8,128)S(1)}, f32[136,256]{1,0:T(8,128)S(1)}, u32[]{:S(2)}, u32[]{:S(2)}) collective-permute-start(f32[136,256]{1,0:T(8,128)S(1)} %select_maximum_fusion.refs_3_), channel_id=1, source_target_pairs={{0,3},{1,4},{2,5},{3,6},{4,7},{5,0},{6,1},{7,2},{8,11},{9,12},{10,... | collective-permute-start | bytes 417800 | tf_op jit(solution)/shard_map/ppermute | solution.py:32
  49.1 5.3 %collective-permute-done.5.refs_9_ = f32[136,256]{1,0:T(8,128)S(1)} collective-permute-done((f32[136,256]{1,0:T(8,128)S(1)}, f32[136,256]{1,0:T(8,128)S(1)}, u32[]{:S(2)}, u32[]{:S(2)}) %collective-permute-start.5) | collective-permute-done | bytes 139296 | tf_op jit(solution)/shard_map/ppermute | solution.py:32
  55.2 0.7 copy-done.2
  55.9 0.7 copy-done.3
  56.6 15.5 %prep.1 = (f32[1024,1024]{1,0:T(8,128)S(1)}, f32[1024,1024]{1,0:T(8,128)}) custom-call(s32[2]{0:T(128)S(1)} %pad_add_fusion.pos, s32[1024,1024]{1,0:T(8,128)} %bitcast.16, s32[1,1024]{1,0:T(1,128)S(1)} %bitcast.14, s32[1,1024]{1,0:T(1,128)S(1)} %bitcast.15), custom_call_target="tpu_custom_call" | custom-call | tf_op jit(solution)/shard_map/prep/pallas_call | solution.py:82
  72.1 2.0 %copy-done = f32[1024,1024]{1,0:T(8,128)} copy-done((f32[1024,1024]{1,0:T(8,128)}, f32[1024,1024]{1,0:T(8,128)S(1)}, u32[]{:S(2)}) %copy-start) | copy-done | bytes 4194328
  74.2 9.3 %main.1 = (f32[128,256]{1,0:T(8,128)S(1)}, f32[128,256]{1,0:T(8,128)S(1)}, f32[128,256]{1,0:T(8,128)S(1)}, f32[128,256]{1,0:T(8,128)S(1)}, f32[128,256]{1,0:T(8,...) custom-call(f32[1]{0:T(128)S(6)} %log.11.refs_0_, ...), custom_call_target="tpu_custom_call" | custom-call | tf_op jit(solution)/shard_map/main/pallas_call | solution.py:135
  83.5 0.8 copy-done.1
  84.2 5.6 %collective-permute-start.16 = (f32[128,256]{1,0:T(8,128)S(1)}, f32[128,256]{1,0:T(8,128)S(1)}, u32[]{:S(2)}, u32[]{:S(2)}) collective-permute-start(f32[128,256]{1,0:T(8,128)S(1)} %get-tuple-element.25), channel_id=1, source_target_pairs={{0,7},{1,0},{2,1},{3,2},{4,3},{5,4},{6,5},{7,6},{8,15},{9,8},{10,9... | collective-permute-start | bytes 393224 | tf_op jit(solution)/shard_map/ppermute | solution.py:32
  89.9 2.0 %collective-permute-start.17 = (f32[128,256]{1,0:T(8,128)S(1)}, f32[128,256]{1,0:T(8,128)S(1)}, u32[]{:S(2)}, u32[]{:S(2)}) collective-permute-start(f32[128,256]{1,0:T(8,128)S(1)} %get-tuple-element.26), channel_id=1, source_target_pairs={{0,6},{1,7},{2,0},{3,1},{4,2},{5,3},{6,4},{7,5},{8,14},{9,15},{10,... | collective-permute-start | bytes 393224 | tf_op jit(solution)/shard_map/ppermute | solution.py:32
  91.9 0.8 copy-done.5
  92.7 2.0 %halves.1 = (f32[64,256]{1,0:T(8,128)}, f32[64,256]{1,0:T(8,128)}, f32[64,256]{1,0:T(8,128)}, f32[64,256]{1,0:T(8,128)}, f32[64,256]{1,0:T(8,128)}, /*index=5*/f...) custom-call(f32[512,256]{1,0:T(8,128)} %copy-done.1, f32[512,256]{1,0:T(8,128)} %copy-done.5), custom_call_target="tpu_custom_call" | custom-call | tf_op jit(solution)/shard_map/halves/pallas_call | solution.py:158
  94.7 1.8 %collective-permute-start.24 = (f32[64,256]{1,0:T(8,128)}, f32[64,256]{1,0:T(8,128)S(1)}, u32[]{:S(2)}, u32[]{:S(2)}) collective-permute-start(f32[64,256]{1,0:T(8,128)} %get-tuple-element.35), channel_id=1, source_target_pairs={{0,112},{8,120},{16,0},{24,8},{32,16},{40,24},{48,32},{56,40},{64,... | collective-permute-start | bytes 196616 | tf_op jit(solution)/shard_map/ppermute | solution.py:34
  96.5 2.7 %collective-permute-start.26 = (f32[64,256]{1,0:T(8,128)}, f32[64,256]{1,0:T(8,128)S(1)}, u32[]{:S(2)}, u32[]{:S(2)}) collective-permute-start(f32[64,256]{1,0:T(8,128)} %get-tuple-element.37), channel_id=1, source_target_pairs={{0,80},{8,88},{16,96},{24,104},{32,112},{40,120},{48,0},{56,8},{64... | collective-permute-start | bytes 196616 | tf_op jit(solution)/shard_map/ppermute | solution.py:34
  99.2 3.3 %collective-permute-start.27 = (f32[64,256]{1,0:T(8,128)}, f32[64,256]{1,0:T(8,128)S(1)}, u32[]{:S(2)}, u32[]{:S(2)}) collective-permute-start(f32[64,256]{1,0:T(8,128)} %get-tuple-element.38), channel_id=1, source_target_pairs={{0,64},{8,72},{16,80},{24,88},{32,96},{40,104},{48,112},{56,120},{... | collective-permute-start | bytes 196616 | tf_op jit(solution)/shard_map/ppermute | solution.py:34
  102.5 1.7 %collective-permute-start.28 = (f32[64,256]{1,0:T(8,128)}, f32[64,256]{1,0:T(8,128)S(1)}, u32[]{:S(2)}, u32[]{:S(2)}) collective-permute-start(f32[64,256]{1,0:T(8,128)} %get-tuple-element.39), channel_id=1, source_target_pairs={{0,48},{8,56},{16,64},{24,72},{32,80},{40,88},{48,96},{56,104},{64... | collective-permute-start | bytes 196616 | tf_op jit(solution)/shard_map/ppermute | solution.py:34
  104.2 2.4 %collective-permute-start.29 = (f32[64,256]{1,0:T(8,128)}, f32[64,256]{1,0:T(8,128)S(1)}, u32[]{:S(2)}, u32[]{:S(2)}) collective-permute-start(f32[64,256]{1,0:T(8,128)} %get-tuple-element.40), channel_id=1, source_target_pairs={{0,32},{8,40},{16,48},{24,56},{32,64},{40,72},{48,80},{56,88},{64,... | collective-permute-start | bytes 196616 | tf_op jit(solution)/shard_map/ppermute | solution.py:34
  106.6 2.0 %collective-permute-start.30 = (f32[64,256]{1,0:T(8,128)}, f32[64,256]{1,0:T(8,128)S(1)}, u32[]{:S(2)}, u32[]{:S(2)}) collective-permute-start(f32[64,256]{1,0:T(8,128)} %get-tuple-element.41), channel_id=1, source_target_pairs={{0,16},{8,24},{16,32},{24,40},{32,48},{40,56},{48,64},{56,72},{64,... | collective-permute-start | bytes 196616 | tf_op jit(solution)/shard_map/ppermute | solution.py:34
  108.6 1.3 %collective-permute-start.18 = (f32[128,256]{1,0:T(8,128)S(1)}, f32[128,256]{1,0:T(8,128)S(1)}, u32[]{:S(2)}, u32[]{:S(2)}) collective-permute-start(f32[128,256]{1,0:T(8,128)S(1)} %get-tuple-element.27), channel_id=1, source_target_pairs={{0,5},{1,6},{2,7},{3,0},{4,1},{5,2},{6,3},{7,4},{8,13},{9,14},{10,... | collective-permute-start | bytes 393224 | tf_op jit(solution)/shard_map/ppermute | solution.py:32
  110.4 1.5 %collective-permute-start.19 = (f32[128,256]{1,0:T(8,128)S(1)}, f32[128,256]{1,0:T(8,128)S(1)}, u32[]{:S(2)}, u32[]{:S(2)}) collective-permute-start(f32[128,256]{1,0:T(8,128)S(1)} %get-tuple-element.28), channel_id=1, source_target_pairs={{0,4},{1,5},{2,6},{3,7},{4,0},{5,1},{6,2},{7,3},{8,12},{9,13},{10,... | collective-permute-start | bytes 393224 | tf_op jit(solution)/shard_map/ppermute | solution.py:32
  112.6 0.6 collective-permute-start.20
  113.2 2.2 %collective-permute-done.29 = f32[64,256]{1,0:T(8,128)S(1)} collective-permute-done((f32[64,256]{1,0:T(8,128)}, f32[64,256]{1,0:T(8,128)S(1)}, u32[]{:S(2)}, u32[]{:S(2)}) %collective-permute-start.29) | collective-permute-done | bytes 65568 | tf_op jit(solution)/shard_map/ppermute | solution.py:34
  115.4 2.5 %collective-permute-start.22 = (f32[128,256]{1,0:T(8,128)S(1)}, f32[128,256]{1,0:T(8,128)S(1)}, u32[]{:S(2)}, u32[]{:S(2)}) collective-permute-start(f32[128,256]{1,0:T(8,128)S(1)} %get-tuple-element.31), channel_id=1, source_target_pairs={{0,1},{1,2},{2,3},{3,4},{4,5},{5,6},{6,7},{7,0},{8,9},{9,10},{10,1... | collective-permute-start | bytes 393224 | tf_op jit(solution)/shard_map/ppermute | solution.py:32
  117.8 0.9 add_add_fusion
  118.7 1.6 %collective-permute-start.31 = (f32[32,256]{1,0:T(8,128)S(1)}, f32[32,256]{1,0:T(8,128)S(1)}, u32[]{:S(2)}, u32[]{:S(2)}) collective-permute-start(f32[32,256]{1,0:T(8,128)S(1)} %slice.29), channel_id=1, source_target_pairs={{0,128},{8,136},{16,144},{24,152},{32,160},{40,168},{48,176},{56,1... | collective-permute-start | bytes 98312 | tf_op jit(solution)/shard_map/ppermute | solution.py:38
  120.3 1.9 %collective-permute-done.20 = f32[128,256]{1,0:T(8,128)S(1)} collective-permute-done((f32[128,256]{1,0:T(8,128)S(1)}, f32[128,256]{1,0:T(8,128)S(1)}, u32[]{:S(2)}, u32[]{:S(2)}) %collective-permute-start.20) | collective-permute-done | bytes 131104 | tf_op jit(solution)/shard_map/ppermute | solution.py:32
  122.2 3.6 %collective-permute-done.21 = f32[128,256]{1,0:T(8,128)S(1)} collective-permute-done((f32[128,256]{1,0:T(8,128)S(1)}, f32[128,256]{1,0:T(8,128)S(1)}, u32[]{:S(2)}, u32[]{:S(2)}) %collective-permute-start.21) | collective-permute-done | bytes 131104 | tf_op jit(solution)/shard_map/ppermute | solution.py:32
  125.7 0.7 subtract_bitcast_fusion
  126.5 0.6 fusion.2
  (56 shorter events, 2.1 us)
Async XLA Ops:
  2.1 4.0 %collective-permute-start.7 = (f32[40,256]{1,0:T(8,128)S(1)}, f32[40,256]{1,0:T(8,128)S(1)}, u32[]{:S(2)}, u32[]{:S(2)}) collective-permute-start(f32[40,256]{1,0:T(8,128)S(1)} %pad_maximum_fusion.1), channel_id=1, source_target_pairs={{0,128},{8,136},{16,144},{24,152},{32,160},{40,168},{48,176},{56,1... | collective-permute-start | bytes 122888 | tf_op jit(solution)/shard_map/ppermute | solution.py:38
  7.0 12.0 %collective-permute-start.8 = (f32[72,256]{1,0:T(8,128)S(1)}, f32[72,256]{1,0:T(8,128)S(1)}, u32[]{:S(2)}, u32[]{:S(2)}) collective-permute-start(f32[72,256]{1,0:T(8,128)S(1)} %pad_maximum_fusion), channel_id=1, source_target_pairs={{0,16},{8,24},{16,32},{24,40},{32,48},{40,56},{48,64},{56,72},{64,... | collective-permute-start | bytes 221192 | tf_op jit(solution)/shard_map/ppermute | solution.py:34
  8.9 25.8 %collective-permute-start.14 = (f32[72,256]{1,0:T(8,128)S(1)}, f32[72,256]{1,0:T(8,128)S(1)}, u32[]{:S(2)}, u32[]{:S(2)}) collective-permute-start(f32[72,256]{1,0:T(8,128)S(1)} %pad_maximum_fusion), channel_id=1, source_target_pairs={{0,112},{8,120},{16,0},{24,8},{32,16},{40,24},{48,32},{56,40},{64,... | collective-permute-start | bytes 221192 | tf_op jit(solution)/shard_map/ppermute | solution.py:34
  9.0 25.6 %collective-permute-start.13 = (f32[72,256]{1,0:T(8,128)S(1)}, f32[72,256]{1,0:T(8,128)S(1)}, u32[]{:S(2)}, u32[]{:S(2)}) collective-permute-start(f32[72,256]{1,0:T(8,128)S(1)} %pad_maximum_fusion), channel_id=1, source_target_pairs={{0,96},{8,104},{16,112},{24,120},{32,0},{40,8},{48,16},{56,24},{64... | collective-permute-start | bytes 221192 | tf_op jit(solution)/shard_map/ppermute | solution.py:34
  14.4 20.2 %collective-permute-start.12 = (f32[72,256]{1,0:T(8,128)S(1)}, f32[72,256]{1,0:T(8,128)S(1)}, u32[]{:S(2)}, u32[]{:S(2)}) collective-permute-start(f32[72,256]{1,0:T(8,128)S(1)} %pad_maximum_fusion), channel_id=1, source_target_pairs={{0,80},{8,88},{16,96},{24,104},{32,112},{40,120},{48,0},{56,8},{64... | collective-permute-start | bytes 221192 | tf_op jit(solution)/shard_map/ppermute | solution.py:34
  17.5 17.1 %collective-permute-start.11 = (f32[72,256]{1,0:T(8,128)S(1)}, f32[72,256]{1,0:T(8,128)S(1)}, u32[]{:S(2)}, u32[]{:S(2)}) collective-permute-start(f32[72,256]{1,0:T(8,128)S(1)} %pad_maximum_fusion), channel_id=1, source_target_pairs={{0,64},{8,72},{16,80},{24,88},{32,96},{40,104},{48,112},{56,120},{... | collective-permute-start | bytes 221192 | tf_op jit(solution)/shard_map/ppermute | solution.py:34
  19.0 8.2 %collective-permute-start.9 = (f32[72,256]{1,0:T(8,128)S(1)}, f32[72,256]{1,0:T(8,128)S(1)}, u32[]{:S(2)}, u32[]{:S(2)}) collective-permute-start(f32[72,256]{1,0:T(8,128)S(1)} %pad_maximum_fusion), channel_id=1, source_target_pairs={{0,32},{8,40},{16,48},{24,56},{32,64},{40,72},{48,80},{56,88},{64,... | collective-permute-start | bytes 221192 | tf_op jit(solution)/shard_map/ppermute | solution.py:34
  27.2 7.4 %collective-permute-start.10 = (f32[72,256]{1,0:T(8,128)S(1)}, f32[72,256]{1,0:T(8,128)S(1)}, u32[]{:S(2)}, u32[]{:S(2)}) collective-permute-start(f32[72,256]{1,0:T(8,128)S(1)} %pad_maximum_fusion), channel_id=1, source_target_pairs={{0,48},{8,56},{16,64},{24,72},{32,80},{40,88},{48,96},{56,104},{64... | collective-permute-start | bytes 221192 | tf_op jit(solution)/shard_map/ppermute | solution.py:34
  34.7 39.5 %collective-permute-start.15 = (f32[576,256]{1,0:T(8,128)S(1)}, f32[576,256]{1,0:T(8,128)S(1)}, u32[]{:S(2)}, u32[]{:S(2)}) collective-permute-start(f32[576,256]{1,0:T(8,128)S(1)} %constant_dynamic-update-slice_fusion.refs_11_), channel_id=1, source_target_pairs={{0,8},{8,0},{16,24},{24,16},{32,40},{40,32},{48,56},{56,48},{64,72... | collective-permute-start | bytes 1769480 | tf_op jit(solution)/shard_map/ppermute | solution.py:38
  36.4 9.6 %collective-permute-start.6 = (f32[136,256]{1,0:T(8,128)S(1)}, f32[136,256]{1,0:T(8,128)S(1)}, u32[]{:S(2)}, u32[]{:S(2)}) collective-permute-start(f32[136,256]{1,0:T(8,128)S(1)} %select_maximum_fusion.refs_3_), channel_id=1, source_target_pairs={{0,7},{1,0},{2,1},{3,2},{4,3},{5,4},{6,5},{7,6},{8,15},{9,8},{10,9... | collective-permute-start | bytes 417800 | tf_op jit(solution)/shard_map/ppermute | solution.py:32
  41.9 12.5 %collective-permute-start.5 = (f32[136,256]{1,0:T(8,128)S(1)}, f32[136,256]{1,0:T(8,128)S(1)}, u32[]{:S(2)}, u32[]{:S(2)}) collective-permute-start(f32[136,256]{1,0:T(8,128)S(1)} %select_maximum_fusion.refs_3_), channel_id=1, source_target_pairs={{0,6},{1,7},{2,0},{3,1},{4,2},{5,3},{6,4},{7,5},{8,14},{9,15},{10,... | collective-permute-start | bytes 417800 | tf_op jit(solution)/shard_map/ppermute | solution.py:32
  42.7 11.7 %collective-permute-start.4 = (f32[136,256]{1,0:T(8,128)S(1)}, f32[136,256]{1,0:T(8,128)S(1)}, u32[]{:S(2)}, u32[]{:S(2)}) collective-permute-start(f32[136,256]{1,0:T(8,128)S(1)} %select_maximum_fusion.refs_3_), channel_id=1, source_target_pairs={{0,5},{1,6},{2,7},{3,0},{4,1},{5,2},{6,3},{7,4},{8,13},{9,14},{10,... | collective-permute-start | bytes 417800 | tf_op jit(solution)/shard_map/ppermute | solution.py:32
  43.1 31.1 %collective-permute-start.3 = (f32[136,256]{1,0:T(8,128)S(1)}, f32[136,256]{1,0:T(8,128)S(1)}, u32[]{:S(2)}, u32[]{:S(2)}) collective-permute-start(f32[136,256]{1,0:T(8,128)S(1)} %select_maximum_fusion.refs_3_), channel_id=1, source_target_pairs={{0,4},{1,5},{2,6},{3,7},{4,0},{5,1},{6,2},{7,3},{8,12},{9,13},{10,... | collective-permute-start | bytes 417800 | tf_op jit(solution)/shard_map/ppermute | solution.py:32
  46.0 28.1 %collective-permute-start.2 = (f32[136,256]{1,0:T(8,128)S(1)}, f32[136,256]{1,0:T(8,128)S(1)}, u32[]{:S(2)}, u32[]{:S(2)}) collective-permute-start(f32[136,256]{1,0:T(8,128)S(1)} %select_maximum_fusion.refs_3_), channel_id=1, source_target_pairs={{0,3},{1,4},{2,5},{3,6},{4,7},{5,0},{6,1},{7,2},{8,11},{9,12},{10,... | collective-permute-start | bytes 417800 | tf_op jit(solution)/shard_map/ppermute | solution.py:32
  54.4 19.7 %collective-permute-start.1 = (f32[136,256]{1,0:T(8,128)S(1)}, f32[136,256]{1,0:T(8,128)S(1)}, u32[]{:S(2)}, u32[]{:S(2)}) collective-permute-start(f32[136,256]{1,0:T(8,128)S(1)} %select_maximum_fusion.refs_3_), channel_id=1, source_target_pairs={{0,2},{1,3},{2,4},{3,5},{4,6},{5,7},{6,0},{7,1},{8,10},{9,11},{10,... | collective-permute-start | bytes 417800 | tf_op jit(solution)/shard_map/ppermute | solution.py:32
  54.4 19.7 %collective-permute-start = (f32[136,256]{1,0:T(8,128)S(1)}, f32[136,256]{1,0:T(8,128)S(1)}, u32[]{:S(2)}, u32[]{:S(2)}) collective-permute-start(f32[136,256]{1,0:T(8,128)S(1)} %select_maximum_fusion.refs_3_), channel_id=1, source_target_pairs={{0,1},{1,2},{2,3},{3,4},{4,5},{5,6},{6,7},{7,0},{8,9},{9,10},{10,1... | collective-permute-start | bytes 417800 | tf_op jit(solution)/shard_map/ppermute | solution.py:32
  55.2 0.7 copy-start.2
  55.9 0.7 copy-start.3
  72.1 2.0 %copy-start = (f32[1024,1024]{1,0:T(8,128)}, f32[1024,1024]{1,0:T(8,128)S(1)}, u32[]{:S(2)}) copy-start(f32[1024,1024]{1,0:T(8,128)S(1)} %get-tuple-element.22.refs_1_) | copy-start | bytes 12582916
  74.2 51.6 %copy-start.4 = (f32[1,128,256]{2,1,0:T(8,128)S(1)}, f32[1,128,256]{2,1,0:T(8,128)}, u32[]{:S(2)}) copy-start(f32[1,128,256]{2,1,0:T(8,128)} %param.11) | copy-start | bytes 393220
  74.2 52.3 %copy-start.6 = (f32[1,32,256]{2,1,0:T(8,128)S(1)}, f32[1,32,256]{2,1,0:T(8,128)}, u32[]{:S(2)}) copy-start(f32[1,32,256]{2,1,0:T(8,128)} %param.12) | copy-start | bytes 98308
  83.5 0.8 copy-start.1
  84.2 7.6 %collective-permute-start.23 = (f32[512,256]{1,0:T(8,128)S(1)}, f32[512,256]{1,0:T(8,128)S(1)}, u32[]{:S(2)}, u32[]{:S(2)}) collective-permute-start(f32[512,256]{1,0:T(8,128)S(1)} %get-tuple-element.33), channel_id=1, source_target_pairs={{0,8},{8,0},{16,24},{24,16},{32,40},{40,32},{48,56},{56,48},{64,72... | collective-permute-start | bytes 1572872 | tf_op jit(solution)/shard_map/ppermute | solution.py:38
  84.2 14.9 %collective-permute-start.16 = (f32[128,256]{1,0:T(8,128)S(1)}, f32[128,256]{1,0:T(8,128)S(1)}, u32[]{:S(2)}, u32[]{:S(2)}) collective-permute-start(f32[128,256]{1,0:T(8,128)S(1)} %get-tuple-element.25), channel_id=1, source_target_pairs={{0,7},{1,0},{2,1},{3,2},{4,3},{5,4},{6,5},{7,6},{8,15},{9,8},{10,9... | collective-permute-start | bytes 393224 | tf_op jit(solution)/shard_map/ppermute | solution.py:32
  89.9 12.6 %collective-permute-start.17 = (f32[128,256]{1,0:T(8,128)S(1)}, f32[128,256]{1,0:T(8,128)S(1)}, u32[]{:S(2)}, u32[]{:S(2)}) collective-permute-start(f32[128,256]{1,0:T(8,128)S(1)} %get-tuple-element.26), channel_id=1, source_target_pairs={{0,6},{1,7},{2,0},{3,1},{4,2},{5,3},{6,4},{7,5},{8,14},{9,15},{10,... | collective-permute-start | bytes 393224 | tf_op jit(solution)/shard_map/ppermute | solution.py:32
  91.9 0.8 copy-start.5
  94.7 9.5 %collective-permute-start.24 = (f32[64,256]{1,0:T(8,128)}, f32[64,256]{1,0:T(8,128)S(1)}, u32[]{:S(2)}, u32[]{:S(2)}) collective-permute-start(f32[64,256]{1,0:T(8,128)} %get-tuple-element.35), channel_id=1, source_target_pairs={{0,112},{8,120},{16,0},{24,8},{32,16},{40,24},{48,32},{56,40},{64,... | collective-permute-start | bytes 196616 | tf_op jit(solution)/shard_map/ppermute | solution.py:34
  96.5 10.2 %collective-permute-start.25 = (f32[64,256]{1,0:T(8,128)}, f32[64,256]{1,0:T(8,128)S(1)}, u32[]{:S(2)}, u32[]{:S(2)}) collective-permute-start(f32[64,256]{1,0:T(8,128)} %get-tuple-element.36), channel_id=1, source_target_pairs={{0,96},{8,104},{16,112},{24,120},{32,0},{40,8},{48,16},{56,24},{64... | collective-permute-start | bytes 196616 | tf_op jit(solution)/shard_map/ppermute | solution.py:34
  96.5 12.1 %collective-permute-start.26 = (f32[64,256]{1,0:T(8,128)}, f32[64,256]{1,0:T(8,128)S(1)}, u32[]{:S(2)}, u32[]{:S(2)}) collective-permute-start(f32[64,256]{1,0:T(8,128)} %get-tuple-element.37), channel_id=1, source_target_pairs={{0,80},{8,88},{16,96},{24,104},{32,112},{40,120},{48,0},{56,8},{64... | collective-permute-start | bytes 196616 | tf_op jit(solution)/shard_map/ppermute | solution.py:34
  99.2 11.3 %collective-permute-start.27 = (f32[64,256]{1,0:T(8,128)}, f32[64,256]{1,0:T(8,128)S(1)}, u32[]{:S(2)}, u32[]{:S(2)}) collective-permute-start(f32[64,256]{1,0:T(8,128)} %get-tuple-element.38), channel_id=1, source_target_pairs={{0,64},{8,72},{16,80},{24,88},{32,96},{40,104},{48,112},{56,120},{... | collective-permute-start | bytes 196616 | tf_op jit(solution)/shard_map/ppermute | solution.py:34
  102.5 10.1 %collective-permute-start.28 = (f32[64,256]{1,0:T(8,128)}, f32[64,256]{1,0:T(8,128)S(1)}, u32[]{:S(2)}, u32[]{:S(2)}) collective-permute-start(f32[64,256]{1,0:T(8,128)} %get-tuple-element.39), channel_id=1, source_target_pairs={{0,48},{8,56},{16,64},{24,72},{32,80},{40,88},{48,96},{56,104},{64... | collective-permute-start | bytes 196616 | tf_op jit(solution)/shard_map/ppermute | solution.py:34
  104.2 11.2 %collective-permute-start.29 = (f32[64,256]{1,0:T(8,128)}, f32[64,256]{1,0:T(8,128)S(1)}, u32[]{:S(2)}, u32[]{:S(2)}) collective-permute-start(f32[64,256]{1,0:T(8,128)} %get-tuple-element.40), channel_id=1, source_target_pairs={{0,32},{8,40},{16,48},{24,56},{32,64},{40,72},{48,80},{56,88},{64,... | collective-permute-start | bytes 196616 | tf_op jit(solution)/shard_map/ppermute | solution.py:34
  106.6 8.7 %collective-permute-start.30 = (f32[64,256]{1,0:T(8,128)}, f32[64,256]{1,0:T(8,128)S(1)}, u32[]{:S(2)}, u32[]{:S(2)}) collective-permute-start(f32[64,256]{1,0:T(8,128)} %get-tuple-element.41), channel_id=1, source_target_pairs={{0,16},{8,24},{16,32},{24,40},{32,48},{40,56},{48,64},{56,72},{64,... | collective-permute-start | bytes 196616 | tf_op jit(solution)/shard_map/ppermute | solution.py:34
  108.6 10.1 %collective-permute-start.18 = (f32[128,256]{1,0:T(8,128)S(1)}, f32[128,256]{1,0:T(8,128)S(1)}, u32[]{:S(2)}, u32[]{:S(2)}) collective-permute-start(f32[128,256]{1,0:T(8,128)S(1)} %get-tuple-element.27), channel_id=1, source_target_pairs={{0,5},{1,6},{2,7},{3,0},{4,1},{5,2},{6,3},{7,4},{8,13},{9,14},{10,... | collective-permute-start | bytes 393224 | tf_op jit(solution)/shard_map/ppermute | solution.py:32
  110.4 9.9 %collective-permute-start.19 = (f32[128,256]{1,0:T(8,128)S(1)}, f32[128,256]{1,0:T(8,128)S(1)}, u32[]{:S(2)}, u32[]{:S(2)}) collective-permute-start(f32[128,256]{1,0:T(8,128)S(1)} %get-tuple-element.28), channel_id=1, source_target_pairs={{0,4},{1,5},{2,6},{3,7},{4,0},{5,1},{6,2},{7,3},{8,12},{9,13},{10,... | collective-permute-start | bytes 393224 | tf_op jit(solution)/shard_map/ppermute | solution.py:32
  112.6 9.6 %collective-permute-start.20 = (f32[128,256]{1,0:T(8,128)S(1)}, f32[128,256]{1,0:T(8,128)S(1)}, u32[]{:S(2)}, u32[]{:S(2)}) collective-permute-start(f32[128,256]{1,0:T(8,128)S(1)} %get-tuple-element.29), channel_id=1, source_target_pairs={{0,3},{1,4},{2,5},{3,6},{4,7},{5,0},{6,1},{7,2},{8,11},{9,12},{10,... | collective-permute-start | bytes 393224 | tf_op jit(solution)/shard_map/ppermute | solution.py:32
  115.4 10.4 %collective-permute-start.21 = (f32[128,256]{1,0:T(8,128)S(1)}, f32[128,256]{1,0:T(8,128)S(1)}, u32[]{:S(2)}, u32[]{:S(2)}) collective-permute-start(f32[128,256]{1,0:T(8,128)S(1)} %get-tuple-element.30), channel_id=1, source_target_pairs={{0,2},{1,3},{2,4},{3,5},{4,6},{5,7},{6,0},{7,1},{8,10},{9,11},{10,... | collective-permute-start | bytes 393224 | tf_op jit(solution)/shard_map/ppermute | solution.py:32
  115.4 10.4 %collective-permute-start.22 = (f32[128,256]{1,0:T(8,128)S(1)}, f32[128,256]{1,0:T(8,128)S(1)}, u32[]{:S(2)}, u32[]{:S(2)}) collective-permute-start(f32[128,256]{1,0:T(8,128)S(1)} %get-tuple-element.31), channel_id=1, source_target_pairs={{0,1},{1,2},{2,3},{3,4},{4,5},{5,6},{6,7},{7,0},{8,9},{9,10},{10,1... | collective-permute-start | bytes 393224 | tf_op jit(solution)/shard_map/ppermute | solution.py:32
  118.7 7.7 %collective-permute-start.31 = (f32[32,256]{1,0:T(8,128)S(1)}, f32[32,256]{1,0:T(8,128)S(1)}, u32[]{:S(2)}, u32[]{:S(2)}) collective-permute-start(f32[32,256]{1,0:T(8,128)S(1)} %slice.29), channel_id=1, source_target_pairs={{0,128},{8,136},{16,144},{24,152},{32,160},{40,168},{48,176},{56,1... | collective-permute-start | bytes 98312 | tf_op jit(solution)/shard_map/ppermute | solution.py:38

commit v2 on v0

v2 whole, which is shorter than its diff:
```python
import jax
import jax.numpy as jnp
from jax import lax
from jax.experimental import pallas as pl
from jax.experimental.pallas import tpu as pltpu
from jax.sharding import PartitionSpec as P

F32 = jnp.float32
BF16 = jnp.bfloat16
N = 1024
D = 256
T = 256
NN = ((1,), (0,))
NT = ((1,), (1,))
VMEM = pl.BlockSpec(memory_space=pltpu.VMEM)
SMEM = pl.BlockSpec(memory_space=pltpu.SMEM)


def f32(*shape):
    return jax.ShapeDtypeStruct(shape, F32)


def bf16(*shape):
    return jax.ShapeDtypeStruct(shape, BF16)


ANY = pl.BlockSpec(memory_space=pl.ANY)
HBM = pl.BlockSpec(memory_space=pltpu.HBM)


def call(body, name, out_shape, operands, smem=0, far=0, after=(), scratch=(), vmem_mb=16, flops=0):
    def run(*refs):
        n = len(operands)
        body(*refs[:n], *refs[n + len(after) :])

    near = len(operands) - smem - far
    operands = [
        pltpu.with_memory_space_constraint(x, pltpu.HBM) if smem <= i < smem + far else x
        for i, x in enumerate(operands)
    ]
    return pl.pallas_call(
        run,
        out_shape=out_shape,
        in_specs=[SMEM] * smem + [HBM] * far + [VMEM] * near + [ANY] * len(after),
        out_specs=[VMEM] * len(out_shape),
        scratch_shapes=list(scratch),
        compiler_params=pltpu.CompilerParams(vmem_limit_bytes=vmem_mb << 20),
        cost_estimate=pl.CostEstimate(flops=flops, bytes_accessed=1 << 16, transcendentals=0),
        name=name,
    )(*operands, *after)


def dot(a, b, dims):
    return lax.dot_general(a, b, (dims, ((), ())), preferred_element_type=F32)


def split(v):
    hi = v.astype(BF16)
    return hi, (v - hi.astype(F32)).astype(BF16)


def move_y(x, k):
    return lax.ppermute(x, "gc", [(i, (i + 2 * k) % 8) for i in range(8)])


def swap_x_hi(x):
    return lax.ppermute(x, "gc", [(i, i ^ 1) for i in range(8)])


def move_z(x, k):
    return lax.ppermute(
        x, "gr", [(i, (i & 17) | (((((i >> 1) & 7) + k) % 8) << 1)) for i in range(32)]
    )


def swap_gr(x, mask):
    return lax.ppermute(x, "gr", [(i, i ^ mask) for i in range(32)])


CORE, Z1, X_LO = 1, 2, 16


def pack_body(total, rows, cols, rm, cm, row_out, col_out, rmv, cmv, sems):
    copies = [
        pltpu.make_async_copy(src, dst, sems.at[i])
        for i, (src, dst) in enumerate(
            [(cols, col_out.at[:32, :]), (cm, cmv), (rows, row_out.at[:128, :]), (rm, rmv)]
        )
    ]
    for c in copies:
        c.start()
    row_out[128:, :] = jnp.zeros((8, D), F32)
    col_out[32:, :] = jnp.zeros((8, D), F32)
    for c in copies:
        c.wait()
    row_out[128:129, :128] = jnp.log(rmv[...].astype(F32))
    log_total = jnp.log(jnp.full((1, 32), total[0], jnp.int32).astype(F32))
    col_out[32:33, :32] = jnp.log(cmv[...].astype(F32)) - log_total


def two_body(a, b, out, *, n, logs):
    out[:n, :] = a[:n, :]
    out[n : 2 * n, :] = b[:n, :]
    out[2 * n :, :] = jnp.zeros((8, D), F32)
    out[2 * n : 2 * n + 1, :128] = a[n : n + 1, :128]
    if logs:
        out[2 * n : 2 * n + 1, logs : 2 * logs] = b[n : n + 1, :logs]
    else:
        out[2 * n + 1 : 2 * n + 2, :128] = b[n : n + 1, :128]


def two(a, b, logs, name, after=()):
    n = a.shape[0] - 8

    def body(*refs):
        two_body(*refs, n=n, logs=logs)

    return call(body, name, [f32(2 * n + 8, D)], [a, b], after=after)[0]


def digits_body(cnt, rs, cs, chi, clo, bt, at, cntv, rsv, csv, sems):
    copies = [pltpu.make_async_copy(rs, rsv, sems.at[0]), pltpu.make_async_copy(cs, csv, sems.at[1])]
    for t in range(4):
        s = pl.ds(T * t, T)
        copies.append(pltpu.make_async_copy(cnt.at[s, :], cntv.at[s, :], sems.at[2 + t]))
    for c in copies:
        c.start()
    gc, gr = lax.axis_index("gc"), lax.axis_index("gr")
    copies[0].wait()
    copies[1].wait()
    rows = rsv[...]
    owner = rows >> 7
    rows = ((((gc >> 1) - (owner >> 1)) & 3) << 8) | (((owner ^ gc) & 1) << 7) | (rows & 127)
    cols = csv[...]
    owner = cols >> 5
    cols = (
        (((owner ^ gr) & 1) << 9)
        | ((((gr >> 2) - (owner >> 2)) & 3) << 7)
        | (((owner ^ gr) & 2) << 5)
        | (((owner ^ gr) & 16) << 1)
        | (cols & 31)
    )
    for t in range(4):
        s = slice(T * t, T * (t + 1))
        j = lax.broadcasted_iota(jnp.int32, (T, N), 0) + t * T
        bt[s, :] = jnp.where(j == cols, 1.0, 0.0).astype(BF16)
        at[s, :] = jnp.where(j == rows, 1.0, 0.0).astype(BF16)
    for t in range(4):
        s = slice(T * t, T * (t + 1))
        copies[2 + t].wait()
        c = cntv[s, :]
        chi[s, :] = (c >> 6).astype(F32).astype(BF16)
        clo[s, :] = (c & 63).astype(F32).astype(BF16)


def order_body(chi, clo, bt, at, w, lx, *, k):
    a = at[T * k : T * (k + 1), :]
    hi = dot(a, chi[...], NN).astype(BF16)
    lo = dot(a, clo[...], NN).astype(BF16)
    x = dot(hi, bt[...], NT) * 64.0 + dot(lo, bt[...], NT)
    w[...] = jnp.where(x > 0, 0.1 + 0.25 * jnp.sqrt(x), 0.0)
    lx[...] = jnp.log(jnp.maximum(x, 1.0))


def half_body(*refs, half, first):
    w, lx, left = refs[:4], refs[4:8], refs[8:12]
    right = refs[12]
    if first:
        gh_out, gl_out, rcat, col_out, lcat, ltr, bvs = refs[13:20]
    else:
        lcat, ltr, bvs = refs[13:16]
        gh_out, gl_out, rcat, col_out = refs[16:20]
    bc, colt = refs[20:]
    for e in range(4):
        at = e * 128
        hi, lo = split(right[e * 136 : e * 136 + 128, :])
        rcat[at : at + 128, :D] = hi
        rcat[at : at + 128, D:] = lo
        bc[:, at : at + 128] = right[e * 136 + 128 : e * 136 + 129, :128]
    h = slice(512 * half, 512 * (half + 1))
    for k in range(4):
        s = slice(T * k, T * (k + 1))
        if first:
            br = left[k][256:264, :128].T
            bvs[s, :] = jnp.concatenate([br[:, 0:1], br[:, 1:2]], 0)
            lh, ll = split(left[k][:256, :])
            lcat[s, :D] = lh
            lcat[s, D:] = ll
            ltr[:, s] = jnp.concatenate([lh, ll], 1).T
        lh, ll = lcat[s, :D], lcat[s, D:]
        score = dot(lh, rcat[:, :D], NT) + dot(lh, rcat[:, D:], NT) + dot(ll, rcat[:, :D], NT)
        d = score + bvs[s, :] + bc[...] - lx[k][:, h]
        wv = w[k][:, h]
        g = jnp.where(wv > 0, wv * d, 0.5 * jnp.tanh(0.5 * d) + 0.5)
        gh, gl = split(g)
        gh_out[s, :] = gh
        gl_out[s, :] = gl
        cc = dot(ltr[:, s], gh, NN)
        cc = cc[:D] + cc[D:] + dot(ltr[:D, s], gl, NN)
        if k == 0:
            colt[...] = cc
        else:
            colt[...] += cc
    col_out[...] = colt[...].T


def rows_body(*refs, first):
    gh, gl, r = refs[:3]
    outs = refs[-4:]
    for k in (2, 1, 3, 0):
        s = slice(T * k, T * (k + 1))
        rr = dot(gh[s, :], r[...], NN)
        rr = rr[:, :D] + rr[:, D:] + dot(gl[s, :], r[:, :D], NN)
        outs[k][...] = rr if first else rr + refs[3 + k][...]


def join_body(*refs):
    for e in range(4):
        refs[4][136 * e : 136 * (e + 1), :] = refs[e][...]


def quarters_body(own, got, *outs):
    for e in range(4):
        s = slice(128 * e, 128 * e + 128)
        outs[e][...] = own[s, :] + got[s, :]


def sum_body(a, b, c, d, keep, give):
    n = keep.shape[0]
    keep[...] = (a[:n, :] + b[:n, :]) + (c[:n, :] + d[:n, :])
    give[...] = (a[n:, :] + b[n:, :]) + (c[n:, :] + d[n:, :])


def add_body(a, b, keep, give):
    n = keep.shape[0]
    keep[...] = a[:n, :] + b[:n, :]
    give[...] = a[n:, :] + b[n:, :]


def last_body(embed, a, b, out):
    out[...] = embed[...] - 0.001 * (a[...] + b[...])


def shards(
    tile_counts, row_slot, col_slot, row_embed, col_embed, row_marginal, col_marginal, total_count
):
    rows, cols = call(
        pack_body,
        "pack",
        [f32(136, D), f32(40, D)],
        [total_count, row_embed[0], col_embed[0], row_marginal, col_marginal],
        smem=1,
        far=4,
        scratch=[
            pltpu.VMEM((1, 128), jnp.int32),
            pltpu.VMEM((1, 32), jnp.int32),
            pltpu.SemaphoreType.DMA((4,)),
        ],
    )
    hot = call(
        digits_body,
        "digits",
        [bf16(N, N)] * 4,
        [tile_counts[0, 0], row_slot[0], col_slot[0]],
        far=3,
        scratch=[
            pltpu.VMEM((N, N), jnp.int32),
            pltpu.VMEM((1, N), jnp.int32),
            pltpu.VMEM((1, N), jnp.int32),
            pltpu.SemaphoreType.DMA((6,)),
        ],
        flops=1 << 30,
    )
    w, lx = [], []

    def order(k, after):
        def body(*refs):
            order_body(*refs, k=k)

        a, b = call(
            body, f"order{k}", [f32(T, N)] * 2, hot, after=after, vmem_mb=24, flops=1 << 31
        )
        w.append(a)
        lx.append(b)

    cols = two(cols, swap_gr(cols, X_LO), 32, "pair_cols", after=hot[:1])
    order(0, [cols])
    rows = two(rows, swap_x_hi(rows), 0, "pair_rows")
    cols = two(cols, swap_gr(cols, Z1), 64, "quad_cols", after=[rows, w[0]])
    for k in range(1, 4):
        order(k, [cols])
    left = [rows] + [move_y(rows, k) for k in range(1, 4)]
    right = call(
        join_body,
        "join",
        [f32(544, D)],
        [cols] + [move_z(cols, 2 * e) for e in range(1, 4)],
        after=left[1:] + w[1:],
    )[0]
    scratch = [pltpu.VMEM((1, 512), F32), pltpu.VMEM((D, 512), F32)]
    half_out = [bf16(N, 512), bf16(N, 512), bf16(512, 2 * D), f32(512, D)]

    def own_body(*refs):
        half_body(*refs, half=0, first=True)

    def other_body(*refs):
        half_body(*refs, half=1, first=False)

    gh1, gl1, r1, col1, lcat, ltr, bvs = call(
        own_body,
        "own",
        half_out + [bf16(N, 2 * D), bf16(2 * D, N), f32(N, 1)],
        [*w, *lx, *left, right],
        scratch=scratch,
        vmem_mb=24,
    )
    gh2, gl2, r2, col2 = call(
        other_body,
        "other",
        half_out,
        [*w, *lx, *left, swap_gr(right, CORE), lcat, ltr, bvs],
        scratch=scratch,
        vmem_mb=24,
    )

    def rows_own(*refs):
        rows_body(*refs, first=True)

    def rows_other(*refs):
        rows_body(*refs, first=False)

    row_own = call(rows_own, "rows_own", [f32(T, D)] * 4, [gh1, gl1, r1], after=[col2], vmem_mb=24)
    parts = call(
        quarters_body, "quarters", [f32(128, D)] * 4, [col1, swap_gr(col2, CORE)], after=row_own[:1]
    )
    outs = call(
        rows_other, "rows_other", [f32(T, D)] * 4, [gh2, gl2, r2, *row_own], after=parts[:1], vmem_mb=24
    )
    row_keep, row_give = call(
        sum_body,
        "sum_rows",
        [f32(128, D)] * 2,
        [outs[0]] + [move_y(outs[k], -k) for k in range(1, 4)],
    )
    col_keep, col_give = call(
        sum_body,
        "sum_cols",
        [f32(64, D)] * 2,
        [parts[0]] + [move_z(parts[e], -2 * e) for e in range(1, 4)],
    )
    col_keep, col_give = call(
        add_body, "add_cols", [f32(32, D)] * 2, [col_keep, swap_gr(col_give, Z1)]
    )
    new_rows = call(
        last_body, "new_rows", [f32(128, D)], [row_embed[0], row_keep, swap_x_hi(row_give)]
    )[0]
    new_cols = call(
        last_body, "new_cols", [f32(32, D)], [col_embed[0], col_keep, swap_gr(col_give, X_LO)]
    )[0]
    return (new_rows[None], new_cols[None])


def solution(mesh):
    return jax.shard_map(
        shards,
        mesh=mesh,
        in_specs=(
            P("gr", "gc", None, None),
            P("gr", "gc", None),
            P("gr", "gc", None),
            P("gr", "gc", None),
            P("gc", "gr", None),
            P("gr", "gc"),
            P("gc", "gr"),
            P(),
        ),
        out_specs=(P("gr", "gc", None), P("gc", "gr", None)),
        check_vma=False,
    )
```

time: 359 us -> 85.6 us (0.24)
  the two profiles are of different devices: /device:TPU:32 before, /device:TPU:24 now
where the time goes in v2:
time: 85.6 us; the launch traced here: 85.4 us
  waiting for transfers between devices  33.1 us (39%)
  starting transfers between devices  27.1 us (32%)
  Pallas kernels  23.8 us (28%)
  between operations  1.48 us (2%)
    pallas_call x20, Pallas kernels, call(): pl.pallas_call(run, out_shape=out_shape, in_specs=[SMEM] * smem + [HBM] *...  23.8 us
    ppermute x6, waiting for transfers between devices, move_z(): lax.ppermute(x, 'gr', [(i, i & 17 | ((i >> 1 & 7) + k) % 8 << 1) for i in...  16.4 us
    ppermute x6, starting transfers between devices, move_z(): lax.ppermute(x, 'gr', [(i, i & 17 | ((i >> 1 & 7) + k) % 8 << 1) for i in...  10 us
    ppermute x6, starting transfers between devices, move_y(): return lax.ppermute(x, 'gc', [(i, (i + 2 * k) % 8) for i in range(8)])  8.96 us
    ppermute x6, waiting for transfers between devices, swap_gr(): return lax.ppermute(x, 'gr', [(i, i ^ mask) for i in range(32)])  8.72 us
    ppermute x6, waiting for transfers between devices, move_y(): return lax.ppermute(x, 'gc', [(i, (i + 2 * k) % 8) for i in range(8)])  7.94 us
    ppermute x6, starting transfers between devices, swap_gr(): return lax.ppermute(x, 'gr', [(i, i ^ mask) for i in range(32)])  4.61 us
    ppermute x2, starting transfers between devices, swap_x_hi(): return lax.ppermute(x, 'gc', [(i, i ^ 1) for i in range(8)])  3.48 us
  transfers between devices with their start and end apart: 20, of which 9 were waited for; matrix products, arithmetic and copies ran while one was open for 0% of the time, Pallas kernels for 21%

profile of v2, /device:TPU:24, one launch (start us, length us, event | category | flops | bytes accessed | tf_op | source)
XLA Modules:
  0.0 85.4 jit_solution(14835520737068696202)
XLA Ops:
  1.3 1.0 %pack.1 = (f32[136,256]{1,0:T(8,128)S(1)}, f32[40,256]{1,0:T(8,128)S(1)}) custom-call(s32[1]{0:T(128)S(6)} %copy.10.refs_0_, f32[128,256]{1,0:T(8,128)} %bitcast.7, f32[32,256]{1,0:T(8,128)} %bitcast.9, s32[1,128]{1,0:T(1,128)} %refs_3_.1, s32[1,32]{1,0:T(1,128)} %refs_4_.1), custom_call_target="tpu_custom_call" | custom-call | bytes 65536 | tf_op jit(solution)/shard_map/pack/pallas_call | solution.py:41
  2.3 1.6 %collective-permute-start = (f32[40,256]{1,0:T(8,128)S(1)}, f32[40,256]{1,0:T(8,128)S(1)}, u32[]{:S(2)}, u32[]{:S(2)}) collective-permute-start(f32[40,256]{1,0:T(8,128)S(1)} %get-tuple-element.49.refs_0_), channel_id=1, source_target_pairs={{0,128},{8,136},{16,144},{24,152},{32,160},{40,168},{48,176},{56,1... | collective-permute-start | bytes 122888 | tf_op jit(solution)/shard_map/ppermute | solution.py:77
  3.9 2.7 %collective-permute-start.2 = (f32[136,256]{1,0:T(8,128)S(1)}, f32[136,256]{1,0:T(8,128)S(1)}, u32[]{:S(2)}, u32[]{:S(2)}) collective-permute-start(f32[136,256]{1,0:T(8,128)S(1)} %get-tuple-element.51.refs_0_), channel_id=1, source_target_pairs={{0,1},{1,0},{2,3},{3,2},{4,5},{5,4},{6,7},{7,6},{8,9},{9,8},{10,11... | collective-permute-start | bytes 417800 | tf_op jit(solution)/shard_map/ppermute | solution.py:67
  6.6 2.4 %digits.1 = (bf16[1024,1024]{1,0:T(8,128)(2,1)S(1)}, bf16[1024,1024]{1,0:T(8,128)(2,1)S(1)}, bf16[1024,1024]{1,0:T(8,128)(2,1)S(1)}, bf16[1024,1024]{1,0:T(8,128)(2,1)S(1)}) custom-call(s32[1024,1024]{1,0:T(8,128)} %bitcast.11, s32[1,1024]{1,0:T(1,128)} %bitcast.14, s32[1,1024]{1,0:T(1,128)} %bitcast.15), custom_call_target="tpu_custom_call" | custom-call | flops 1073741824 | bytes 65536 | tf_op jit(solution)/shard_map/digits/pallas_call | solution.py:41
  9.0 0.0 collective-permute-done.refs_1_
  9.0 0.1 pair_cols.1.refs_4_.refs_0_
  9.1 1.9 %collective-permute-start.1 = (f32[72,256]{1,0:T(8,128)S(1)}, f32[72,256]{1,0:T(8,128)S(1)}, u32[]{:S(2)}, u32[]{:S(2)}) collective-permute-start(f32[72,256]{1,0:T(8,128)S(1)} %pair_cols.1.refs_4_.refs_0_), channel_id=1, source_target_pairs={{0,16},{8,24},{16,0},{24,8},{32,48},{40,56},{48,32},{56,40},{64,80... | collective-permute-start | bytes 221192 | tf_op jit(solution)/shard_map/ppermute | solution.py:77
  11.0 2.6 %order0.1 = (f32[256,1024]{1,0:T(8,128)S(1)}, f32[256,1024]{1,0:T(8,128)S(1)}) custom-call(bf16[1024,1024]{1,0:T(8,128)(2,1)S(1)} %get-tuple-element.45.refs_2_.refs_0_, bf16[1024,1024]{1,0:T(8,128)(2,1)S(1)} %get-tuple-element.46.refs_1_, bf16[1024,1024]{1,0:T(8,128)(2,1)S(1)} %get-tuple-element.47.refs_2_, ...), custom_call_target="tpu_custom_call" | custom-call | flops 2147483648 | bytes 65536 | tf_op jit(solution)/shard_map/order0/pallas_call | solution.py:41
  13.6 0.0 collective-permute-done.2.refs_1_
  13.7 0.8 collective-permute-start.5
  14.5 0.9 %collective-permute-start.4 = (f32[264,256]{1,0:T(8,128)S(1)}, f32[264,256]{1,0:T(8,128)S(1)}, u32[]{:S(2)}, u32[]{:S(2)}) collective-permute-start(f32[264,256]{1,0:T(8,128)S(1)} %pair_rows.1.refs_2_.refs_8_), channel_id=1, source_target_pairs={{0,4},{1,5},{2,6},{3,7},{4,0},{5,1},{6,2},{7,3},{8,12},{9,13},{10,... | collective-permute-start | bytes 811016 | tf_op jit(solution)/shard_map/ppermute | solution.py:63
  15.4 2.2 %collective-permute-start.3 = (f32[264,256]{1,0:T(8,128)S(1)}, f32[264,256]{1,0:T(8,128)S(1)}, u32[]{:S(2)}, u32[]{:S(2)}) collective-permute-start(f32[264,256]{1,0:T(8,128)S(1)} %pair_rows.1.refs_2_.refs_8_), channel_id=1, source_target_pairs={{0,2},{1,3},{2,4},{3,5},{4,6},{5,7},{6,0},{7,1},{8,10},{9,11},{10,... | collective-permute-start | bytes 811016 | tf_op jit(solution)/shard_map/ppermute | solution.py:63
  17.6 0.1 quad_cols.1.refs_4_.refs_0_
  17.7 5.4 %collective-permute-start.8 = (f32[136,256]{1,0:T(8,128)S(1)}, f32[136,256]{1,0:T(8,128)S(1)}, u32[]{:S(2)}, u32[]{:S(2)}) collective-permute-start(f32[136,256]{1,0:T(8,128)S(1)} %quad_cols.1.refs_4_.refs_0_), channel_id=1, source_target_pairs={{0,96},{8,104},{16,112},{24,120},{32,0},{40,8},{48,16},{56,24},{64... | collective-permute-start | bytes 417800 | tf_op jit(solution)/shard_map/ppermute | solution.py:71
  23.1 1.4 %collective-permute-start.7 = (f32[136,256]{1,0:T(8,128)S(1)}, f32[136,256]{1,0:T(8,128)S(1)}, u32[]{:S(2)}, u32[]{:S(2)}) collective-permute-start(f32[136,256]{1,0:T(8,128)S(1)} %quad_cols.1.refs_4_.refs_0_), channel_id=1, source_target_pairs={{0,64},{8,72},{16,80},{24,88},{32,96},{40,104},{48,112},{56,120},{... | collective-permute-start | bytes 417800 | tf_op jit(solution)/shard_map/ppermute | solution.py:71
  24.5 2.6 %order3.1 = (f32[256,1024]{1,0:T(8,128)S(1)}, f32[256,1024]{1,0:T(8,128)S(1)}) custom-call(bf16[1024,1024]{1,0:T(8,128)(2,1)S(1)} %get-tuple-element.45.refs_2_.refs_0_, bf16[1024,1024]{1,0:T(8,128)(2,1)S(1)} %get-tuple-element.46.refs_1_, bf16[1024,1024]{1,0:T(8,128)(2,1)S(1)} %get-tuple-element.47.refs_2_, ...), custom_call_target="tpu_custom_call" | custom-call | flops 2147483648 | bytes 65536 | tf_op jit(solution)/shard_map/order3/pallas_call | solution.py:41
  27.1 2.6 %order2.1 = (f32[256,1024]{1,0:T(8,128)S(1)}, f32[256,1024]{1,0:T(8,128)S(1)}) custom-call(bf16[1024,1024]{1,0:T(8,128)(2,1)S(1)} %get-tuple-element.45.refs_2_.refs_0_, bf16[1024,1024]{1,0:T(8,128)(2,1)S(1)} %get-tuple-element.46.refs_1_, bf16[1024,1024]{1,0:T(8,128)(2,1)S(1)} %get-tuple-element.47.refs_2_, ...), custom_call_target="tpu_custom_call" | custom-call | flops 2147483648 | bytes 65536 | tf_op jit(solution)/shard_map/order2/pallas_call | solution.py:41
  29.7 4.1 %collective-permute-done.8.refs_3_ = f32[136,256]{1,0:T(8,128)S(1)} collective-permute-done((f32[136,256]{1,0:T(8,128)S(1)}, f32[136,256]{1,0:T(8,128)S(1)}, u32[]{:S(2)}, u32[]{:S(2)}) %collective-permute-start.8) | collective-permute-done | bytes 139296 | tf_op jit(solution)/shard_map/ppermute | solution.py:71
  33.8 2.6 %order1.1 = (f32[256,1024]{1,0:T(8,128)S(1)}, f32[256,1024]{1,0:T(8,128)S(1)}) custom-call(bf16[1024,1024]{1,0:T(8,128)(2,1)S(1)} %get-tuple-element.45.refs_2_.refs_0_, bf16[1024,1024]{1,0:T(8,128)(2,1)S(1)} %get-tuple-element.46.refs_1_, bf16[1024,1024]{1,0:T(8,128)(2,1)S(1)} %get-tuple-element.47.refs_2_, ...), custom_call_target="tpu_custom_call" | custom-call | flops 2147483648 | bytes 65536 | tf_op jit(solution)/shard_map/order1/pallas_call | solution.py:41
  36.4 0.0 collective-permute-done.7.refs_2_
  36.4 5.0 %collective-permute-done.6.refs_1_ = f32[136,256]{1,0:T(8,128)S(1)} collective-permute-done((f32[136,256]{1,0:T(8,128)S(1)}, f32[136,256]{1,0:T(8,128)S(1)}, u32[]{:S(2)}, u32[]{:S(2)}) %collective-permute-start.6) | collective-permute-done | bytes 139296 | tf_op jit(solution)/shard_map/ppermute | solution.py:71
  41.5 0.3 collective-permute-start.9
  41.8 3.3 %own.1 = (bf16[1024,512]{1,0:T(8,128)(2,1)S(1)}, bf16[1024,512]{1,0:T(8,128)(2,1)S(1)}, bf16[512,512]{1,0:T(8,128)(2,1)S(1)}, f32[512,256]{1,0:T(8,128)S(1)}, bf...) custom-call(f32[256,1024]{1,0:T(8,128)S(1)} %get-tuple-element.50.refs_3_.refs_0_, ...), custom_call_target="tpu_custom_call" | custom-call | bytes 65536 | tf_op jit(solution)/shard_map/own/pallas_call | solution.py:41
  45.2 3.2 %other.1 = (bf16[1024,512]{1,0:T(8,128)(2,1)S(1)}, bf16[1024,512]{1,0:T(8,128)(2,1)S(1)}, bf16[512,512]{1,0:T(8,128)(2,1)S(1)}, f32[512,256]{1,0:T(8,128)S(1)}) custom-call(f32[256,1024]{1,0:T(8,128)S(1)} %get-tuple-element.50.refs_3_.refs_0_, f32[256,1024]{1,0:T(8,128)S(1)} %get-tuple-element.52.refs_7_.refs_1_, ...), custom_call_target="tpu_custom_call" | custom-call | bytes 65536 | tf_op jit(solution)/shard_map/other/pallas_call | solution.py:41
  48.4 0.6 collective-permute-start.10
  49.0 1.0 %rows_own.1 = (f32[256,256]{1,0:T(8,128)S(1)}, f32[256,256]{1,0:T(8,128)S(1)}, f32[256,256]{1,0:T(8,128)S(1)}, f32[256,256]{1,0:T(8,128)S(1)}) custom-call(bf16[1024,512]{1,0:T(8,128)(2,1)S(1)} %get-tuple-element.65.refs_0_, bf16[1024,512]{1,0:T(8,128)(2,1)S(1)} %get-tuple-element.66.refs_1_, bf16[512,512]{1,0:T(8,128)(2,1)S(1)} %get-tuple-element.67.refs_2_, ...), custom_call_target="tpu_custom_call" | custom-call | bytes 65536 | tf_op jit(solution)/shard_map/rows_own/pallas_call | solution.py:41
  49.9 0.6 collective-permute-done.10.refs_1_
  50.5 0.1 quarters.1
  50.6 0.0 copy-start.1
  50.6 0.0 copy-start
  50.6 1.0 %rows_other.1 = (f32[256,256]{1,0:T(8,128)S(1)}, f32[256,256]{1,0:T(8,128)S(1)}, f32[256,256]{1,0:T(8,128)S(1)}, f32[256,256]{1,0:T(8,128)S(1)}) custom-call(bf16[1024,512]{1,0:T(8,128)(2,1)S(1)} %get-tuple-element.62.refs_0_, bf16[1024,512]{1,0:T(8,128)(2,1)S(1)} %get-tuple-element.63.refs_1_, bf16[512,512]{1,0:T(8,128)(2,1)S(1)} %get-tuple-element.64.refs_2_, ...), custom_call_target="tpu_custom_call" | custom-call | bytes 65536 | tf_op jit(solution)/shard_map/rows_other/pallas_call | solution.py:41
  51.6 0.5 collective-permute-start.11
  52.1 2.0 %collective-permute-start.12 = (f32[256,256]{1,0:T(8,128)S(1)}, f32[256,256]{1,0:T(8,128)S(1)}, u32[]{:S(2)}, u32[]{:S(2)}) collective-permute-start(f32[256,256]{1,0:T(8,128)S(1)} %get-tuple-element.77), channel_id=1, source_target_pairs={{0,4},{1,5},{2,6},{3,7},{4,0},{5,1},{6,2},{7,3},{8,12},{9,13},{10,... | collective-permute-start | bytes 786440 | tf_op jit(solution)/shard_map/ppermute | solution.py:63
  54.1 2.5 %collective-permute-start.13 = (f32[256,256]{1,0:T(8,128)S(1)}, f32[256,256]{1,0:T(8,128)S(1)}, u32[]{:S(2)}, u32[]{:S(2)}) collective-permute-start(f32[256,256]{1,0:T(8,128)S(1)} %get-tuple-element.78), channel_id=1, source_target_pairs={{0,2},{1,3},{2,4},{3,5},{4,6},{5,7},{6,0},{7,1},{8,10},{9,11},{10,... | collective-permute-start | bytes 786440 | tf_op jit(solution)/shard_map/ppermute | solution.py:63
  56.6 2.9 %collective-permute-start.15 = (f32[128,256]{1,0:T(8,128)S(1)}, f32[128,256]{1,0:T(8,128)S(1)}, u32[]{:S(2)}, u32[]{:S(2)}) collective-permute-start(f32[128,256]{1,0:T(8,128)S(1)} %get-tuple-element.81), channel_id=1, source_target_pairs={{0,96},{8,104},{16,112},{24,120},{32,0},{40,8},{48,16},{56,24},{64... | collective-permute-start | bytes 393224 | tf_op jit(solution)/shard_map/ppermute | solution.py:71
  59.5 0.2 collective-permute-start.16
  59.7 7.3 %collective-permute-done.11.refs_1_ = f32[256,256]{1,0:T(8,128)S(1)} collective-permute-done((f32[256,256]{1,0:T(8,128)S(1)}, f32[256,256]{1,0:T(8,128)S(1)}, u32[]{:S(2)}, u32[]{:S(2)}) %collective-permute-start.11) | collective-permute-done | bytes 262176 | tf_op jit(solution)/shard_map/ppermute | solution.py:63
  67.1 0.6 collective-permute-done.13.refs_3_
  67.7 0.1 sum_rows.1
  67.7 0.7 collective-permute-start.14
  68.5 5.3 %collective-permute-done.16.refs_2_ = f32[128,256]{1,0:T(8,128)S(1)} collective-permute-done((f32[128,256]{1,0:T(8,128)S(1)}, f32[128,256]{1,0:T(8,128)S(1)}, u32[]{:S(2)}, u32[]{:S(2)}) %collective-permute-start.16) | collective-permute-done | bytes 131104 | tf_op jit(solution)/shard_map/ppermute | solution.py:71
  73.8 1.9 %collective-permute-done.17.refs_3_ = f32[128,256]{1,0:T(8,128)S(1)} collective-permute-done((f32[128,256]{1,0:T(8,128)S(1)}, f32[128,256]{1,0:T(8,128)S(1)}, u32[]{:S(2)}, u32[]{:S(2)}) %collective-permute-start.17) | collective-permute-done | bytes 131104 | tf_op jit(solution)/shard_map/ppermute | solution.py:71
  75.8 0.1 collective-permute-start.18
  75.9 4.3 %collective-permute-done.18.refs_1_ = f32[64,256]{1,0:T(8,128)S(1)} collective-permute-done((f32[64,256]{1,0:T(8,128)S(1)}, f32[64,256]{1,0:T(8,128)S(1)}, u32[]{:S(2)}, u32[]{:S(2)}) %collective-permute-start.18) | collective-permute-done | bytes 65568 | tf_op jit(solution)/shard_map/ppermute | solution.py:77
  80.1 0.1 collective-permute-start.19
  80.2 3.9 %collective-permute-done.19.refs_2_ = f32[32,256]{1,0:T(8,128)S(1)} collective-permute-done((f32[32,256]{1,0:T(8,128)S(1)}, f32[32,256]{1,0:T(8,128)S(1)}, u32[]{:S(2)}, u32[]{:S(2)}) %collective-permute-start.19) | collective-permute-done | bytes 32800 | tf_op jit(solution)/shard_map/ppermute | solution.py:77
  84.1 0.6 new_cols.1
  84.8 0.7 new_rows.1
  (16 shorter events, 0.1 us)
Async XLA Ops:
  2.3 6.7 %collective-permute-start = (f32[40,256]{1,0:T(8,128)S(1)}, f32[40,256]{1,0:T(8,128)S(1)}, u32[]{:S(2)}, u32[]{:S(2)}) collective-permute-start(f32[40,256]{1,0:T(8,128)S(1)} %get-tuple-element.49.refs_0_), channel_id=1, source_target_pairs={{0,128},{8,136},{16,144},{24,152},{32,160},{40,168},{48,176},{56,1... | collective-permute-start | bytes 122888 | tf_op jit(solution)/shard_map/ppermute | solution.py:77
  3.9 9.8 %collective-permute-start.2 = (f32[136,256]{1,0:T(8,128)S(1)}, f32[136,256]{1,0:T(8,128)S(1)}, u32[]{:S(2)}, u32[]{:S(2)}) collective-permute-start(f32[136,256]{1,0:T(8,128)S(1)} %get-tuple-element.51.refs_0_), channel_id=1, source_target_pairs={{0,1},{1,0},{2,3},{3,2},{4,5},{5,4},{6,7},{7,6},{8,9},{9,8},{10,11... | collective-permute-start | bytes 417800 | tf_op jit(solution)/shard_map/ppermute | solution.py:67
  9.1 8.5 %collective-permute-start.1 = (f32[72,256]{1,0:T(8,128)S(1)}, f32[72,256]{1,0:T(8,128)S(1)}, u32[]{:S(2)}, u32[]{:S(2)}) collective-permute-start(f32[72,256]{1,0:T(8,128)S(1)} %pair_cols.1.refs_4_.refs_0_), channel_id=1, source_target_pairs={{0,16},{8,24},{16,0},{24,8},{32,48},{40,56},{48,32},{56,40},{64,80... | collective-permute-start | bytes 221192 | tf_op jit(solution)/shard_map/ppermute | solution.py:77
  13.7 27.8 %collective-permute-start.5 = (f32[264,256]{1,0:T(8,128)S(1)}, f32[264,256]{1,0:T(8,128)S(1)}, u32[]{:S(2)}, u32[]{:S(2)}) collective-permute-start(f32[264,256]{1,0:T(8,128)S(1)} %pair_rows.1.refs_2_.refs_8_), channel_id=1, source_target_pairs={{0,6},{1,7},{2,0},{3,1},{4,2},{5,3},{6,4},{7,5},{8,14},{9,15},{10,... | collective-permute-start | bytes 811016 | tf_op jit(solution)/shard_map/ppermute | solution.py:63
  14.5 27.0 %collective-permute-start.4 = (f32[264,256]{1,0:T(8,128)S(1)}, f32[264,256]{1,0:T(8,128)S(1)}, u32[]{:S(2)}, u32[]{:S(2)}) collective-permute-start(f32[264,256]{1,0:T(8,128)S(1)} %pair_rows.1.refs_2_.refs_8_), channel_id=1, source_target_pairs={{0,4},{1,5},{2,6},{3,7},{4,0},{5,1},{6,2},{7,3},{8,12},{9,13},{10,... | collective-permute-start | bytes 811016 | tf_op jit(solution)/shard_map/ppermute | solution.py:63
  15.4 26.0 %collective-permute-start.3 = (f32[264,256]{1,0:T(8,128)S(1)}, f32[264,256]{1,0:T(8,128)S(1)}, u32[]{:S(2)}, u32[]{:S(2)}) collective-permute-start(f32[264,256]{1,0:T(8,128)S(1)} %pair_rows.1.refs_2_.refs_8_), channel_id=1, source_target_pairs={{0,2},{1,3},{2,4},{3,5},{4,6},{5,7},{6,0},{7,1},{8,10},{9,11},{10,... | collective-permute-start | bytes 811016 | tf_op jit(solution)/shard_map/ppermute | solution.py:63
  17.7 16.2 %collective-permute-start.8 = (f32[136,256]{1,0:T(8,128)S(1)}, f32[136,256]{1,0:T(8,128)S(1)}, u32[]{:S(2)}, u32[]{:S(2)}) collective-permute-start(f32[136,256]{1,0:T(8,128)S(1)} %quad_cols.1.refs_4_.refs_0_), channel_id=1, source_target_pairs={{0,96},{8,104},{16,112},{24,120},{32,0},{40,8},{48,16},{56,24},{64... | collective-permute-start | bytes 417800 | tf_op jit(solution)/shard_map/ppermute | solution.py:71
  23.1 13.3 %collective-permute-start.7 = (f32[136,256]{1,0:T(8,128)S(1)}, f32[136,256]{1,0:T(8,128)S(1)}, u32[]{:S(2)}, u32[]{:S(2)}) collective-permute-start(f32[136,256]{1,0:T(8,128)S(1)} %quad_cols.1.refs_4_.refs_0_), channel_id=1, source_target_pairs={{0,64},{8,72},{16,80},{24,88},{32,96},{40,104},{48,112},{56,120},{... | collective-permute-start | bytes 417800 | tf_op jit(solution)/shard_map/ppermute | solution.py:71
  33.8 7.6 %collective-permute-start.6 = (f32[136,256]{1,0:T(8,128)S(1)}, f32[136,256]{1,0:T(8,128)S(1)}, u32[]{:S(2)}, u32[]{:S(2)}) collective-permute-start(f32[136,256]{1,0:T(8,128)S(1)} %quad_cols.1.refs_4_.refs_0_), channel_id=1, source_target_pairs={{0,32},{8,40},{16,48},{24,56},{32,64},{40,72},{48,80},{56,88},{64,... | collective-permute-start | bytes 417800 | tf_op jit(solution)/shard_map/ppermute | solution.py:71
  41.5 3.7 %collective-permute-start.9 = (f32[544,256]{1,0:T(8,128)S(1)}, f32[544,256]{1,0:T(8,128)S(1)}, u32[]{:S(2)}, u32[]{:S(2)}) collective-permute-start(f32[544,256]{1,0:T(8,128)S(1)} %join.1.refs_12_), channel_id=1, source_target_pairs={{0,8},{8,0},{16,24},{24,16},{32,40},{40,32},{48,56},{56,48},{64,72... | collective-permute-start | bytes 1671176 | tf_op jit(solution)/shard_map/ppermute | solution.py:77
  48.4 2.1 %collective-permute-start.10 = (f32[512,256]{1,0:T(8,128)S(1)}, f32[512,256]{1,0:T(8,128)S(1)}, u32[]{:S(2)}, u32[]{:S(2)}) collective-permute-start(f32[512,256]{1,0:T(8,128)S(1)} %get-tuple-element.68.refs_3_), channel_id=1, source_target_pairs={{0,8},{8,0},{16,24},{24,16},{32,40},{40,32},{48,56},{56,48},{64,72... | collective-permute-start | bytes 1572872 | tf_op jit(solution)/shard_map/ppermute | solution.py:77
  50.6 33.6 %copy-start.1 = (f32[1,32,256]{2,1,0:T(8,128)S(1)}, f32[1,32,256]{2,1,0:T(8,128)}, u32[]{:S(2)}) copy-start(f32[1,32,256]{2,1,0:T(8,128)} %param.12) | copy-start | bytes 98308
  50.6 34.2 %copy-start = (f32[1,128,256]{2,1,0:T(8,128)S(1)}, f32[1,128,256]{2,1,0:T(8,128)}, u32[]{:S(2)}) copy-start(f32[1,128,256]{2,1,0:T(8,128)} %param.11) | copy-start | bytes 393220
  51.6 15.5 %collective-permute-start.11 = (f32[256,256]{1,0:T(8,128)S(1)}, f32[256,256]{1,0:T(8,128)S(1)}, u32[]{:S(2)}, u32[]{:S(2)}) collective-permute-start(f32[256,256]{1,0:T(8,128)S(1)} %get-tuple-element.76), channel_id=1, source_target_pairs={{0,6},{1,7},{2,0},{3,1},{4,2},{5,3},{6,4},{7,5},{8,14},{9,15},{10,... | collective-permute-start | bytes 786440 | tf_op jit(solution)/shard_map/ppermute | solution.py:63
  52.1 15.0 %collective-permute-start.12 = (f32[256,256]{1,0:T(8,128)S(1)}, f32[256,256]{1,0:T(8,128)S(1)}, u32[]{:S(2)}, u32[]{:S(2)}) collective-permute-start(f32[256,256]{1,0:T(8,128)S(1)} %get-tuple-element.77), channel_id=1, source_target_pairs={{0,4},{1,5},{2,6},{3,7},{4,0},{5,1},{6,2},{7,3},{8,12},{9,13},{10,... | collective-permute-start | bytes 786440 | tf_op jit(solution)/shard_map/ppermute | solution.py:63
  54.1 13.6 %collective-permute-start.13 = (f32[256,256]{1,0:T(8,128)S(1)}, f32[256,256]{1,0:T(8,128)S(1)}, u32[]{:S(2)}, u32[]{:S(2)}) collective-permute-start(f32[256,256]{1,0:T(8,128)S(1)} %get-tuple-element.78), channel_id=1, source_target_pairs={{0,2},{1,3},{2,4},{3,5},{4,6},{5,7},{6,0},{7,1},{8,10},{9,11},{10,... | collective-permute-start | bytes 786440 | tf_op jit(solution)/shard_map/ppermute | solution.py:63
  56.6 11.9 %collective-permute-start.15 = (f32[128,256]{1,0:T(8,128)S(1)}, f32[128,256]{1,0:T(8,128)S(1)}, u32[]{:S(2)}, u32[]{:S(2)}) collective-permute-start(f32[128,256]{1,0:T(8,128)S(1)} %get-tuple-element.81), channel_id=1, source_target_pairs={{0,96},{8,104},{16,112},{24,120},{32,0},{40,8},{48,16},{56,24},{64... | collective-permute-start | bytes 393224 | tf_op jit(solution)/shard_map/ppermute | solution.py:71
  59.5 14.3 %collective-permute-start.16 = (f32[128,256]{1,0:T(8,128)S(1)}, f32[128,256]{1,0:T(8,128)S(1)}, u32[]{:S(2)}, u32[]{:S(2)}) collective-permute-start(f32[128,256]{1,0:T(8,128)S(1)} %get-tuple-element.82), channel_id=1, source_target_pairs={{0,64},{8,72},{16,80},{24,88},{32,96},{40,104},{48,112},{56,120},{... | collective-permute-start | bytes 393224 | tf_op jit(solution)/shard_map/ppermute | solution.py:71
  67.1 8.7 %collective-permute-start.17 = (f32[128,256]{1,0:T(8,128)S(1)}, f32[128,256]{1,0:T(8,128)S(1)}, u32[]{:S(2)}, u32[]{:S(2)}) collective-permute-start(f32[128,256]{1,0:T(8,128)S(1)} %get-tuple-element.83), channel_id=1, source_target_pairs={{0,32},{8,40},{16,48},{24,56},{32,64},{40,72},{48,80},{56,88},{64,... | collective-permute-start | bytes 393224 | tf_op jit(solution)/shard_map/ppermute | solution.py:71
  67.7 17.0 %collective-permute-start.14 = (f32[128,256]{1,0:T(8,128)S(1)}, f32[128,256]{1,0:T(8,128)S(1)}, u32[]{:S(2)}, u32[]{:S(2)}) collective-permute-start(f32[128,256]{1,0:T(8,128)S(1)} %get-tuple-element.80), channel_id=1, source_target_pairs={{0,1},{1,0},{2,3},{3,2},{4,5},{5,4},{6,7},{7,6},{8,9},{9,8},{10,11... | collective-permute-start | bytes 393224 | tf_op jit(solution)/shard_map/ppermute | solution.py:67
  75.8 4.4 %collective-permute-start.18 = (f32[64,256]{1,0:T(8,128)S(1)}, f32[64,256]{1,0:T(8,128)S(1)}, u32[]{:S(2)}, u32[]{:S(2)}) collective-permute-start(f32[64,256]{1,0:T(8,128)S(1)} %get-tuple-element.85), channel_id=1, source_target_pairs={{0,16},{8,24},{16,0},{24,8},{32,48},{40,56},{48,32},{56,40},{64,80... | collective-permute-start | bytes 196616 | tf_op jit(solution)/shard_map/ppermute | solution.py:77
  80.1 4.0 %collective-permute-start.19 = (f32[32,256]{1,0:T(8,128)S(1)}, f32[32,256]{1,0:T(8,128)S(1)}, u32[]{:S(2)}, u32[]{:S(2)}) collective-permute-start(f32[32,256]{1,0:T(8,128)S(1)} %get-tuple-element.87), channel_id=1, source_target_pairs={{0,128},{8,136},{16,144},{24,152},{32,160},{40,168},{48,176},{56,1... | collective-permute-start | bytes 98312 | tf_op jit(solution)/shard_map/ppermute | solution.py:77

commit v3 on v2

--- a/solution.py
+++ b/solution.py
@@ -7,6 +7,7 @@
 
 F32 = jnp.float32
 BF16 = jnp.bfloat16
+F8 = jnp.float8_e4m3fn
 N = 1024
 D = 256
 T = 256
@@ -73,11 +74,20 @@
     )
 
 
+def move_z_by_core(x, k):
+    return lax.ppermute(
+        x,
+        "gr",
+        [(i, (i & 17) | (((((i >> 1) & 7) + (-k if i & 1 else k)) % 8) << 1)) for i in range(32)],
+    )
+
+
 def swap_gr(x, mask):
     return lax.ppermute(x, "gr", [(i, i ^ mask) for i in range(32)])
 
 
 CORE, Z1, X_LO = 1, 2, 16
+CFG = dict(r1=(1, 2), r2=(3,), y1=0, y2=0, early=1, pr=1, sr=1, qo=1, ro=1, of=31, kf=1 << 33, ownfar=0)
 
 
 def pack_body(total, rows, cols, rm, cm, row_out, col_out, rmv, cmv, sems):
@@ -118,7 +128,7 @@
     return call(body, name, [f32(2 * n + 8, D)], [a, b], after=after)[0]
 
 
-def digits_body(cnt, rs, cs, chi, clo, bt, at, cntv, rsv, csv, sems):
+def digits_body(cnt, rs, cs, c2, c1, c0, bt, at, cntv, rsv, csv, sems):
     copies = [pltpu.make_async_copy(rs, rsv, sems.at[0]), pltpu.make_async_copy(cs, csv, sems.at[1])]
     for t in range(4):
         s = pl.ds(T * t, T)
@@ -133,9 +143,10 @@
     rows = ((((gc >> 1) - (owner >> 1)) & 3) << 8) | (((owner ^ gc) & 1) << 7) | (rows & 127)
     cols = csv[...]
     owner = cols >> 5
+    away = (((gr >> 2) - (owner >> 2)) * (1 - 2 * (gr & 1))) & 3
     cols = (
-        (((owner ^ gr) & 1) << 9)
-        | ((((gr >> 2) - (owner >> 2)) & 3) << 7)
+        ((away ^ (away >> 1)) << 8)
+        | (((owner ^ gr) & 1) << 7)
         | (((owner ^ gr) & 2) << 5)
         | (((owner ^ gr) & 16) << 1)
         | (cols & 31)
@@ -143,44 +154,39 @@
     for t in range(4):
         s = slice(T * t, T * (t + 1))
         j = lax.broadcasted_iota(jnp.int32, (T, N), 0) + t * T
-        bt[s, :] = jnp.where(j == cols, 1.0, 0.0).astype(BF16)
-        at[s, :] = jnp.where(j == rows, 1.0, 0.0).astype(BF16)
+        bt[s, :] = jnp.where(j == cols, 1.0, 0.0).astype(F8)
+        at[s, :] = jnp.where(j == rows, 1.0, 0.0).astype(F8)
     for t in range(4):
         s = slice(T * t, T * (t + 1))
         copies[2 + t].wait()
         c = cntv[s, :]
-        chi[s, :] = (c >> 6).astype(F32).astype(BF16)
-        clo[s, :] = (c & 63).astype(F32).astype(BF16)
-
-
-def order_body(chi, clo, bt, at, w, lx, *, k):
+        c2[s, :] = (c >> 8).astype(F32).astype(F8)
+        c1[s, :] = ((c >> 4) & 15).astype(F32).astype(F8)
+        c0[s, :] = (c & 15).astype(F32).astype(F8)
+
+
+def order_body(c2, c1, c0, bt, at, w, lx, *, k):
     a = at[T * k : T * (k + 1), :]
-    hi = dot(a, chi[...], NN).astype(BF16)
-    lo = dot(a, clo[...], NN).astype(BF16)
-    x = dot(hi, bt[...], NT) * 64.0 + dot(lo, bt[...], NT)
+    d2, d1, d0 = (dot(a, c[...], NN).astype(F8) for c in (c2, c1, c0))
+    x = dot(d2, bt[...], NT) * 256.0 + dot(d1, bt[...], NT) * 16.0 + dot(d0, bt[...], NT)
     w[...] = jnp.where(x > 0, 0.1 + 0.25 * jnp.sqrt(x), 0.0)
     lx[...] = jnp.log(jnp.maximum(x, 1.0))
 
 
-def half_body(*refs, half, first):
-    w, lx, left = refs[:4], refs[4:8], refs[8:12]
-    right = refs[12]
-    if first:
-        gh_out, gl_out, rcat, col_out, lcat, ltr, bvs = refs[13:20]
-    else:
-        lcat, ltr, bvs = refs[13:16]
-        gh_out, gl_out, rcat, col_out = refs[16:20]
-    bc, colt = refs[20:]
+def half_body(w, lx, left, right, saved, outs, bc, *, half):
+    gh_out, gl_out, rcat = outs
+    lcat, ltr, bvs = saved
     for e in range(4):
         at = e * 128
-        hi, lo = split(right[e * 136 : e * 136 + 128, :])
+        src, off = right[e]
+        hi, lo = split(src[off : off + 128, :])
         rcat[at : at + 128, :D] = hi
         rcat[at : at + 128, D:] = lo
-        bc[:, at : at + 128] = right[e * 136 + 128 : e * 136 + 129, :128]
+        bc[:, at : at + 128] = src[off + 128 : off + 129, :128]
     h = slice(512 * half, 512 * (half + 1))
     for k in range(4):
         s = slice(T * k, T * (k + 1))
-        if first:
+        if half == 0:
             br = left[k][256:264, :128].T
             bvs[s, :] = jnp.concatenate([br[:, 0:1], br[:, 1:2]], 0)
             lh, ll = split(left[k][:256, :])
@@ -195,13 +201,33 @@
         gh, gl = split(g)
         gh_out[s, :] = gh
         gl_out[s, :] = gl
-        cc = dot(ltr[:, s], gh, NN)
-        cc = cc[:D] + cc[D:] + dot(ltr[:D, s], gl, NN)
-        if k == 0:
-            colt[...] = cc
-        else:
-            colt[...] += cc
-    col_out[...] = colt[...].T
+    cc = dot(ltr[...], gh_out[...], NN)
+    cc = cc[:D] + cc[D:] + dot(ltr[:D, :], gl_out[...], NN)
+    return cc.T
+
+
+def own_body(*refs):
+    w, lx, left = refs[:4], refs[4:8], refs[8:12]
+    near, beside, first = refs[12:15]
+    gh, gl, rcat, col, lcat, ltr, bvs = refs[15:22]
+    (bc,) = refs[22:]
+    right = [(near, 0), (beside, 0), (first, 0), (first, 136)]
+    col[...] = half_body(w, lx, left, right, (lcat, ltr, bvs), (gh, gl, rcat), bc, half=0)
+
+
+def other_body(*refs):
+    w, lx = refs[:4], refs[4:8]
+    second, far, far_beside = refs[8:11]
+    saved = refs[11:14]
+    col1 = refs[14]
+    gh, gl, rcat, keep, give = refs[15:20]
+    (bc,) = refs[20:]
+    give[:128, :] = col1[128:256, :]
+    right = [(second, 136), (second, 0), (far, 0), (far_beside, 0)]
+    col = half_body(w, lx, None, right, saved, (gh, gl, rcat), bc, half=1)
+    give[256:512, :] = col[:256]
+    keep[...] = col[256:384]
+    give[128:256, :] = col[384:]
 
 
 def rows_body(*refs, first):
@@ -214,21 +240,23 @@
         outs[k][...] = rr if first else rr + refs[3 + k][...]
 
 
-def join_body(*refs):
-    for e in range(4):
-        refs[4][136 * e : 136 * (e + 1), :] = refs[e][...]
-
-
-def quarters_body(own, got, *outs):
-    for e in range(4):
-        s = slice(128 * e, 128 * e + 128)
-        outs[e][...] = own[s, :] + got[s, :]
+def join_body(a, b, out):
+    out[:136, :] = a[...]
+    out[136:, :] = b[...]
+
+
+def quarters_body(col1, far, got, near_out, far_out, first_out):
+    near_out[...] = col1[:128, :] + got[:128, :]
+    far_out[...] = far[...] + got[128:256, :]
+    first_out[:128, :] = col1[256:384, :] + got[384:, :]
+    first_out[128:, :] = col1[384:, :] + got[256:384, :]
 
 
 def sum_body(a, b, c, d, keep, give):
     n = keep.shape[0]
+    m = 2 * n
     keep[...] = (a[:n, :] + b[:n, :]) + (c[:n, :] + d[:n, :])
-    give[...] = (a[n:, :] + b[n:, :]) + (c[n:, :] + d[n:, :])
+    give[...] = (a[n:m, :] + b[n:m, :]) + (c[n:m, :] + d[n:m, :])
 
 
 def add_body(a, b, keep, give):
@@ -237,8 +265,9 @@
     give[...] = a[n:, :] + b[n:, :]
 
 
-def last_body(embed, a, b, out):
-    out[...] = embed[...] - 0.001 * (a[...] + b[...])
+def last_body(rows, ra, rb, cols, ca, cb, new_rows, new_cols):
+    new_rows[...] = rows[...] - 0.001 * (ra[...] + rb[...])
+    new_cols[...] = cols[...] - 0.001 * (ca[...] + cb[...])
 
 
 def shards(
@@ -260,7 +289,7 @@
     hot = call(
         digits_body,
         "digits",
-        [bf16(N, N)] * 4,
+        [jax.ShapeDtypeStruct((N, N), F8)] * 5,
         [tile_counts[0, 0], row_slot[0], col_slot[0]],
         far=3,
         scratch=[
@@ -269,7 +298,7 @@
             pltpu.VMEM((1, N), jnp.int32),
             pltpu.SemaphoreType.DMA((6,)),
         ],
-        flops=1 << 30,
+        flops=1 << CFG["of"],
     )
     w, lx = [], []
 
@@ -278,7 +307,7 @@
             order_body(*refs, k=k)
 
         a, b = call(
-            body, f"order{k}", [f32(T, N)] * 2, hot, after=after, vmem_mb=24, flops=1 << 31
+            body, f"order{k}", [f32(T, N)] * 2, hot, after=after, vmem_mb=24, flops=1 << CFG["of"]
         )
         w.append(a)
         lx.append(b)
@@ -286,39 +315,46 @@
     cols = two(cols, swap_gr(cols, X_LO), 32, "pair_cols", after=hot[:1])
     order(0, [cols])
     rows = two(rows, swap_x_hi(rows), 0, "pair_rows")
-    cols = two(cols, swap_gr(cols, Z1), 64, "quad_cols", after=[rows, w[0]])
-    for k in range(1, 4):
+    for k in range(1, CFG["early"]):
+        order(k, [cols])
+    cols = two(cols, swap_gr(cols, Z1), 64, "quad_cols", after=([rows] if CFG["pr"] else []) + w)
+    for k in range(CFG["early"], 4):
         order(k, [cols])
     left = [rows] + [move_y(rows, k) for k in range(1, 4)]
-    right = call(
-        join_body,
-        "join",
-        [f32(544, D)],
-        [cols] + [move_z(cols, 2 * e) for e in range(1, 4)],
-        after=left[1:] + w[1:],
-    )[0]
-    scratch = [pltpu.VMEM((1, 512), F32), pltpu.VMEM((D, 512), F32)]
-    half_out = [bf16(N, 512), bf16(N, 512), bf16(512, 2 * D), f32(512, D)]
-
-    def own_body(*refs):
-        half_body(*refs, half=0, first=True)
-
-    def other_body(*refs):
-        half_body(*refs, half=1, first=False)
-
-    gh1, gl1, r1, col1, lcat, ltr, bvs = call(
+    beside = swap_gr(cols, CORE)
+    far = move_z(cols, 4)
+    both = call(join_body, "join", [f32(272, D)], [cols, beside])[0]
+    first = move_z_by_core(both, 2)
+
+    def relay(x, name, after):
+        def body(a, out):
+            out[...] = a[...]
+
+        return call(body, name, [f32(*x.shape)], [x], after=after)[0] if after else x
+
+    first = relay(first, "relay_first", [w[k] for k in CFG["r1"]] + left[1:] * CFG["y1"])
+    far = relay(far, "relay_far", [w[k] for k in CFG["r2"]] + left[1:] * CFG["y2"])
+    second = swap_gr(first, CORE)
+    far_beside = swap_gr(far, CORE)
+
+    scratch = [pltpu.VMEM((1, 512), F32)]
+    half_out = [bf16(N, 512), bf16(N, 512), bf16(512, 2 * D)]
+    gh1, gl1, r1, col1, *saved = call(
         own_body,
         "own",
-        half_out + [bf16(N, 2 * D), bf16(2 * D, N), f32(N, 1)],
-        [*w, *lx, *left, right],
+        half_out + [f32(512, D), bf16(N, 2 * D), bf16(2 * D, N), f32(N, 1)],
+        [*w, *lx, *left, cols, beside, first],
+        after=[far] * CFG["ownfar"],
+        flops=CFG["kf"],
         scratch=scratch,
         vmem_mb=24,
     )
-    gh2, gl2, r2, col2 = call(
+    gh2, gl2, r2, keep, give = call(
         other_body,
         "other",
-        half_out,
-        [*w, *lx, *left, swap_gr(right, CORE), lcat, ltr, bvs],
+        half_out + [f32(128, D), f32(512, D)],
+        [*w, *lx, second, far, far_beside, *saved, col1],
+        flops=CFG["kf"],
         scratch=scratch,
         vmem_mb=24,
     )
@@ -329,34 +365,46 @@
     def rows_other(*refs):
         rows_body(*refs, first=False)
 
-    row_own = call(rows_own, "rows_own", [f32(T, D)] * 4, [gh1, gl1, r1], after=[col2], vmem_mb=24)
-    parts = call(
-        quarters_body, "quarters", [f32(128, D)] * 4, [col1, swap_gr(col2, CORE)], after=row_own[:1]
+    row_own = call(rows_own, "rows_own", [f32(T, D)] * 4, [gh1, gl1, r1], after=[keep], vmem_mb=24)
+    near, far, first = call(
+        quarters_body,
+        "quarters",
+        [f32(128, D), f32(128, D), f32(256, D)],
+        [col1, keep, swap_gr(give, CORE)],
+        after=row_own[: CFG["qo"]],
     )
     outs = call(
-        rows_other, "rows_other", [f32(T, D)] * 4, [gh2, gl2, r2, *row_own], after=parts[:1], vmem_mb=24
+        rows_other, "rows_other", [f32(T, D)] * 4, [gh2, gl2, r2, *row_own], after=[near] * CFG["ro"], vmem_mb=24
+    )
+    far = move_z(far, 4)
+    first = move_z_by_core(first, -2)
+    second = swap_gr(first[128:], CORE)
+    col_keep, col_give = call(
+        sum_body, "sum_cols", [f32(64, D)] * 2, [near, far, first, second]
     )
     row_keep, row_give = call(
         sum_body,
         "sum_rows",
         [f32(128, D)] * 2,
         [outs[0]] + [move_y(outs[k], -k) for k in range(1, 4)],
-    )
-    col_keep, col_give = call(
-        sum_body,
-        "sum_cols",
-        [f32(64, D)] * 2,
-        [parts[0]] + [move_z(parts[e], -2 * e) for e in range(1, 4)],
+        after=[col_keep] * CFG["sr"],
     )
     col_keep, col_give = call(
         add_body, "add_cols", [f32(32, D)] * 2, [col_keep, swap_gr(col_give, Z1)]
     )
-    new_rows = call(
-        last_body, "new_rows", [f32(128, D)], [row_embed[0], row_keep, swap_x_hi(row_give)]
-    )[0]
-    new_cols = call(
-        last_body, "new_cols", [f32(32, D)], [col_embed[0], col_keep, swap_gr(col_give, X_LO)]
-    )[0]
+    new_rows, new_cols = call(
+        last_body,
+        "last",
+        [f32(128, D), f32(32, D)],
+        [
+            row_embed[0],
+            row_keep,
+            swap_x_hi(row_give),
+            col_embed[0],
+            col_keep,
+            swap_gr(col_give, X_LO),
+        ],
+    )
     return (new_rows[None], new_cols[None])
 
 

time: 85.6 us -> 75.1 us (0.88)
  the two profiles are of different devices: /device:TPU:24 before, /device:TPU:32 now
where the time goes in v3:
time: 75.1 us; the launch traced here: 74.6 us
  starting transfers between devices  30.3 us (40%)
  waiting for transfers between devices  22.1 us (29%)
  Pallas kernels  20.7 us (28%)
  between operations  1.54 us (2%)
    pallas_call x21, Pallas kernels, call(): pl.pallas_call(run, out_shape=out_shape, in_specs=[SMEM] * smem + [HBM] *...  20.7 us
    ppermute x2, starting transfers between devices, move_z(): lax.ppermute(x, 'gr', [(i, i & 17 | ((i >> 1 & 7) + k) % 8 << 1) for i in...  10.9 us
    ppermute x6, starting transfers between devices, move_y(): return lax.ppermute(x, 'gc', [(i, (i + 2 * k) % 8) for i in range(8)])  8.95 us
    ppermute x9, waiting for transfers between devices, swap_gr(): return lax.ppermute(x, 'gr', [(i, i ^ mask) for i in range(32)])  7.45 us
    ppermute x2, waiting for transfers between devices, move_z(): lax.ppermute(x, 'gr', [(i, i & 17 | ((i >> 1 & 7) + k) % 8 << 1) for i in...  6.1 us
    ppermute x2, waiting for transfers between devices, move_z_by_core(): lax.ppermute(x, 'gr', [(i, i & 17 | ((i >> 1 & 7) + (-k if i & 1 else k))...  5.27 us
    ppermute x9, starting transfers between devices, swap_gr(): return lax.ppermute(x, 'gr', [(i, i ^ mask) for i in range(32)])  4.09 us
    ppermute x2, starting transfers between devices, swap_x_hi(): return lax.ppermute(x, 'gc', [(i, i ^ 1) for i in range(8)])  3.75 us
  transfers between devices with their start and end apart: 21, of which 6 were waited for; matrix products, arithmetic and copies ran while one was open for 0% of the time, Pallas kernels for 22%

profile of v3, /device:TPU:32, one launch (start us, length us, event | category | flops | bytes accessed | tf_op | source)
XLA Modules:
  0.0 74.6 jit_solution(13008142156232048603)
XLA Ops:
  1.3 1.0 %pack.1 = (f32[136,256]{1,0:T(8,128)S(1)}, f32[40,256]{1,0:T(8,128)S(1)}) custom-call(s32[1]{0:T(128)S(6)} %copy.10.refs_0_, f32[128,256]{1,0:T(8,128)} %bitcast.7, f32[32,256]{1,0:T(8,128)} %bitcast.9, s32[1,128]{1,0:T(1,128)} %refs_3_.1, s32[1,32]{1,0:T(1,128)} %refs_4_.1), custom_call_target="tpu_custom_call" | custom-call | bytes 65536 | tf_op jit(solution)/shard_map/pack/pallas_call | solution.py:42
  2.3 1.6 %collective-permute-start = (f32[40,256]{1,0:T(8,128)S(1)}, f32[40,256]{1,0:T(8,128)S(1)}, u32[]{:S(2)}, u32[]{:S(2)}) collective-permute-start(f32[40,256]{1,0:T(8,128)S(1)} %get-tuple-element.53.refs_0_), channel_id=1, source_target_pairs={{0,128},{8,136},{16,144},{24,152},{32,160},{40,168},{48,176},{56,1... | collective-permute-start | bytes 122888 | tf_op jit(solution)/shard_map/ppermute | solution.py:86
  3.9 2.7 %collective-permute-start.2 = (f32[136,256]{1,0:T(8,128)S(1)}, f32[136,256]{1,0:T(8,128)S(1)}, u32[]{:S(2)}, u32[]{:S(2)}) collective-permute-start(f32[136,256]{1,0:T(8,128)S(1)} %get-tuple-element.55.refs_0_), channel_id=1, source_target_pairs={{0,1},{1,0},{2,3},{3,2},{4,5},{5,4},{6,7},{7,6},{8,9},{9,8},{10,11... | collective-permute-start | bytes 417800 | tf_op jit(solution)/shard_map/ppermute | solution.py:68
  6.6 2.8 %digits.1 = (f8e4m3fn[1024,1024]{1,0:T(32,128)(4,1)S(1)}, f8e4m3fn[1024,1024]{1,0:T(32,128)(4,1)S(1)}, f8e4m3fn[1024,1024]{1,0:T(32,128)(4,1)S(1)}, f8e4m3fn[102...) custom-call(s32[1024,1024]{1,0:T(8,128)} %bitcast.11, s32[1,1024]{1,0:T(1,128)} %bitcast.14, s32[1,1024]{1,0:T(1,128)} %bitcast.15), custom_call_target="tpu_custom_call" | custom-call | flops 2147483648 | bytes 65536 | tf_op jit(solution)/shard_map/digits/pallas_call | solution.py:42
  9.4 0.1 pair_cols.1.refs_5_.refs_0_
  9.5 0.1 collective-permute-start.1
  9.6 2.2 %order0.1 = (f32[256,1024]{1,0:T(8,128)S(1)}, f32[256,1024]{1,0:T(8,128)S(1)}) custom-call(f8e4m3fn[1024,1024]{1,0:T(32,128)(4,1)S(1)} %get-tuple-element.48.refs_2_.refs_0_, f8e4m3fn[1024,1024]{1,0:T(32,128)(4,1)S(1)} %get-tuple-element.49.refs_1_, f8e4m3fn[1024,1024]{1,0:T(32,128)(4,1)S(1)} %get-tuple-element.50.refs_2_, ...), custom_call_target="tpu_custom_call" | custom-call | flops 2147483648 | bytes 65536 | tf_op jit(solution)/shard_map/order0/pallas_call | solution.py:42
  11.8 0.0 collective-permute-done.2.refs_1_
  11.8 3.1 %collective-permute-start.10 = (f32[264,256]{1,0:T(8,128)S(1)}, f32[264,256]{1,0:T(8,128)S(1)}, u32[]{:S(2)}, u32[]{:S(2)}) collective-permute-start(f32[264,256]{1,0:T(8,128)S(1)} %pair_rows.1.refs_2_.refs_8_), channel_id=1, source_target_pairs={{0,6},{1,7},{2,0},{3,1},{4,2},{5,3},{6,4},{7,5},{8,14},{9,15},{10,... | collective-permute-start | bytes 811016 | tf_op jit(solution)/shard_map/ppermute | solution.py:64
  14.9 0.6 collective-permute-start.9
  15.5 1.0 %collective-permute-start.8 = (f32[264,256]{1,0:T(8,128)S(1)}, f32[264,256]{1,0:T(8,128)S(1)}, u32[]{:S(2)}, u32[]{:S(2)}) collective-permute-start(f32[264,256]{1,0:T(8,128)S(1)} %pair_rows.1.refs_2_.refs_8_), channel_id=1, source_target_pairs={{0,2},{1,3},{2,4},{3,5},{4,6},{5,7},{6,0},{7,1},{8,10},{9,11},{10,... | collective-permute-start | bytes 811016 | tf_op jit(solution)/shard_map/ppermute | solution.py:64
  16.5 0.1 quad_cols.1.refs_5_.refs_0_.refs_12_
  16.6 7.2 %collective-permute-start.6 = (f32[136,256]{1,0:T(8,128)S(1)}, f32[136,256]{1,0:T(8,128)S(1)}, u32[]{:S(2)}, u32[]{:S(2)}) collective-permute-start(f32[136,256]{1,0:T(8,128)S(1)} %quad_cols.1.refs_5_.refs_0_.refs_12_), channel_id=1, source_target_pairs={{0,64},{8,72},{16,80},{24,88},{32,96},{40,104},{48,112},{56,120},{... | collective-permute-start | bytes 417800 | tf_op jit(solution)/shard_map/ppermute | solution.py:72
  23.8 0.0 collective-permute-start.3
  23.8 2.2 %order3.1 = (f32[256,1024]{1,0:T(8,128)S(1)}, f32[256,1024]{1,0:T(8,128)S(1)}) custom-call(f8e4m3fn[1024,1024]{1,0:T(32,128)(4,1)S(1)} %get-tuple-element.48.refs_2_.refs_0_, f8e4m3fn[1024,1024]{1,0:T(32,128)(4,1)S(1)} %get-tuple-element.49.refs_1_, f8e4m3fn[1024,1024]{1,0:T(32,128)(4,1)S(1)} %get-tuple-element.50.refs_2_, ...), custom_call_target="tpu_custom_call" | custom-call | flops 2147483648 | bytes 65536 | tf_op jit(solution)/shard_map/order3/pallas_call | solution.py:42
  26.0 0.0 collective-permute-done.3.refs_1_.refs_13_
  26.0 1.7 %collective-permute-start.4 = (f32[272,256]{1,0:T(8,128)S(1)}, f32[272,256]{1,0:T(8,128)S(1)}, u32[]{:S(2)}, u32[]{:S(2)}) collective-permute-start(f32[272,256]{1,0:T(8,128)S(1)} %join.1), channel_id=1, source_target_pairs={{0,32},{8,104},{16,48},{24,120},{32,64},{40,8},{48,80},{56,24},{64... | collective-permute-start | bytes 835592 | tf_op jit(solution)/shard_map/ppermute | solution.py:78
  27.8 2.2 %order2.1 = (f32[256,1024]{1,0:T(8,128)S(1)}, f32[256,1024]{1,0:T(8,128)S(1)}) custom-call(f8e4m3fn[1024,1024]{1,0:T(32,128)(4,1)S(1)} %get-tuple-element.48.refs_2_.refs_0_, f8e4m3fn[1024,1024]{1,0:T(32,128)(4,1)S(1)} %get-tuple-element.49.refs_1_, f8e4m3fn[1024,1024]{1,0:T(32,128)(4,1)S(1)} %get-tuple-element.50.refs_2_, ...), custom_call_target="tpu_custom_call" | custom-call | flops 2147483648 | bytes 65536 | tf_op jit(solution)/shard_map/order2/pallas_call | solution.py:42
  29.9 2.2 %order1.1 = (f32[256,1024]{1,0:T(8,128)S(1)}, f32[256,1024]{1,0:T(8,128)S(1)}) custom-call(f8e4m3fn[1024,1024]{1,0:T(32,128)(4,1)S(1)} %get-tuple-element.48.refs_2_.refs_0_, f8e4m3fn[1024,1024]{1,0:T(32,128)(4,1)S(1)} %get-tuple-element.49.refs_1_, f8e4m3fn[1024,1024]{1,0:T(32,128)(4,1)S(1)} %get-tuple-element.50.refs_2_, ...), custom_call_target="tpu_custom_call" | custom-call | flops 2147483648 | bytes 65536 | tf_op jit(solution)/shard_map/order1/pallas_call | solution.py:42
  32.1 0.1 collective-permute-start.7
  32.2 5.3 %collective-permute-done.4.refs_0_ = f32[272,256]{1,0:T(8,128)S(1)} collective-permute-done((f32[272,256]{1,0:T(8,128)S(1)}, f32[272,256]{1,0:T(8,128)S(1)}, u32[]{:S(2)}, u32[]{:S(2)}) %collective-permute-start.4) | collective-permute-done | bytes 278560 | tf_op jit(solution)/shard_map/ppermute | solution.py:78
  37.5 0.1 collective-permute-start.5
  37.6 0.0 collective-permute-done.10.refs_11_
  37.6 0.0 collective-permute-done.9.refs_10_
  37.6 2.7 %own.1 = (bf16[1024,512]{1,0:T(8,128)(2,1)S(1)}, bf16[1024,512]{1,0:T(8,128)(2,1)S(1)}, bf16[512,512]{1,0:T(8,128)(2,1)S(1)}, f32[512,256]{1,0:T(8,128)S(1)}, bf...) custom-call(f32[256,1024]{1,0:T(8,128)S(1)} %get-tuple-element.54.refs_3_.refs_0_, ...), custom_call_target="tpu_custom_call" | custom-call | flops 8589934592 | bytes 65536 | tf_op jit(solution)/shard_map/own/pallas_call | solution.py:42
  40.4 0.0 collective-permute-done.7.refs_10_
  40.4 2.5 %other.1 = (bf16[1024,512]{1,0:T(8,128)(2,1)S(1)}, bf16[1024,512]{1,0:T(8,128)(2,1)S(1)}, bf16[512,512]{1,0:T(8,128)(2,1)S(1)}, f32[128,256]{1,0:T(8,128)S(1)}, f32[512,256]{1,0:T(8,128)S(1)}) custom-call(f32[256,1024]{1,0:T(8,128)S(1)} %get-tuple-element.54.refs_3_.refs_0_, f32[256,1024]{1,0:T(8,128)S(1)} %get-tuple-element.56.refs_1_, ...), custom_call_target="tpu_custom_call" | custom-call | flops 8589934592 | bytes 65536 | tf_op jit(solution)/shard_map/other/pallas_call | solution.py:42
  42.9 0.6 collective-permute-start.11
  43.5 1.0 %rows_own.1 = (f32[256,256]{1,0:T(8,128)S(1)}, f32[256,256]{1,0:T(8,128)S(1)}, f32[256,256]{1,0:T(8,128)S(1)}, f32[256,256]{1,0:T(8,128)S(1)}) custom-call(bf16[1024,512]{1,0:T(8,128)(2,1)S(1)} %get-tuple-element.70.refs_0_, bf16[1024,512]{1,0:T(8,128)(2,1)S(1)} %get-tuple-element.71.refs_1_, bf16[512,512]{1,0:T(8,128)(2,1)S(1)} %get-tuple-element.72.refs_2_, ...), custom_call_target="tpu_custom_call" | custom-call | bytes 65536 | tf_op jit(solution)/shard_map/rows_own/pallas_call | solution.py:42
  44.5 0.0 copy-start
  44.5 0.0 copy-start.1
  44.5 0.5 collective-permute-done.11.refs_2_
  45.0 0.1 quarters.1
  45.1 0.9 %collective-permute-start.16 = (f32[256,256]{1,0:T(8,128)S(1)}, f32[256,256]{1,0:T(8,128)S(1)}, u32[]{:S(2)}, u32[]{:S(2)}) collective-permute-start(f32[256,256]{1,0:T(8,128)S(1)} %get-tuple-element.85), channel_id=1, source_target_pairs={{0,96},{8,40},{16,112},{24,56},{32,0},{40,72},{48,16},{56,88},{64,... | collective-permute-start | bytes 786440 | tf_op jit(solution)/shard_map/ppermute | solution.py:78
  46.0 1.0 %rows_other.1 = (f32[256,256]{1,0:T(8,128)S(1)}, f32[256,256]{1,0:T(8,128)S(1)}, f32[256,256]{1,0:T(8,128)S(1)}, f32[256,256]{1,0:T(8,128)S(1)}) custom-call(bf16[1024,512]{1,0:T(8,128)(2,1)S(1)} %get-tuple-element.67.refs_0_, bf16[1024,512]{1,0:T(8,128)(2,1)S(1)} %get-tuple-element.68.refs_1_, bf16[512,512]{1,0:T(8,128)(2,1)S(1)} %get-tuple-element.69.refs_2_, ...), custom_call_target="tpu_custom_call" | custom-call | bytes 65536 | tf_op jit(solution)/shard_map/rows_other/pallas_call | solution.py:42
  47.0 2.6 %collective-permute-start.12 = (f32[256,256]{1,0:T(8,128)S(1)}, f32[256,256]{1,0:T(8,128)S(1)}, u32[]{:S(2)}, u32[]{:S(2)}) collective-permute-start(f32[256,256]{1,0:T(8,128)S(1)} %get-tuple-element.81), channel_id=1, source_target_pairs={{0,6},{1,7},{2,0},{3,1},{4,2},{5,3},{6,4},{7,5},{8,14},{9,15},{10,... | collective-permute-start | bytes 786440 | tf_op jit(solution)/shard_map/ppermute | solution.py:64
  49.5 1.7 %collective-permute-start.13 = (f32[256,256]{1,0:T(8,128)S(1)}, f32[256,256]{1,0:T(8,128)S(1)}, u32[]{:S(2)}, u32[]{:S(2)}) collective-permute-start(f32[256,256]{1,0:T(8,128)S(1)} %get-tuple-element.82), channel_id=1, source_target_pairs={{0,4},{1,5},{2,6},{3,7},{4,0},{5,1},{6,2},{7,3},{8,12},{9,13},{10,... | collective-permute-start | bytes 786440 | tf_op jit(solution)/shard_map/ppermute | solution.py:64
  51.2 3.7 %collective-permute-start.15 = (f32[128,256]{1,0:T(8,128)S(1)}, f32[128,256]{1,0:T(8,128)S(1)}, u32[]{:S(2)}, u32[]{:S(2)}) collective-permute-start(f32[128,256]{1,0:T(8,128)S(1)} %get-tuple-element.84), channel_id=1, source_target_pairs={{0,64},{8,72},{16,80},{24,88},{32,96},{40,104},{48,112},{56,120},{... | collective-permute-start | bytes 393224 | tf_op jit(solution)/shard_map/ppermute | solution.py:72
  54.9 0.2 collective-permute-start.17
  55.2 6.1 %collective-permute-done.15.refs_1_ = f32[128,256]{1,0:T(8,128)S(1)} collective-permute-done((f32[128,256]{1,0:T(8,128)S(1)}, f32[128,256]{1,0:T(8,128)S(1)}, u32[]{:S(2)}, u32[]{:S(2)}) %collective-permute-start.15) | collective-permute-done | bytes 131104 | tf_op jit(solution)/shard_map/ppermute | solution.py:72
  61.3 3.2 %collective-permute-done.14.refs_3_ = f32[256,256]{1,0:T(8,128)S(1)} collective-permute-done((f32[256,256]{1,0:T(8,128)S(1)}, f32[256,256]{1,0:T(8,128)S(1)}, u32[]{:S(2)}, u32[]{:S(2)}) %collective-permute-start.14) | collective-permute-done | bytes 262176 | tf_op jit(solution)/shard_map/ppermute | solution.py:64
  64.6 0.1 sum_rows.1
  64.6 1.0 %collective-permute-start.18 = (f32[128,256]{1,0:T(8,128)S(1)}, f32[128,256]{1,0:T(8,128)S(1)}, u32[]{:S(2)}, u32[]{:S(2)}) collective-permute-start(f32[128,256]{1,0:T(8,128)S(1)} %get-tuple-element.88), channel_id=1, source_target_pairs={{0,1},{1,0},{2,3},{3,2},{4,5},{5,4},{6,7},{7,6},{8,9},{9,8},{10,11... | collective-permute-start | bytes 393224 | tf_op jit(solution)/shard_map/ppermute | solution.py:68
  65.6 0.7 collective-permute-start.19
  66.4 3.5 %collective-permute-done.19.refs_1_ = f32[64,256]{1,0:T(8,128)S(1)} collective-permute-done((f32[64,256]{1,0:T(8,128)S(1)}, f32[64,256]{1,0:T(8,128)S(1)}, u32[]{:S(2)}, u32[]{:S(2)}) %collective-permute-start.19) | collective-permute-done | bytes 65568 | tf_op jit(solution)/shard_map/ppermute | solution.py:86
  69.9 0.6 collective-permute-start.20
  70.6 3.4 %collective-permute-done.20.refs_5_ = f32[32,256]{1,0:T(8,128)S(1)} collective-permute-done((f32[32,256]{1,0:T(8,128)S(1)}, f32[32,256]{1,0:T(8,128)S(1)}, u32[]{:S(2)}, u32[]{:S(2)}) %collective-permute-start.20) | collective-permute-done | bytes 32800 | tf_op jit(solution)/shard_map/ppermute | solution.py:86
  73.9 0.7 last.1
  (20 shorter events, 0.2 us)
Async XLA Ops:
  2.3 7.1 %collective-permute-start = (f32[40,256]{1,0:T(8,128)S(1)}, f32[40,256]{1,0:T(8,128)S(1)}, u32[]{:S(2)}, u32[]{:S(2)}) collective-permute-start(f32[40,256]{1,0:T(8,128)S(1)} %get-tuple-element.53.refs_0_), channel_id=1, source_target_pairs={{0,128},{8,136},{16,144},{24,152},{32,160},{40,168},{48,176},{56,1... | collective-permute-start | bytes 122888 | tf_op jit(solution)/shard_map/ppermute | solution.py:86
  3.9 7.9 %collective-permute-start.2 = (f32[136,256]{1,0:T(8,128)S(1)}, f32[136,256]{1,0:T(8,128)S(1)}, u32[]{:S(2)}, u32[]{:S(2)}) collective-permute-start(f32[136,256]{1,0:T(8,128)S(1)} %get-tuple-element.55.refs_0_), channel_id=1, source_target_pairs={{0,1},{1,0},{2,3},{3,2},{4,5},{5,4},{6,7},{7,6},{8,9},{9,8},{10,11... | collective-permute-start | bytes 417800 | tf_op jit(solution)/shard_map/ppermute | solution.py:68
  9.5 7.0 %collective-permute-start.1 = (f32[72,256]{1,0:T(8,128)S(1)}, f32[72,256]{1,0:T(8,128)S(1)}, u32[]{:S(2)}, u32[]{:S(2)}) collective-permute-start(f32[72,256]{1,0:T(8,128)S(1)} %pair_cols.1.refs_5_.refs_0_), channel_id=1, source_target_pairs={{0,16},{8,24},{16,0},{24,8},{32,48},{40,56},{48,32},{56,40},{64,80... | collective-permute-start | bytes 221192 | tf_op jit(solution)/shard_map/ppermute | solution.py:86
  11.8 25.8 %collective-permute-start.10 = (f32[264,256]{1,0:T(8,128)S(1)}, f32[264,256]{1,0:T(8,128)S(1)}, u32[]{:S(2)}, u32[]{:S(2)}) collective-permute-start(f32[264,256]{1,0:T(8,128)S(1)} %pair_rows.1.refs_2_.refs_8_), channel_id=1, source_target_pairs={{0,6},{1,7},{2,0},{3,1},{4,2},{5,3},{6,4},{7,5},{8,14},{9,15},{10,... | collective-permute-start | bytes 811016 | tf_op jit(solution)/shard_map/ppermute | solution.py:64
  14.9 22.7 %collective-permute-start.9 = (f32[264,256]{1,0:T(8,128)S(1)}, f32[264,256]{1,0:T(8,128)S(1)}, u32[]{:S(2)}, u32[]{:S(2)}) collective-permute-start(f32[264,256]{1,0:T(8,128)S(1)} %pair_rows.1.refs_2_.refs_8_), channel_id=1, source_target_pairs={{0,4},{1,5},{2,6},{3,7},{4,0},{5,1},{6,2},{7,3},{8,12},{9,13},{10,... | collective-permute-start | bytes 811016 | tf_op jit(solution)/shard_map/ppermute | solution.py:64
  15.5 22.1 %collective-permute-start.8 = (f32[264,256]{1,0:T(8,128)S(1)}, f32[264,256]{1,0:T(8,128)S(1)}, u32[]{:S(2)}, u32[]{:S(2)}) collective-permute-start(f32[264,256]{1,0:T(8,128)S(1)} %pair_rows.1.refs_2_.refs_8_), channel_id=1, source_target_pairs={{0,2},{1,3},{2,4},{3,5},{4,6},{5,7},{6,0},{7,1},{8,10},{9,11},{10,... | collective-permute-start | bytes 811016 | tf_op jit(solution)/shard_map/ppermute | solution.py:64
  16.6 15.5 %collective-permute-start.6 = (f32[136,256]{1,0:T(8,128)S(1)}, f32[136,256]{1,0:T(8,128)S(1)}, u32[]{:S(2)}, u32[]{:S(2)}) collective-permute-start(f32[136,256]{1,0:T(8,128)S(1)} %quad_cols.1.refs_5_.refs_0_.refs_12_), channel_id=1, source_target_pairs={{0,64},{8,72},{16,80},{24,88},{32,96},{40,104},{48,112},{56,120},{... | collective-permute-start | bytes 417800 | tf_op jit(solution)/shard_map/ppermute | solution.py:72
  23.8 2.2 %collective-permute-start.3 = (f32[136,256]{1,0:T(8,128)S(1)}, f32[136,256]{1,0:T(8,128)S(1)}, u32[]{:S(2)}, u32[]{:S(2)}) collective-permute-start(f32[136,256]{1,0:T(8,128)S(1)} %quad_cols.1.refs_5_.refs_0_.refs_12_), channel_id=1, source_target_pairs={{0,8},{8,0},{16,24},{24,16},{32,40},{40,32},{48,56},{56,48},{64,72... | collective-permute-start | bytes 417800 | tf_op jit(solution)/shard_map/ppermute | solution.py:86
  26.0 11.5 %collective-permute-start.4 = (f32[272,256]{1,0:T(8,128)S(1)}, f32[272,256]{1,0:T(8,128)S(1)}, u32[]{:S(2)}, u32[]{:S(2)}) collective-permute-start(f32[272,256]{1,0:T(8,128)S(1)} %join.1), channel_id=1, source_target_pairs={{0,32},{8,104},{16,48},{24,120},{32,64},{40,8},{48,80},{56,24},{64... | collective-permute-start | bytes 835592 | tf_op jit(solution)/shard_map/ppermute | solution.py:78
  32.1 8.3 %collective-permute-start.7 = (f32[136,256]{1,0:T(8,128)S(1)}, f32[136,256]{1,0:T(8,128)S(1)}, u32[]{:S(2)}, u32[]{:S(2)}) collective-permute-start(f32[136,256]{1,0:T(8,128)S(1)} %relay_far.1.refs_9_), channel_id=1, source_target_pairs={{0,8},{8,0},{16,24},{24,16},{32,40},{40,32},{48,56},{56,48},{64,72... | collective-permute-start | bytes 417800 | tf_op jit(solution)/shard_map/ppermute | solution.py:86
  37.5 2.9 %collective-permute-start.5 = (f32[272,256]{1,0:T(8,128)S(1)}, f32[272,256]{1,0:T(8,128)S(1)}, u32[]{:S(2)}, u32[]{:S(2)}) collective-permute-start(f32[272,256]{1,0:T(8,128)S(1)} %relay_first.1.refs_14_), channel_id=1, source_target_pairs={{0,8},{8,0},{16,24},{24,16},{32,40},{40,32},{48,56},{56,48},{64,72... | collective-permute-start | bytes 835592 | tf_op jit(solution)/shard_map/ppermute | solution.py:86
  42.9 2.1 %collective-permute-start.11 = (f32[512,256]{1,0:T(8,128)S(1)}, f32[512,256]{1,0:T(8,128)S(1)}, u32[]{:S(2)}, u32[]{:S(2)}) collective-permute-start(f32[512,256]{1,0:T(8,128)S(1)} %get-tuple-element.78), channel_id=1, source_target_pairs={{0,8},{8,0},{16,24},{24,16},{32,40},{40,32},{48,56},{56,48},{64,72... | collective-permute-start | bytes 1572872 | tf_op jit(solution)/shard_map/ppermute | solution.py:86
  44.5 29.5 %copy-start = (f32[1,128,256]{2,1,0:T(8,128)S(1)}, f32[1,128,256]{2,1,0:T(8,128)}, u32[]{:S(2)}) copy-start(f32[1,128,256]{2,1,0:T(8,128)} %param.11) | copy-start | bytes 393220
  44.5 29.4 %copy-start.1 = (f32[1,32,256]{2,1,0:T(8,128)S(1)}, f32[1,32,256]{2,1,0:T(8,128)}, u32[]{:S(2)}) copy-start(f32[1,32,256]{2,1,0:T(8,128)} %param.12) | copy-start | bytes 98308
  45.1 9.8 %collective-permute-start.16 = (f32[256,256]{1,0:T(8,128)S(1)}, f32[256,256]{1,0:T(8,128)S(1)}, u32[]{:S(2)}, u32[]{:S(2)}) collective-permute-start(f32[256,256]{1,0:T(8,128)S(1)} %get-tuple-element.85), channel_id=1, source_target_pairs={{0,96},{8,40},{16,112},{24,56},{32,0},{40,72},{48,16},{56,88},{64,... | collective-permute-start | bytes 786440 | tf_op jit(solution)/shard_map/ppermute | solution.py:78
  47.0 14.3 %collective-permute-start.12 = (f32[256,256]{1,0:T(8,128)S(1)}, f32[256,256]{1,0:T(8,128)S(1)}, u32[]{:S(2)}, u32[]{:S(2)}) collective-permute-start(f32[256,256]{1,0:T(8,128)S(1)} %get-tuple-element.81), channel_id=1, source_target_pairs={{0,6},{1,7},{2,0},{3,1},{4,2},{5,3},{6,4},{7,5},{8,14},{9,15},{10,... | collective-permute-start | bytes 786440 | tf_op jit(solution)/shard_map/ppermute | solution.py:64
  49.5 11.8 %collective-permute-start.13 = (f32[256,256]{1,0:T(8,128)S(1)}, f32[256,256]{1,0:T(8,128)S(1)}, u32[]{:S(2)}, u32[]{:S(2)}) collective-permute-start(f32[256,256]{1,0:T(8,128)S(1)} %get-tuple-element.82), channel_id=1, source_target_pairs={{0,4},{1,5},{2,6},{3,7},{4,0},{5,1},{6,2},{7,3},{8,12},{9,13},{10,... | collective-permute-start | bytes 786440 | tf_op jit(solution)/shard_map/ppermute | solution.py:64
  51.2 13.3 %collective-permute-start.14 = (f32[256,256]{1,0:T(8,128)S(1)}, f32[256,256]{1,0:T(8,128)S(1)}, u32[]{:S(2)}, u32[]{:S(2)}) collective-permute-start(f32[256,256]{1,0:T(8,128)S(1)} %get-tuple-element.83), channel_id=1, source_target_pairs={{0,2},{1,3},{2,4},{3,5},{4,6},{5,7},{6,0},{7,1},{8,10},{9,11},{10,... | collective-permute-start | bytes 786440 | tf_op jit(solution)/shard_map/ppermute | solution.py:64
  51.2 10.0 %collective-permute-start.15 = (f32[128,256]{1,0:T(8,128)S(1)}, f32[128,256]{1,0:T(8,128)S(1)}, u32[]{:S(2)}, u32[]{:S(2)}) collective-permute-start(f32[128,256]{1,0:T(8,128)S(1)} %get-tuple-element.84), channel_id=1, source_target_pairs={{0,64},{8,72},{16,80},{24,88},{32,96},{40,104},{48,112},{56,120},{... | collective-permute-start | bytes 393224 | tf_op jit(solution)/shard_map/ppermute | solution.py:72
  54.9 6.4 %collective-permute-start.17 = (f32[128,256]{1,0:T(8,128)S(1)}, f32[128,256]{1,0:T(8,128)S(1)}, u32[]{:S(2)}, u32[]{:S(2)}) collective-permute-start(f32[128,256]{1,0:T(8,128)S(1)} %slice.4), channel_id=1, source_target_pairs={{0,8},{8,0},{16,24},{24,16},{32,40},{40,32},{48,56},{56,48},{64,72... | collective-permute-start | bytes 393224 | tf_op jit(solution)/shard_map/ppermute | solution.py:86
  64.6 9.3 %collective-permute-start.18 = (f32[128,256]{1,0:T(8,128)S(1)}, f32[128,256]{1,0:T(8,128)S(1)}, u32[]{:S(2)}, u32[]{:S(2)}) collective-permute-start(f32[128,256]{1,0:T(8,128)S(1)} %get-tuple-element.88), channel_id=1, source_target_pairs={{0,1},{1,0},{2,3},{3,2},{4,5},{5,4},{6,7},{7,6},{8,9},{9,8},{10,11... | collective-permute-start | bytes 393224 | tf_op jit(solution)/shard_map/ppermute | solution.py:68
  65.6 4.3 %collective-permute-start.19 = (f32[64,256]{1,0:T(8,128)S(1)}, f32[64,256]{1,0:T(8,128)S(1)}, u32[]{:S(2)}, u32[]{:S(2)}) collective-permute-start(f32[64,256]{1,0:T(8,128)S(1)} %get-tuple-element.89), channel_id=1, source_target_pairs={{0,16},{8,24},{16,0},{24,8},{32,48},{40,56},{48,32},{56,40},{64,80... | collective-permute-start | bytes 196616 | tf_op jit(solution)/shard_map/ppermute | solution.py:86
  69.9 4.0 %collective-permute-start.20 = (f32[32,256]{1,0:T(8,128)S(1)}, f32[32,256]{1,0:T(8,128)S(1)}, u32[]{:S(2)}, u32[]{:S(2)}) collective-permute-start(f32[32,256]{1,0:T(8,128)S(1)} %get-tuple-element.91), channel_id=1, source_target_pairs={{0,128},{8,136},{16,144},{24,152},{32,160},{40,168},{48,176},{56,1... | collective-permute-start | bytes 98312 | tf_op jit(solution)/shard_map/ppermute | solution.py:86

commit v4 on v3

--- a/solution.py
+++ b/solution.py
@@ -34,6 +34,7 @@
         n = len(operands)
         body(*refs[:n], *refs[n + len(after) :])
 
+    flops = COST.get(name, flops)
     near = len(operands) - smem - far
     operands = [
         pltpu.with_memory_space_constraint(x, pltpu.HBM) if smem <= i < smem + far else x
@@ -87,7 +88,8 @@
 
 
 CORE, Z1, X_LO = 1, 2, 16
-CFG = dict(r1=(1, 2), r2=(3,), y1=0, y2=0, early=1, pr=1, sr=1, qo=1, ro=1, of=31, kf=1 << 33, ownfar=0)
+COST = {'digits': 0, 'order2': 1073741824, 'other': 4294967296, 'rows_other': 1073741824, 'rows': 17179869184, 'quarters': 1073741824, 'arrived': 0, 'pair_rows': 4294967296, 'sum_cols': 134217728}
+CFG = {'ao': 0, 'sy': 0, 'r1': (1, 2), 'r2': (3,), 'y1': 1, 'y2': 0, 'early': 1, 'pr': 1, 'sr': 0, 'qo': 1, 'ro': 0, 'of': 31, 'kf': 8589934592, 'ownfar': 0, 'mc': 1, 'rf': 1, 'rz': 0, 'cr': (1,)}
 
 
 def pack_body(total, rows, cols, rm, cm, row_out, col_out, rmv, cmv, sems):
@@ -215,16 +217,12 @@
     col[...] = half_body(w, lx, left, right, (lcat, ltr, bvs), (gh, gl, rcat), bc, half=0)
 
 
-def other_body(*refs):
-    w, lx = refs[:4], refs[4:8]
-    second, far, far_beside = refs[8:11]
-    saved = refs[11:14]
-    col1 = refs[14]
-    gh, gl, rcat, keep, give = refs[15:20]
-    (bc,) = refs[20:]
+def other_body(sums, right, *refs):
+    saved = refs[:3]
+    col1 = refs[3]
+    gh, gl, rcat, keep, give, bc = refs[4:]
     give[:128, :] = col1[128:256, :]
-    right = [(second, 136), (second, 0), (far, 0), (far_beside, 0)]
-    col = half_body(w, lx, None, right, saved, (gh, gl, rcat), bc, half=1)
+    col = half_body(sums[:4], sums[4:], None, right, saved, (gh, gl, rcat), bc, half=1)
     give[256:512, :] = col[:256]
     keep[...] = col[256:384]
     give[128:256, :] = col[384:]
@@ -252,11 +250,21 @@
     first_out[128:, :] = col1[384:, :] + got[256:384, :]
 
 
-def sum_body(a, b, c, d, keep, give):
+def sum_body(*refs):
+    *terms, keep, give = refs
     n = keep.shape[0]
-    m = 2 * n
-    keep[...] = (a[:n, :] + b[:n, :]) + (c[:n, :] + d[:n, :])
-    give[...] = (a[n:m, :] + b[n:m, :]) + (c[n:m, :] + d[n:m, :])
+    for out, at in ((keep, 0), (give, n)):
+        total = terms[0][at : at + n, :]
+        for t in terms[1:]:
+            total = total + t[at : at + n, :]
+        out[...] = total
+
+
+def fold_body(one, low, three, high, down, up):
+    down[:128, :] = one[:128, :] + low[...]
+    down[128:, :] = one[128:, :]
+    up[:128, :] = three[:128, :]
+    up[128:, :] = three[128:, :] + high[...]
 
 
 def add_body(a, b, keep, give):
@@ -326,16 +334,20 @@
     both = call(join_body, "join", [f32(272, D)], [cols, beside])[0]
     first = move_z_by_core(both, 2)
 
-    def relay(x, name, after):
-        def body(a, out):
-            out[...] = a[...]
-
-        return call(body, name, [f32(*x.shape)], [x], after=after)[0] if after else x
-
-    first = relay(first, "relay_first", [w[k] for k in CFG["r1"]] + left[1:] * CFG["y1"])
-    far = relay(far, "relay_far", [w[k] for k in CFG["r2"]] + left[1:] * CFG["y2"])
-    second = swap_gr(first, CORE)
-    far_beside = swap_gr(far, CORE)
+    def relay(name, parts, after):
+        def body(*refs):
+            at = 0
+            for p in refs[:-1]:
+                refs[-1][at : at + p.shape[0], :] = p[...]
+                at += p.shape[0]
+
+        rows = sum(p.shape[0] for p in parts)
+        return call(body, name, [f32(rows, D)], parts, after=after)[0]
+
+    def other_run(*refs):
+        n = 8 + len(crossed)
+        right = [(refs[8 + i], at) for i, at in spots]
+        other_body(refs[:8], right, *refs[n:])
 
     scratch = [pltpu.VMEM((1, 512), F32)]
     half_out = [bf16(N, 512), bf16(N, 512), bf16(512, 2 * D)]
@@ -349,11 +361,22 @@
         scratch=scratch,
         vmem_mb=24,
     )
+    if CFG["mc"]:
+        give = relay("arrived", [first, far], [w[k] for k in CFG["cr"]] + left[1:] * CFG["y1"] + [gh1] * CFG["ao"])
+        second = swap_gr(give, CORE)
+        crossed = [second, far]
+        spots = [(0, 136), (0, 0), (1, 0), (0, 272)]
+    else:
+        first = relay("relay_first", [first], [w[k] for k in CFG["r1"]] + left[1:] * CFG["y1"])
+        far = relay("relay_far", [far], [w[k] for k in CFG["r2"]] + left[1:] * CFG["y2"])
+        crossed = [swap_gr(first, CORE), far, swap_gr(far, CORE)]
+        spots = [(0, 136), (0, 0), (1, 0), (2, 0)]
+
     gh2, gl2, r2, keep, give = call(
-        other_body,
+        other_run,
         "other",
         half_out + [f32(128, D), f32(512, D)],
-        [*w, *lx, second, far, far_beside, *saved, col1],
+        [*w, *lx, *crossed, *saved, col1],
         flops=CFG["kf"],
         scratch=scratch,
         vmem_mb=24,
@@ -365,7 +388,24 @@
     def rows_other(*refs):
         rows_body(*refs, first=False)
 
-    row_own = call(rows_own, "rows_own", [f32(T, D)] * 4, [gh1, gl1, r1], after=[keep], vmem_mb=24)
+    def rows_all(*refs):
+        outs = refs[-4:]
+        for k in (2, 1, 3, 0):
+            s = slice(T * k, T * (k + 1))
+            total = 0.0
+            for gh, gl, r in (refs[:3], refs[3:6]):
+                rr = dot(gh[s, :], r[...], NN)
+                total += rr[:, :D] + rr[:, D:] + dot(gl[s, :], r[:, :D], NN)
+            outs[k][...] = total
+
+    if CFG["rf"]:
+        row_own = outs = call(
+            rows_all, "rows", [f32(T, D)] * 4, [gh1, gl1, r1, gh2, gl2, r2], vmem_mb=24
+        )
+    else:
+        row_own = call(
+            rows_own, "rows_own", [f32(T, D)] * 4, [gh1, gl1, r1], after=[keep], vmem_mb=24
+        )
     near, far, first = call(
         quarters_body,
         "quarters",
@@ -373,21 +413,33 @@
         [col1, keep, swap_gr(give, CORE)],
         after=row_own[: CFG["qo"]],
     )
-    outs = call(
-        rows_other, "rows_other", [f32(T, D)] * 4, [gh2, gl2, r2, *row_own], after=[near] * CFG["ro"], vmem_mb=24
-    )
+    if not CFG["rf"]:
+        outs = call(
+            rows_other,
+            "rows_other",
+            [f32(T, D)] * 4,
+            [gh2, gl2, r2, *row_own],
+            after=[near] * CFG["ro"],
+            vmem_mb=24,
+        )
     far = move_z(far, 4)
     first = move_z_by_core(first, -2)
-    second = swap_gr(first[128:], CORE)
+    second = first[128:]
+    if CFG["rz"]:
+        second = relay("relay_far_sum", [second], [far])
+    second = swap_gr(second, CORE)
     col_keep, col_give = call(
         sum_body, "sum_cols", [f32(64, D)] * 2, [near, far, first, second]
     )
+    if CFG["sy"]:
+        low = move_y(outs[2][:128], -1)
+        high = move_y(outs[2][128:], 1)
+        down, up = call(fold_body, "fold", [f32(T, D)] * 2, [outs[1], low, outs[3], high])
+        row_terms = [outs[0], move_y(down, -1), move_y(up, 1)]
+    else:
+        row_terms = [outs[0]] + [move_y(outs[k], -k) for k in range(1, 4)]
     row_keep, row_give = call(
-        sum_body,
-        "sum_rows",
-        [f32(128, D)] * 2,
-        [outs[0]] + [move_y(outs[k], -k) for k in range(1, 4)],
-        after=[col_keep] * CFG["sr"],
+        sum_body, "sum_rows", [f32(128, D)] * 2, row_terms, after=[col_keep] * CFG["sr"]
     )
     col_keep, col_give = call(
         add_body, "add_cols", [f32(32, D)] * 2, [col_keep, swap_gr(col_give, Z1)]

time: 75.1 us -> 74.7 us (level)
    ppermute x2, waiting for transfers between devices: 6.1 us -> 0.01 us  [move_z(): lax.ppermute(x, 'gr', [(i, i & 17 | ((i >> 1 & 7) + k) % 8 << 1) for i in...]
    ppermute x2, waiting for transfers between devices: 5.27 us -> 8.52 us  [move_z_by_core(): lax.ppermute(x, 'gr', [(i, i & 17 | ((i >> 1 & 7) + (-k if i & 1 else k))...]
    ppermute x6, waiting for transfers between devices: 3.25 us -> 6 us  [move_y(): return lax.ppermute(x, 'gc', [(i, (i + 2 * k) % 8) for i in range(8)])]
    ppermute x2, starting transfers between devices: 2.63 us -> 4.21 us  [move_z_by_core(): lax.ppermute(x, 'gr', [(i, i & 17 | ((i >> 1 & 7) + (-k if i & 1 else k))...]
    ppermute x2, waiting for transfers between devices: 0.01 us -> 1.1 us  [swap_x_hi(): return lax.ppermute(x, 'gc', [(i, i ^ 1) for i in range(8)])]
    ppermute x9 -> x8, waiting for transfers between devices: 7.45 us -> 6.49 us  [swap_gr(): return lax.ppermute(x, 'gr', [(i, i ^ mask) for i in range(32)])]
    ppermute x9 -> x8, starting transfers between devices: 4.09 us -> 3.29 us  [swap_gr(): return lax.ppermute(x, 'gr', [(i, i ^ mask) for i in range(32)])]
    pallas_call x21 -> x19, Pallas kernels: 20.7 us -> 20.5 us  [call(): pl.pallas_call(run, out_shape=out_shape, in_specs=[SMEM] * smem + [HBM] *...]
  transfers between devices with their start and end apart: 21 -> 20, of which waited for: 6 -> 8; matrix products, arithmetic and copies ran while one was open for 0% -> 0% of each run, Pallas kernels for 22% -> 22%
where the time goes in v4:
time: 74.7 us; the launch traced here: 74.6 us
  starting transfers between devices  30.4 us (41%)
  waiting for transfers between devices  22.1 us (30%)
  Pallas kernels  20.5 us (27%)
  between operations  1.51 us (2%)
    pallas_call x19, Pallas kernels, call(): pl.pallas_call(run, out_shape=out_shape, in_specs=[SMEM] * smem + [HBM] *...  20.5 us
    ppermute x2, starting transfers between devices, move_z(): lax.ppermute(x, 'gr', [(i, i & 17 | ((i >> 1 & 7) + k) % 8 << 1) for i in...  10.7 us
    ppermute x6, starting transfers between devices, move_y(): return lax.ppermute(x, 'gc', [(i, (i + 2 * k) % 8) for i in range(8)])  8.64 us
    ppermute x2, waiting for transfers between devices, move_z_by_core(): lax.ppermute(x, 'gr', [(i, i & 17 | ((i >> 1 & 7) + (-k if i & 1 else k))...  8.52 us
    ppermute x8, waiting for transfers between devices, swap_gr(): return lax.ppermute(x, 'gr', [(i, i ^ mask) for i in range(32)])  6.49 us
    ppermute x6, waiting for transfers between devices, move_y(): return lax.ppermute(x, 'gc', [(i, (i + 2 * k) % 8) for i in range(8)])  6 us
    ppermute x2, starting transfers between devices, move_z_by_core(): lax.ppermute(x, 'gr', [(i, i & 17 | ((i >> 1 & 7) + (-k if i & 1 else k))...  4.21 us
    ppermute x2, starting transfers between devices, swap_x_hi(): return lax.ppermute(x, 'gc', [(i, i ^ 1) for i in range(8)])  3.61 us
  transfers between devices with their start and end apart: 20, of which 8 were waited for; matrix products, arithmetic and copies ran while one was open for 0% of the time, Pallas kernels for 22%

profile of v4, /device:TPU:32, one launch (start us, length us, event | category | flops | bytes accessed | tf_op | source)
XLA Modules:
  0.0 74.6 jit_solution(14002267181992779896)
XLA Ops:
  1.3 1.0 %pack.1 = (f32[136,256]{1,0:T(8,128)S(1)}, f32[40,256]{1,0:T(8,128)S(1)}) custom-call(s32[1]{0:T(128)S(6)} %copy.10.refs_0_, f32[128,256]{1,0:T(8,128)} %bitcast.7, f32[32,256]{1,0:T(8,128)} %bitcast.9, s32[1,128]{1,0:T(1,128)} %refs_3_.1, s32[1,32]{1,0:T(1,128)} %refs_4_.1), custom_call_target="tpu_custom_call" | custom-call | bytes 65536 | tf_op jit(solution)/shard_map/pack/pallas_call | solution.py:43
  2.3 1.6 %collective-permute-start = (f32[40,256]{1,0:T(8,128)S(1)}, f32[40,256]{1,0:T(8,128)S(1)}, u32[]{:S(2)}, u32[]{:S(2)}) collective-permute-start(f32[40,256]{1,0:T(8,128)S(1)} %get-tuple-element.49.refs_0_), channel_id=1, source_target_pairs={{0,128},{8,136},{16,144},{24,152},{32,160},{40,168},{48,176},{56,1... | collective-permute-start | bytes 122888 | tf_op jit(solution)/shard_map/ppermute | solution.py:87
  3.9 2.7 %collective-permute-start.2 = (f32[136,256]{1,0:T(8,128)S(1)}, f32[136,256]{1,0:T(8,128)S(1)}, u32[]{:S(2)}, u32[]{:S(2)}) collective-permute-start(f32[136,256]{1,0:T(8,128)S(1)} %get-tuple-element.51.refs_0_), channel_id=1, source_target_pairs={{0,1},{1,0},{2,3},{3,2},{4,5},{5,4},{6,7},{7,6},{8,9},{9,8},{10,11... | collective-permute-start | bytes 417800 | tf_op jit(solution)/shard_map/ppermute | solution.py:69
  6.6 2.8 %digits.1 = (f8e4m3fn[1024,1024]{1,0:T(32,128)(4,1)S(1)}, f8e4m3fn[1024,1024]{1,0:T(32,128)(4,1)S(1)}, f8e4m3fn[1024,1024]{1,0:T(32,128)(4,1)S(1)}, f8e4m3fn[102...) custom-call(s32[1024,1024]{1,0:T(8,128)} %bitcast.11, s32[1,1024]{1,0:T(1,128)} %bitcast.12, s32[1,1024]{1,0:T(1,128)} %bitcast.13), custom_call_target="tpu_custom_call" | custom-call | bytes 65536 | tf_op jit(solution)/shard_map/digits/pallas_call | solution.py:43
  9.4 0.0 collective-permute-done.refs_1_
  9.4 0.1 pair_cols.1.refs_5_.refs_0_
  9.5 0.1 collective-permute-start.1
  9.6 2.2 %order0.1 = (f32[256,1024]{1,0:T(8,128)S(1)}, f32[256,1024]{1,0:T(8,128)S(1)}) custom-call(f8e4m3fn[1024,1024]{1,0:T(32,128)(4,1)S(1)} %get-tuple-element.44.refs_2_.refs_0_, f8e4m3fn[1024,1024]{1,0:T(32,128)(4,1)S(1)} %get-tuple-element.45.refs_1_, f8e4m3fn[1024,1024]{1,0:T(32,128)(4,1)S(1)} %get-tuple-element.46.refs_2_, ...), custom_call_target="tpu_custom_call" | custom-call | flops 2147483648 | bytes 65536 | tf_op jit(solution)/shard_map/order0/pallas_call | solution.py:43
  11.8 0.0 collective-permute-done.2.refs_1_
  11.8 1.7 %collective-permute-start.3 = (f32[264,256]{1,0:T(8,128)S(1)}, f32[264,256]{1,0:T(8,128)S(1)}, u32[]{:S(2)}, u32[]{:S(2)}) collective-permute-start(f32[264,256]{1,0:T(8,128)S(1)} %pair_rows.1.refs_2_.refs_8_), channel_id=1, source_target_pairs={{0,2},{1,3},{2,4},{3,5},{4,6},{5,7},{6,0},{7,1},{8,10},{9,11},{10,... | collective-permute-start | bytes 811016 | tf_op jit(solution)/shard_map/ppermute | solution.py:65
  13.5 2.9 %collective-permute-start.4 = (f32[264,256]{1,0:T(8,128)S(1)}, f32[264,256]{1,0:T(8,128)S(1)}, u32[]{:S(2)}, u32[]{:S(2)}) collective-permute-start(f32[264,256]{1,0:T(8,128)S(1)} %pair_rows.1.refs_2_.refs_8_), channel_id=1, source_target_pairs={{0,4},{1,5},{2,6},{3,7},{4,0},{5,1},{6,2},{7,3},{8,12},{9,13},{10,... | collective-permute-start | bytes 811016 | tf_op jit(solution)/shard_map/ppermute | solution.py:65
  16.4 1.3 %collective-permute-start.5 = (f32[264,256]{1,0:T(8,128)S(1)}, f32[264,256]{1,0:T(8,128)S(1)}, u32[]{:S(2)}, u32[]{:S(2)}) collective-permute-start(f32[264,256]{1,0:T(8,128)S(1)} %pair_rows.1.refs_2_.refs_8_), channel_id=1, source_target_pairs={{0,6},{1,7},{2,0},{3,1},{4,2},{5,3},{6,4},{7,5},{8,14},{9,15},{10,... | collective-permute-start | bytes 811016 | tf_op jit(solution)/shard_map/ppermute | solution.py:65
  17.7 0.1 quad_cols.1.refs_5_.refs_0_.refs_12_
  17.8 0.0 collective-permute-start.6
  17.9 7.3 %collective-permute-start.8 = (f32[136,256]{1,0:T(8,128)S(1)}, f32[136,256]{1,0:T(8,128)S(1)}, u32[]{:S(2)}, u32[]{:S(2)}) collective-permute-start(f32[136,256]{1,0:T(8,128)S(1)} %quad_cols.1.refs_5_.refs_0_.refs_12_), channel_id=1, source_target_pairs={{0,64},{8,72},{16,80},{24,88},{32,96},{40,104},{48,112},{56,120},{... | collective-permute-start | bytes 417800 | tf_op jit(solution)/shard_map/ppermute | solution.py:73
  25.1 2.2 %order1.1 = (f32[256,1024]{1,0:T(8,128)S(1)}, f32[256,1024]{1,0:T(8,128)S(1)}) custom-call(f8e4m3fn[1024,1024]{1,0:T(32,128)(4,1)S(1)} %get-tuple-element.44.refs_2_.refs_0_, f8e4m3fn[1024,1024]{1,0:T(32,128)(4,1)S(1)} %get-tuple-element.45.refs_1_, f8e4m3fn[1024,1024]{1,0:T(32,128)(4,1)S(1)} %get-tuple-element.46.refs_2_, ...), custom_call_target="tpu_custom_call" | custom-call | flops 2147483648 | bytes 65536 | tf_op jit(solution)/shard_map/order1/pallas_call | solution.py:43
  27.3 0.0 collective-permute-done.6.refs_1_.refs_13_
  27.3 1.7 %collective-permute-start.7 = (f32[272,256]{1,0:T(8,128)S(1)}, f32[272,256]{1,0:T(8,128)S(1)}, u32[]{:S(2)}, u32[]{:S(2)}) collective-permute-start(f32[272,256]{1,0:T(8,128)S(1)} %join.1), channel_id=1, source_target_pairs={{0,32},{8,104},{16,48},{24,120},{32,64},{40,8},{48,80},{56,24},{64... | collective-permute-start | bytes 835592 | tf_op jit(solution)/shard_map/ppermute | solution.py:79
  29.1 2.2 %order3.1 = (f32[256,1024]{1,0:T(8,128)S(1)}, f32[256,1024]{1,0:T(8,128)S(1)}) custom-call(f8e4m3fn[1024,1024]{1,0:T(32,128)(4,1)S(1)} %get-tuple-element.44.refs_2_.refs_0_, f8e4m3fn[1024,1024]{1,0:T(32,128)(4,1)S(1)} %get-tuple-element.45.refs_1_, f8e4m3fn[1024,1024]{1,0:T(32,128)(4,1)S(1)} %get-tuple-element.46.refs_2_, ...), custom_call_target="tpu_custom_call" | custom-call | flops 2147483648 | bytes 65536 | tf_op jit(solution)/shard_map/order3/pallas_call | solution.py:43
  31.2 2.2 %order2.1 = (f32[256,1024]{1,0:T(8,128)S(1)}, f32[256,1024]{1,0:T(8,128)S(1)}) custom-call(f8e4m3fn[1024,1024]{1,0:T(32,128)(4,1)S(1)} %get-tuple-element.44.refs_2_.refs_0_, f8e4m3fn[1024,1024]{1,0:T(32,128)(4,1)S(1)} %get-tuple-element.45.refs_1_, f8e4m3fn[1024,1024]{1,0:T(32,128)(4,1)S(1)} %get-tuple-element.46.refs_2_, ...), custom_call_target="tpu_custom_call" | custom-call | flops 1073741824 | bytes 65536 | tf_op jit(solution)/shard_map/order2/pallas_call | solution.py:43
  33.4 0.0 collective-permute-done.8.refs_1_.refs_9_
  33.4 0.0 collective-permute-done.4.refs_10_.refs_4_
  33.4 0.0 collective-permute-done.5.refs_11_.refs_5_
  33.4 5.8 %collective-permute-done.7.refs_14_.refs_0_ = f32[272,256]{1,0:T(8,128)S(1)} collective-permute-done((f32[272,256]{1,0:T(8,128)S(1)}, f32[272,256]{1,0:T(8,128)S(1)}, u32[]{:S(2)}, u32[]{:S(2)}) %collective-permute-start.7) | collective-permute-done | bytes 278560 | tf_op jit(solution)/shard_map/ppermute | solution.py:79
  39.3 0.1 collective-permute-start.9
  39.4 2.8 %own.1 = (bf16[1024,512]{1,0:T(8,128)(2,1)S(1)}, bf16[1024,512]{1,0:T(8,128)(2,1)S(1)}, bf16[512,512]{1,0:T(8,128)(2,1)S(1)}, f32[512,256]{1,0:T(8,128)S(1)}, bf...) custom-call(f32[256,1024]{1,0:T(8,128)S(1)} %get-tuple-element.50.refs_3_.refs_0_, ...), custom_call_target="tpu_custom_call" | custom-call | flops 8589934592 | bytes 65536 | tf_op jit(solution)/shard_map/own/pallas_call | solution.py:43
  42.1 2.5 %other.1 = (bf16[1024,512]{1,0:T(8,128)(2,1)S(1)}, bf16[1024,512]{1,0:T(8,128)(2,1)S(1)}, bf16[512,512]{1,0:T(8,128)(2,1)S(1)}, f32[128,256]{1,0:T(8,128)S(1)}, f32[512,256]{1,0:T(8,128)S(1)}) custom-call(f32[256,1024]{1,0:T(8,128)S(1)} %get-tuple-element.50.refs_3_.refs_0_, f32[256,1024]{1,0:T(8,128)S(1)} %get-tuple-element.52.refs_1_.refs_2_, ...), custom_call_target="tpu_custom_call" | custom-call | flops 4294967296 | bytes 65536 | tf_op jit(solution)/shard_map/other/pallas_call | solution.py:43
  44.6 0.6 collective-permute-start.14
  45.2 1.8 %rows.1 = (f32[256,256]{1,0:T(8,128)S(1)}, f32[256,256]{1,0:T(8,128)S(1)}, f32[256,256]{1,0:T(8,128)S(1)}, f32[256,256]{1,0:T(8,128)S(1)}) custom-call(bf16[1024,512]{1,0:T(8,128)(2,1)S(1)} %get-tuple-element.59.refs_0_, bf16[1024,512]{1,0:T(8,128)(2,1)S(1)} %get-tuple-element.60.refs_1_, bf16[512,512]{1,0:T(8,128)(2,1)S(1)} %get-tuple-element.61.refs_2_, ...), custom_call_target="tpu_custom_call" | custom-call | flops 17179869184 | bytes 65536 | tf_op jit(solution)/shard_map/rows/pallas_call | solution.py:43
  47.0 0.0 copy-start
  47.0 0.0 copy-start.1
  47.0 0.1 quarters.1
  47.1 2.5 %collective-permute-start.16 = (f32[256,256]{1,0:T(8,128)S(1)}, f32[256,256]{1,0:T(8,128)S(1)}, u32[]{:S(2)}, u32[]{:S(2)}) collective-permute-start(f32[256,256]{1,0:T(8,128)S(1)} %get-tuple-element.79), channel_id=1, source_target_pairs={{0,96},{8,40},{16,112},{24,56},{32,0},{40,72},{48,16},{56,88},{64,... | collective-permute-start | bytes 786440 | tf_op jit(solution)/shard_map/ppermute | solution.py:79
  49.6 2.7 %collective-permute-start.11 = (f32[256,256]{1,0:T(8,128)S(1)}, f32[256,256]{1,0:T(8,128)S(1)}, u32[]{:S(2)}, u32[]{:S(2)}) collective-permute-start(f32[256,256]{1,0:T(8,128)S(1)} %get-tuple-element.71), channel_id=1, source_target_pairs={{0,4},{1,5},{2,6},{3,7},{4,0},{5,1},{6,2},{7,3},{8,12},{9,13},{10,... | collective-permute-start | bytes 786440 | tf_op jit(solution)/shard_map/ppermute | solution.py:65
  52.3 0.0 collective-permute-start.12
  52.3 3.4 %collective-permute-start.15 = (f32[128,256]{1,0:T(8,128)S(1)}, f32[128,256]{1,0:T(8,128)S(1)}, u32[]{:S(2)}, u32[]{:S(2)}) collective-permute-start(f32[128,256]{1,0:T(8,128)S(1)} %get-tuple-element.78), channel_id=1, source_target_pairs={{0,64},{8,72},{16,80},{24,88},{32,96},{40,104},{48,112},{56,120},{... | collective-permute-start | bytes 393224 | tf_op jit(solution)/shard_map/ppermute | solution.py:73
  55.7 2.7 %collective-permute-done.16.refs_2_ = f32[256,256]{1,0:T(8,128)S(1)} collective-permute-done((f32[256,256]{1,0:T(8,128)S(1)}, f32[256,256]{1,0:T(8,128)S(1)}, u32[]{:S(2)}, u32[]{:S(2)}) %collective-permute-start.16) | collective-permute-done | bytes 262176 | tf_op jit(solution)/shard_map/ppermute | solution.py:79
  58.5 0.1 collective-permute-start.17
  58.6 0.3 collective-permute-done.10.refs_1_
  58.8 1.6 %collective-permute-done.11.refs_2_ = f32[256,256]{1,0:T(8,128)S(1)} collective-permute-done((f32[256,256]{1,0:T(8,128)S(1)}, f32[256,256]{1,0:T(8,128)S(1)}, u32[]{:S(2)}, u32[]{:S(2)}) %collective-permute-start.11) | collective-permute-done | bytes 262176 | tf_op jit(solution)/shard_map/ppermute | solution.py:65
  60.4 4.2 %collective-permute-done.12.refs_3_ = f32[256,256]{1,0:T(8,128)S(1)} collective-permute-done((f32[256,256]{1,0:T(8,128)S(1)}, f32[256,256]{1,0:T(8,128)S(1)}, u32[]{:S(2)}, u32[]{:S(2)}) %collective-permute-start.12) | collective-permute-done | bytes 262176 | tf_op jit(solution)/shard_map/ppermute | solution.py:65
  64.6 0.9 %collective-permute-start.13 = (f32[128,256]{1,0:T(8,128)S(1)}, f32[128,256]{1,0:T(8,128)S(1)}, u32[]{:S(2)}, u32[]{:S(2)}) collective-permute-start(f32[128,256]{1,0:T(8,128)S(1)} %get-tuple-element.74), channel_id=1, source_target_pairs={{0,1},{1,0},{2,3},{3,2},{4,5},{5,4},{6,7},{7,6},{8,9},{9,8},{10,11... | collective-permute-start | bytes 393224 | tf_op jit(solution)/shard_map/ppermute | solution.py:69
  65.5 0.2 collective-permute-start.18
  65.7 4.2 %collective-permute-done.18.refs_1_ = f32[64,256]{1,0:T(8,128)S(1)} collective-permute-done((f32[64,256]{1,0:T(8,128)S(1)}, f32[64,256]{1,0:T(8,128)S(1)}, u32[]{:S(2)}, u32[]{:S(2)}) %collective-permute-start.18) | collective-permute-done | bytes 65568 | tf_op jit(solution)/shard_map/ppermute | solution.py:87
  69.9 0.6 collective-permute-start.19
  70.5 1.1 %collective-permute-done.13.refs_2_ = f32[128,256]{1,0:T(8,128)S(1)} collective-permute-done((f32[128,256]{1,0:T(8,128)S(1)}, f32[128,256]{1,0:T(8,128)S(1)}, u32[]{:S(2)}, u32[]{:S(2)}) %collective-permute-start.13) | collective-permute-done | bytes 131104 | tf_op jit(solution)/shard_map/ppermute | solution.py:69
  71.6 2.3 %collective-permute-done.19.refs_5_ = f32[32,256]{1,0:T(8,128)S(1)} collective-permute-done((f32[32,256]{1,0:T(8,128)S(1)}, f32[32,256]{1,0:T(8,128)S(1)}, u32[]{:S(2)}, u32[]{:S(2)}) %collective-permute-start.19) | collective-permute-done | bytes 32800 | tf_op jit(solution)/shard_map/ppermute | solution.py:87
  73.9 0.7 last.1
  (16 shorter events, 0.2 us)
Async XLA Ops:
  2.3 7.1 %collective-permute-start = (f32[40,256]{1,0:T(8,128)S(1)}, f32[40,256]{1,0:T(8,128)S(1)}, u32[]{:S(2)}, u32[]{:S(2)}) collective-permute-start(f32[40,256]{1,0:T(8,128)S(1)} %get-tuple-element.49.refs_0_), channel_id=1, source_target_pairs={{0,128},{8,136},{16,144},{24,152},{32,160},{40,168},{48,176},{56,1... | collective-permute-start | bytes 122888 | tf_op jit(solution)/shard_map/ppermute | solution.py:87
  3.9 7.9 %collective-permute-start.2 = (f32[136,256]{1,0:T(8,128)S(1)}, f32[136,256]{1,0:T(8,128)S(1)}, u32[]{:S(2)}, u32[]{:S(2)}) collective-permute-start(f32[136,256]{1,0:T(8,128)S(1)} %get-tuple-element.51.refs_0_), channel_id=1, source_target_pairs={{0,1},{1,0},{2,3},{3,2},{4,5},{5,4},{6,7},{7,6},{8,9},{9,8},{10,11... | collective-permute-start | bytes 417800 | tf_op jit(solution)/shard_map/ppermute | solution.py:69
  9.5 8.3 %collective-permute-start.1 = (f32[72,256]{1,0:T(8,128)S(1)}, f32[72,256]{1,0:T(8,128)S(1)}, u32[]{:S(2)}, u32[]{:S(2)}) collective-permute-start(f32[72,256]{1,0:T(8,128)S(1)} %pair_cols.1.refs_5_.refs_0_), channel_id=1, source_target_pairs={{0,16},{8,24},{16,0},{24,8},{32,48},{40,56},{48,32},{56,40},{64,80... | collective-permute-start | bytes 221192 | tf_op jit(solution)/shard_map/ppermute | solution.py:87
  11.8 21.6 %collective-permute-start.3 = (f32[264,256]{1,0:T(8,128)S(1)}, f32[264,256]{1,0:T(8,128)S(1)}, u32[]{:S(2)}, u32[]{:S(2)}) collective-permute-start(f32[264,256]{1,0:T(8,128)S(1)} %pair_rows.1.refs_2_.refs_8_), channel_id=1, source_target_pairs={{0,2},{1,3},{2,4},{3,5},{4,6},{5,7},{6,0},{7,1},{8,10},{9,11},{10,... | collective-permute-start | bytes 811016 | tf_op jit(solution)/shard_map/ppermute | solution.py:65
  13.5 19.9 %collective-permute-start.4 = (f32[264,256]{1,0:T(8,128)S(1)}, f32[264,256]{1,0:T(8,128)S(1)}, u32[]{:S(2)}, u32[]{:S(2)}) collective-permute-start(f32[264,256]{1,0:T(8,128)S(1)} %pair_rows.1.refs_2_.refs_8_), channel_id=1, source_target_pairs={{0,4},{1,5},{2,6},{3,7},{4,0},{5,1},{6,2},{7,3},{8,12},{9,13},{10,... | collective-permute-start | bytes 811016 | tf_op jit(solution)/shard_map/ppermute | solution.py:65
  16.4 17.0 %collective-permute-start.5 = (f32[264,256]{1,0:T(8,128)S(1)}, f32[264,256]{1,0:T(8,128)S(1)}, u32[]{:S(2)}, u32[]{:S(2)}) collective-permute-start(f32[264,256]{1,0:T(8,128)S(1)} %pair_rows.1.refs_2_.refs_8_), channel_id=1, source_target_pairs={{0,6},{1,7},{2,0},{3,1},{4,2},{5,3},{6,4},{7,5},{8,14},{9,15},{10,... | collective-permute-start | bytes 811016 | tf_op jit(solution)/shard_map/ppermute | solution.py:65
  17.8 9.5 %collective-permute-start.6 = (f32[136,256]{1,0:T(8,128)S(1)}, f32[136,256]{1,0:T(8,128)S(1)}, u32[]{:S(2)}, u32[]{:S(2)}) collective-permute-start(f32[136,256]{1,0:T(8,128)S(1)} %quad_cols.1.refs_5_.refs_0_.refs_12_), channel_id=1, source_target_pairs={{0,8},{8,0},{16,24},{24,16},{32,40},{40,32},{48,56},{56,48},{64,72... | collective-permute-start | bytes 417800 | tf_op jit(solution)/shard_map/ppermute | solution.py:87
  17.9 15.5 %collective-permute-start.8 = (f32[136,256]{1,0:T(8,128)S(1)}, f32[136,256]{1,0:T(8,128)S(1)}, u32[]{:S(2)}, u32[]{:S(2)}) collective-permute-start(f32[136,256]{1,0:T(8,128)S(1)} %quad_cols.1.refs_5_.refs_0_.refs_12_), channel_id=1, source_target_pairs={{0,64},{8,72},{16,80},{24,88},{32,96},{40,104},{48,112},{56,120},{... | collective-permute-start | bytes 417800 | tf_op jit(solution)/shard_map/ppermute | solution.py:73
  27.3 11.9 %collective-permute-start.7 = (f32[272,256]{1,0:T(8,128)S(1)}, f32[272,256]{1,0:T(8,128)S(1)}, u32[]{:S(2)}, u32[]{:S(2)}) collective-permute-start(f32[272,256]{1,0:T(8,128)S(1)} %join.1), channel_id=1, source_target_pairs={{0,32},{8,104},{16,48},{24,120},{32,64},{40,8},{48,80},{56,24},{64... | collective-permute-start | bytes 835592 | tf_op jit(solution)/shard_map/ppermute | solution.py:79
  39.3 2.9 %collective-permute-start.9 = (f32[408,256]{1,0:T(8,128)S(1)}, f32[408,256]{1,0:T(8,128)S(1)}, u32[]{:S(2)}, u32[]{:S(2)}) collective-permute-start(f32[408,256]{1,0:T(8,128)S(1)} %arrived.1), channel_id=1, source_target_pairs={{0,8},{8,0},{16,24},{24,16},{32,40},{40,32},{48,56},{56,48},{64,72... | collective-permute-start | bytes 1253384 | tf_op jit(solution)/shard_map/ppermute | solution.py:87
  44.6 2.4 %collective-permute-start.14 = (f32[512,256]{1,0:T(8,128)S(1)}, f32[512,256]{1,0:T(8,128)S(1)}, u32[]{:S(2)}, u32[]{:S(2)}) collective-permute-start(f32[512,256]{1,0:T(8,128)S(1)} %get-tuple-element.76), channel_id=1, source_target_pairs={{0,8},{8,0},{16,24},{24,16},{32,40},{40,32},{48,56},{56,48},{64,72... | collective-permute-start | bytes 1572872 | tf_op jit(solution)/shard_map/ppermute | solution.py:87
  47.0 26.9 %copy-start = (f32[1,128,256]{2,1,0:T(8,128)S(1)}, f32[1,128,256]{2,1,0:T(8,128)}, u32[]{:S(2)}) copy-start(f32[1,128,256]{2,1,0:T(8,128)} %param.11) | copy-start | bytes 393220
  47.0 26.9 %copy-start.1 = (f32[1,32,256]{2,1,0:T(8,128)S(1)}, f32[1,32,256]{2,1,0:T(8,128)}, u32[]{:S(2)}) copy-start(f32[1,32,256]{2,1,0:T(8,128)} %param.12) | copy-start | bytes 98308
  47.1 11.3 %collective-permute-start.16 = (f32[256,256]{1,0:T(8,128)S(1)}, f32[256,256]{1,0:T(8,128)S(1)}, u32[]{:S(2)}, u32[]{:S(2)}) collective-permute-start(f32[256,256]{1,0:T(8,128)S(1)} %get-tuple-element.79), channel_id=1, source_target_pairs={{0,96},{8,40},{16,112},{24,56},{32,0},{40,72},{48,16},{56,88},{64,... | collective-permute-start | bytes 786440 | tf_op jit(solution)/shard_map/ppermute | solution.py:79
  49.6 9.2 %collective-permute-start.10 = (f32[256,256]{1,0:T(8,128)S(1)}, f32[256,256]{1,0:T(8,128)S(1)}, u32[]{:S(2)}, u32[]{:S(2)}) collective-permute-start(f32[256,256]{1,0:T(8,128)S(1)} %get-tuple-element.70), channel_id=1, source_target_pairs={{0,6},{1,7},{2,0},{3,1},{4,2},{5,3},{6,4},{7,5},{8,14},{9,15},{10,... | collective-permute-start | bytes 786440 | tf_op jit(solution)/shard_map/ppermute | solution.py:65
  49.6 10.8 %collective-permute-start.11 = (f32[256,256]{1,0:T(8,128)S(1)}, f32[256,256]{1,0:T(8,128)S(1)}, u32[]{:S(2)}, u32[]{:S(2)}) collective-permute-start(f32[256,256]{1,0:T(8,128)S(1)} %get-tuple-element.71), channel_id=1, source_target_pairs={{0,4},{1,5},{2,6},{3,7},{4,0},{5,1},{6,2},{7,3},{8,12},{9,13},{10,... | collective-permute-start | bytes 786440 | tf_op jit(solution)/shard_map/ppermute | solution.py:65
  52.3 12.2 %collective-permute-start.12 = (f32[256,256]{1,0:T(8,128)S(1)}, f32[256,256]{1,0:T(8,128)S(1)}, u32[]{:S(2)}, u32[]{:S(2)}) collective-permute-start(f32[256,256]{1,0:T(8,128)S(1)} %get-tuple-element.72), channel_id=1, source_target_pairs={{0,2},{1,3},{2,4},{3,5},{4,6},{5,7},{6,0},{7,1},{8,10},{9,11},{10,... | collective-permute-start | bytes 786440 | tf_op jit(solution)/shard_map/ppermute | solution.py:65
  52.3 13.2 %collective-permute-start.15 = (f32[128,256]{1,0:T(8,128)S(1)}, f32[128,256]{1,0:T(8,128)S(1)}, u32[]{:S(2)}, u32[]{:S(2)}) collective-permute-start(f32[128,256]{1,0:T(8,128)S(1)} %get-tuple-element.78), channel_id=1, source_target_pairs={{0,64},{8,72},{16,80},{24,88},{32,96},{40,104},{48,112},{56,120},{... | collective-permute-start | bytes 393224 | tf_op jit(solution)/shard_map/ppermute | solution.py:73
  58.5 7.0 %collective-permute-start.17 = (f32[128,256]{1,0:T(8,128)S(1)}, f32[128,256]{1,0:T(8,128)S(1)}, u32[]{:S(2)}, u32[]{:S(2)}) collective-permute-start(f32[128,256]{1,0:T(8,128)S(1)} %slice.4), channel_id=1, source_target_pairs={{0,8},{8,0},{16,24},{24,16},{32,40},{40,32},{48,56},{56,48},{64,72... | collective-permute-start | bytes 393224 | tf_op jit(solution)/shard_map/ppermute | solution.py:87
  64.6 7.0 %collective-permute-start.13 = (f32[128,256]{1,0:T(8,128)S(1)}, f32[128,256]{1,0:T(8,128)S(1)}, u32[]{:S(2)}, u32[]{:S(2)}) collective-permute-start(f32[128,256]{1,0:T(8,128)S(1)} %get-tuple-element.74), channel_id=1, source_target_pairs={{0,1},{1,0},{2,3},{3,2},{4,5},{5,4},{6,7},{7,6},{8,9},{9,8},{10,11... | collective-permute-start | bytes 393224 | tf_op jit(solution)/shard_map/ppermute | solution.py:69
  65.5 4.4 %collective-permute-start.18 = (f32[64,256]{1,0:T(8,128)S(1)}, f32[64,256]{1,0:T(8,128)S(1)}, u32[]{:S(2)}, u32[]{:S(2)}) collective-permute-start(f32[64,256]{1,0:T(8,128)S(1)} %get-tuple-element.81), channel_id=1, source_target_pairs={{0,16},{8,24},{16,0},{24,8},{32,48},{40,56},{48,32},{56,40},{64,80... | collective-permute-start | bytes 196616 | tf_op jit(solution)/shard_map/ppermute | solution.py:87
  69.9 4.0 %collective-permute-start.19 = (f32[32,256]{1,0:T(8,128)S(1)}, f32[32,256]{1,0:T(8,128)S(1)}, u32[]{:S(2)}, u32[]{:S(2)}) collective-permute-start(f32[32,256]{1,0:T(8,128)S(1)} %get-tuple-element.83), channel_id=1, source_target_pairs={{0,128},{8,136},{16,144},{24,152},{32,160},{40,168},{48,176},{56,1... | collective-permute-start | bytes 98312 | tf_op jit(solution)/shard_map/ppermute | solution.py:87

commit v5 on v4

--- a/solution.py
+++ b/solution.py
@@ -188,13 +188,6 @@
     h = slice(512 * half, 512 * (half + 1))
     for k in range(4):
         s = slice(T * k, T * (k + 1))
-        if half == 0:
-            br = left[k][256:264, :128].T
-            bvs[s, :] = jnp.concatenate([br[:, 0:1], br[:, 1:2]], 0)
-            lh, ll = split(left[k][:256, :])
-            lcat[s, :D] = lh
-            lcat[s, D:] = ll
-            ltr[:, s] = jnp.concatenate([lh, ll], 1).T
         lh, ll = lcat[s, :D], lcat[s, D:]
         score = dot(lh, rcat[:, :D], NT) + dot(lh, rcat[:, D:], NT) + dot(ll, rcat[:, :D], NT)
         d = score + bvs[s, :] + bc[...] - lx[k][:, h]
@@ -208,13 +201,25 @@
     return cc.T
 
 
+def lefts_body(*refs):
+    left, (lcat, ltr, bvs) = refs[:4], refs[4:]
+    for k in range(4):
+        s = slice(T * k, T * (k + 1))
+        br = left[k][256:264, :128].T
+        bvs[s, :] = jnp.concatenate([br[:, 0:1], br[:, 1:2]], 0)
+        lh, ll = split(left[k][:256, :])
+        lcat[s, :D] = lh
+        lcat[s, D:] = ll
+        ltr[:, s] = jnp.concatenate([lh, ll], 1).T
+
+
 def own_body(*refs):
-    w, lx, left = refs[:4], refs[4:8], refs[8:12]
-    near, beside, first = refs[12:15]
-    gh, gl, rcat, col, lcat, ltr, bvs = refs[15:22]
-    (bc,) = refs[22:]
+    w, lx, saved = refs[:4], refs[4:8], refs[8:11]
+    near, beside, first = refs[11:14]
+    gh, gl, rcat, col = refs[14:18]
+    (bc,) = refs[18:]
     right = [(near, 0), (beside, 0), (first, 0), (first, 136)]
-    col[...] = half_body(w, lx, left, right, (lcat, ltr, bvs), (gh, gl, rcat), bc, half=0)
+    col[...] = half_body(w, lx, None, right, saved, (gh, gl, rcat), bc, half=0)
 
 
 def other_body(sums, right, *refs):
@@ -351,18 +356,21 @@
 
     scratch = [pltpu.VMEM((1, 512), F32)]
     half_out = [bf16(N, 512), bf16(N, 512), bf16(512, 2 * D)]
-    gh1, gl1, r1, col1, *saved = call(
+    saved = call(
+        lefts_body, "lefts", [bf16(N, 2 * D), bf16(2 * D, N), f32(N, 1)], left, vmem_mb=24
+    )
+    gh1, gl1, r1, col1 = call(
         own_body,
         "own",
-        half_out + [f32(512, D), bf16(N, 2 * D), bf16(2 * D, N), f32(N, 1)],
-        [*w, *lx, *left, cols, beside, first],
+        half_out + [f32(512, D)],
+        [*w, *lx, *saved, cols, beside, first],
         after=[far] * CFG["ownfar"],
         flops=CFG["kf"],
         scratch=scratch,
         vmem_mb=24,
     )
     if CFG["mc"]:
-        give = relay("arrived", [first, far], [w[k] for k in CFG["cr"]] + left[1:] * CFG["y1"] + [gh1] * CFG["ao"])
+        give = relay("arrived", [first, far], [w[k] for k in CFG["cr"]] + left[1:] * CFG["y1"] + [saved[0]])
         second = swap_gr(give, CORE)
         crossed = [second, far]
         spots = [(0, 136), (0, 0), (1, 0), (0, 272)]

time: 74.7 us -> 74.4 us (level)
    pallas_call x19 -> x20, Pallas kernels: 20.5 us -> 20.8 us  [call(): pl.pallas_call(run, out_shape=out_shape, in_specs=[SMEM] * smem + [HBM] *...]
where the time goes in v5:
time: 74.4 us; the launch traced here: 74.3 us
  starting transfers between devices  30.4 us (41%)
  waiting for transfers between devices  21.5 us (29%)
  Pallas kernels  20.8 us (28%)
  between operations  1.53 us (2%)
    pallas_call x20, Pallas kernels, call(): pl.pallas_call(run, out_shape=out_shape, in_specs=[SMEM] * smem + [HBM] *...  20.8 us
    ppermute x2, starting transfers between devices, move_z(): lax.ppermute(x, 'gr', [(i, i & 17 | ((i >> 1 & 7) + k) % 8 << 1) for i in...  10.7 us
    ppermute x6, starting transfers between devices, move_y(): return lax.ppermute(x, 'gc', [(i, (i + 2 * k) % 8) for i in range(8)])  8.65 us
    ppermute x2, waiting for transfers between devices, move_z_by_core(): lax.ppermute(x, 'gr', [(i, i & 17 | ((i >> 1 & 7) + (-k if i & 1 else k))...  7.98 us
    ppermute x8, waiting for transfers between devices, swap_gr(): return lax.ppermute(x, 'gr', [(i, i ^ mask) for i in range(32)])  6.49 us
    ppermute x6, waiting for transfers between devices, move_y(): return lax.ppermute(x, 'gc', [(i, (i + 2 * k) % 8) for i in range(8)])  5.95 us
    ppermute x2, starting transfers between devices, move_z_by_core(): lax.ppermute(x, 'gr', [(i, i & 17 | ((i >> 1 & 7) + (-k if i & 1 else k))...  4.19 us
    ppermute x2, starting transfers between devices, swap_x_hi(): return lax.ppermute(x, 'gc', [(i, i ^ 1) for i in range(8)])  3.61 us
  transfers between devices with their start and end apart: 20, of which 8 were waited for; matrix products, arithmetic and copies ran while one was open for 0% of the time, Pallas kernels for 22%

profile of v5, /device:TPU:32, one launch (start us, length us, event | category | flops | bytes accessed | tf_op | source)
XLA Modules:
  0.0 74.3 jit_solution(1164672514423173491)
XLA Ops:
  1.3 1.0 %pack.1 = (f32[136,256]{1,0:T(8,128)S(1)}, f32[40,256]{1,0:T(8,128)S(1)}) custom-call(s32[1]{0:T(128)S(6)} %copy.10.refs_0_, f32[128,256]{1,0:T(8,128)} %bitcast.7, f32[32,256]{1,0:T(8,128)} %bitcast.9, s32[1,128]{1,0:T(1,128)} %refs_3_.1, s32[1,32]{1,0:T(1,128)} %refs_4_.1), custom_call_target="tpu_custom_call" | custom-call | bytes 65536 | tf_op jit(solution)/shard_map/pack/pallas_call | solution.py:43
  2.3 1.6 %collective-permute-start = (f32[40,256]{1,0:T(8,128)S(1)}, f32[40,256]{1,0:T(8,128)S(1)}, u32[]{:S(2)}, u32[]{:S(2)}) collective-permute-start(f32[40,256]{1,0:T(8,128)S(1)} %get-tuple-element.49.refs_0_), channel_id=1, source_target_pairs={{0,128},{8,136},{16,144},{24,152},{32,160},{40,168},{48,176},{56,1... | collective-permute-start | bytes 122888 | tf_op jit(solution)/shard_map/ppermute | solution.py:87
  3.9 2.7 %collective-permute-start.2 = (f32[136,256]{1,0:T(8,128)S(1)}, f32[136,256]{1,0:T(8,128)S(1)}, u32[]{:S(2)}, u32[]{:S(2)}) collective-permute-start(f32[136,256]{1,0:T(8,128)S(1)} %get-tuple-element.51.refs_0_), channel_id=1, source_target_pairs={{0,1},{1,0},{2,3},{3,2},{4,5},{5,4},{6,7},{7,6},{8,9},{9,8},{10,11... | collective-permute-start | bytes 417800 | tf_op jit(solution)/shard_map/ppermute | solution.py:69
  6.6 2.8 %digits.1 = (f8e4m3fn[1024,1024]{1,0:T(32,128)(4,1)S(1)}, f8e4m3fn[1024,1024]{1,0:T(32,128)(4,1)S(1)}, f8e4m3fn[1024,1024]{1,0:T(32,128)(4,1)S(1)}, f8e4m3fn[102...) custom-call(s32[1024,1024]{1,0:T(8,128)} %bitcast.11, s32[1,1024]{1,0:T(1,128)} %bitcast.12, s32[1,1024]{1,0:T(1,128)} %bitcast.13), custom_call_target="tpu_custom_call" | custom-call | bytes 65536 | tf_op jit(solution)/shard_map/digits/pallas_call | solution.py:43
  9.4 0.1 pair_cols.1.refs_5_.refs_0_
  9.5 0.1 collective-permute-start.1
  9.6 2.2 %order0.1 = (f32[256,1024]{1,0:T(8,128)S(1)}, f32[256,1024]{1,0:T(8,128)S(1)}) custom-call(f8e4m3fn[1024,1024]{1,0:T(32,128)(4,1)S(1)} %get-tuple-element.44.refs_2_.refs_0_, f8e4m3fn[1024,1024]{1,0:T(32,128)(4,1)S(1)} %get-tuple-element.45.refs_1_, f8e4m3fn[1024,1024]{1,0:T(32,128)(4,1)S(1)} %get-tuple-element.46.refs_2_, ...), custom_call_target="tpu_custom_call" | custom-call | flops 2147483648 | bytes 65536 | tf_op jit(solution)/shard_map/order0/pallas_call | solution.py:43
  11.8 0.0 collective-permute-done.2.refs_1_
  11.8 1.7 %collective-permute-start.3 = (f32[264,256]{1,0:T(8,128)S(1)}, f32[264,256]{1,0:T(8,128)S(1)}, u32[]{:S(2)}, u32[]{:S(2)}) collective-permute-start(f32[264,256]{1,0:T(8,128)S(1)} %pair_rows.1.refs_2_.refs_0_), channel_id=1, source_target_pairs={{0,2},{1,3},{2,4},{3,5},{4,6},{5,7},{6,0},{7,1},{8,10},{9,11},{10,... | collective-permute-start | bytes 811016 | tf_op jit(solution)/shard_map/ppermute | solution.py:65
  13.5 2.9 %collective-permute-start.4 = (f32[264,256]{1,0:T(8,128)S(1)}, f32[264,256]{1,0:T(8,128)S(1)}, u32[]{:S(2)}, u32[]{:S(2)}) collective-permute-start(f32[264,256]{1,0:T(8,128)S(1)} %pair_rows.1.refs_2_.refs_0_), channel_id=1, source_target_pairs={{0,4},{1,5},{2,6},{3,7},{4,0},{5,1},{6,2},{7,3},{8,12},{9,13},{10,... | collective-permute-start | bytes 811016 | tf_op jit(solution)/shard_map/ppermute | solution.py:65
  16.4 1.3 %collective-permute-start.5 = (f32[264,256]{1,0:T(8,128)S(1)}, f32[264,256]{1,0:T(8,128)S(1)}, u32[]{:S(2)}, u32[]{:S(2)}) collective-permute-start(f32[264,256]{1,0:T(8,128)S(1)} %pair_rows.1.refs_2_.refs_0_), channel_id=1, source_target_pairs={{0,6},{1,7},{2,0},{3,1},{4,2},{5,3},{6,4},{7,5},{8,14},{9,15},{10,... | collective-permute-start | bytes 811016 | tf_op jit(solution)/shard_map/ppermute | solution.py:65
  17.7 0.1 quad_cols.1.refs_5_.refs_0_.refs_11_
  17.8 0.0 collective-permute-start.6
  17.9 7.3 %collective-permute-start.8 = (f32[136,256]{1,0:T(8,128)S(1)}, f32[136,256]{1,0:T(8,128)S(1)}, u32[]{:S(2)}, u32[]{:S(2)}) collective-permute-start(f32[136,256]{1,0:T(8,128)S(1)} %quad_cols.1.refs_5_.refs_0_.refs_11_), channel_id=1, source_target_pairs={{0,64},{8,72},{16,80},{24,88},{32,96},{40,104},{48,112},{56,120},{... | collective-permute-start | bytes 417800 | tf_op jit(solution)/shard_map/ppermute | solution.py:73
  25.1 2.2 %order1.1 = (f32[256,1024]{1,0:T(8,128)S(1)}, f32[256,1024]{1,0:T(8,128)S(1)}) custom-call(f8e4m3fn[1024,1024]{1,0:T(32,128)(4,1)S(1)} %get-tuple-element.44.refs_2_.refs_0_, f8e4m3fn[1024,1024]{1,0:T(32,128)(4,1)S(1)} %get-tuple-element.45.refs_1_, f8e4m3fn[1024,1024]{1,0:T(32,128)(4,1)S(1)} %get-tuple-element.46.refs_2_, ...), custom_call_target="tpu_custom_call" | custom-call | flops 2147483648 | bytes 65536 | tf_op jit(solution)/shard_map/order1/pallas_call | solution.py:43
  27.4 1.7 %collective-permute-start.7 = (f32[272,256]{1,0:T(8,128)S(1)}, f32[272,256]{1,0:T(8,128)S(1)}, u32[]{:S(2)}, u32[]{:S(2)}) collective-permute-start(f32[272,256]{1,0:T(8,128)S(1)} %join.1), channel_id=1, source_target_pairs={{0,32},{8,104},{16,48},{24,120},{32,64},{40,8},{48,80},{56,24},{64... | collective-permute-start | bytes 835592 | tf_op jit(solution)/shard_map/ppermute | solution.py:79
  29.1 2.2 %order3.1 = (f32[256,1024]{1,0:T(8,128)S(1)}, f32[256,1024]{1,0:T(8,128)S(1)}) custom-call(f8e4m3fn[1024,1024]{1,0:T(32,128)(4,1)S(1)} %get-tuple-element.44.refs_2_.refs_0_, f8e4m3fn[1024,1024]{1,0:T(32,128)(4,1)S(1)} %get-tuple-element.45.refs_1_, f8e4m3fn[1024,1024]{1,0:T(32,128)(4,1)S(1)} %get-tuple-element.46.refs_2_, ...), custom_call_target="tpu_custom_call" | custom-call | flops 2147483648 | bytes 65536 | tf_op jit(solution)/shard_map/order3/pallas_call | solution.py:43
  31.3 2.2 %order2.1 = (f32[256,1024]{1,0:T(8,128)S(1)}, f32[256,1024]{1,0:T(8,128)S(1)}) custom-call(f8e4m3fn[1024,1024]{1,0:T(32,128)(4,1)S(1)} %get-tuple-element.44.refs_2_.refs_0_, f8e4m3fn[1024,1024]{1,0:T(32,128)(4,1)S(1)} %get-tuple-element.45.refs_1_, f8e4m3fn[1024,1024]{1,0:T(32,128)(4,1)S(1)} %get-tuple-element.46.refs_2_, ...), custom_call_target="tpu_custom_call" | custom-call | flops 1073741824 | bytes 65536 | tf_op jit(solution)/shard_map/order2/pallas_call | solution.py:43
  33.5 0.0 collective-permute-done.3.refs_1_.refs_3_
  33.5 0.0 collective-permute-done.4.refs_2_.refs_4_
  33.5 0.5 lefts.1
  34.0 0.0 collective-permute-done.8.refs_1_.refs_9_
  34.0 5.2 %collective-permute-done.7.refs_13_.refs_0_ = f32[272,256]{1,0:T(8,128)S(1)} collective-permute-done((f32[272,256]{1,0:T(8,128)S(1)}, f32[272,256]{1,0:T(8,128)S(1)}, u32[]{:S(2)}, u32[]{:S(2)}) %collective-permute-start.7) | collective-permute-done | bytes 278560 | tf_op jit(solution)/shard_map/ppermute | solution.py:79
  39.3 0.1 collective-permute-start.9
  39.4 2.5 %own.1 = (bf16[1024,512]{1,0:T(8,128)(2,1)S(1)}, bf16[1024,512]{1,0:T(8,128)(2,1)S(1)}, bf16[512,512]{1,0:T(8,128)(2,1)S(1)}, f32[512,256]{1,0:T(8,128)S(1)}) custom-call(f32[256,1024]{1,0:T(8,128)S(1)} %get-tuple-element.50.refs_3_.refs_0_, f32[256,1024]{1,0:T(8,128)S(1)} %get-tuple-element.52.refs_1_.refs_2_, f32[256,1024]{1,0:T(8,128)S(1)} %get-tuple-element.53.refs_2_, ...), custom_call_target="tpu_custom_call" | custom-call | flops 8589934592 | bytes 65536 | tf_op jit(solution)/shard_map/own/pallas_call | solution.py:43
  41.9 0.0 collective-permute-done.9.refs_8_
  41.9 2.5 %other.1 = (bf16[1024,512]{1,0:T(8,128)(2,1)S(1)}, bf16[1024,512]{1,0:T(8,128)(2,1)S(1)}, bf16[512,512]{1,0:T(8,128)(2,1)S(1)}, f32[128,256]{1,0:T(8,128)S(1)}, f32[512,256]{1,0:T(8,128)S(1)}) custom-call(f32[256,1024]{1,0:T(8,128)S(1)} %get-tuple-element.50.refs_3_.refs_0_, f32[256,1024]{1,0:T(8,128)S(1)} %get-tuple-element.52.refs_1_.refs_2_, ...), custom_call_target="tpu_custom_call" | custom-call | flops 4294967296 | bytes 65536 | tf_op jit(solution)/shard_map/other/pallas_call | solution.py:43
  44.4 0.6 collective-permute-start.14
  44.9 1.8 %rows.1 = (f32[256,256]{1,0:T(8,128)S(1)}, f32[256,256]{1,0:T(8,128)S(1)}, f32[256,256]{1,0:T(8,128)S(1)}, f32[256,256]{1,0:T(8,128)S(1)}) custom-call(bf16[1024,512]{1,0:T(8,128)(2,1)S(1)} %get-tuple-element.62.refs_0_, bf16[1024,512]{1,0:T(8,128)(2,1)S(1)} %get-tuple-element.63.refs_1_, bf16[512,512]{1,0:T(8,128)(2,1)S(1)} %get-tuple-element.64.refs_2_, ...), custom_call_target="tpu_custom_call" | custom-call | flops 17179869184 | bytes 65536 | tf_op jit(solution)/shard_map/rows/pallas_call | solution.py:43
  46.7 0.0 copy-start
  46.7 0.0 copy-start.1
  46.7 0.1 quarters.1
  46.8 2.5 %collective-permute-start.16 = (f32[256,256]{1,0:T(8,128)S(1)}, f32[256,256]{1,0:T(8,128)S(1)}, u32[]{:S(2)}, u32[]{:S(2)}) collective-permute-start(f32[256,256]{1,0:T(8,128)S(1)} %get-tuple-element.79), channel_id=1, source_target_pairs={{0,96},{8,40},{16,112},{24,56},{32,0},{40,72},{48,16},{56,88},{64,... | collective-permute-start | bytes 786440 | tf_op jit(solution)/shard_map/ppermute | solution.py:79
  49.3 0.0 collective-permute-start.10
  49.3 2.7 %collective-permute-start.11 = (f32[256,256]{1,0:T(8,128)S(1)}, f32[256,256]{1,0:T(8,128)S(1)}, u32[]{:S(2)}, u32[]{:S(2)}) collective-permute-start(f32[256,256]{1,0:T(8,128)S(1)} %get-tuple-element.71), channel_id=1, source_target_pairs={{0,4},{1,5},{2,6},{3,7},{4,0},{5,1},{6,2},{7,3},{8,12},{9,13},{10,... | collective-permute-start | bytes 786440 | tf_op jit(solution)/shard_map/ppermute | solution.py:65
  52.0 3.4 %collective-permute-start.15 = (f32[128,256]{1,0:T(8,128)S(1)}, f32[128,256]{1,0:T(8,128)S(1)}, u32[]{:S(2)}, u32[]{:S(2)}) collective-permute-start(f32[128,256]{1,0:T(8,128)S(1)} %get-tuple-element.78), channel_id=1, source_target_pairs={{0,64},{8,72},{16,80},{24,88},{32,96},{40,104},{48,112},{56,120},{... | collective-permute-start | bytes 393224 | tf_op jit(solution)/shard_map/ppermute | solution.py:73
  55.4 2.8 %collective-permute-done.16.refs_2_ = f32[256,256]{1,0:T(8,128)S(1)} collective-permute-done((f32[256,256]{1,0:T(8,128)S(1)}, f32[256,256]{1,0:T(8,128)S(1)}, u32[]{:S(2)}, u32[]{:S(2)}) %collective-permute-start.16) | collective-permute-done | bytes 262176 | tf_op jit(solution)/shard_map/ppermute | solution.py:79
  58.2 0.1 collective-permute-start.17
  58.3 0.2 collective-permute-done.10.refs_1_
  58.5 1.6 %collective-permute-done.11.refs_2_ = f32[256,256]{1,0:T(8,128)S(1)} collective-permute-done((f32[256,256]{1,0:T(8,128)S(1)}, f32[256,256]{1,0:T(8,128)S(1)}, u32[]{:S(2)}, u32[]{:S(2)}) %collective-permute-start.11) | collective-permute-done | bytes 262176 | tf_op jit(solution)/shard_map/ppermute | solution.py:65
  60.0 4.2 %collective-permute-done.12.refs_3_ = f32[256,256]{1,0:T(8,128)S(1)} collective-permute-done((f32[256,256]{1,0:T(8,128)S(1)}, f32[256,256]{1,0:T(8,128)S(1)}, u32[]{:S(2)}, u32[]{:S(2)}) %collective-permute-start.12) | collective-permute-done | bytes 262176 | tf_op jit(solution)/shard_map/ppermute | solution.py:65
  64.3 0.9 %collective-permute-start.13 = (f32[128,256]{1,0:T(8,128)S(1)}, f32[128,256]{1,0:T(8,128)S(1)}, u32[]{:S(2)}, u32[]{:S(2)}) collective-permute-start(f32[128,256]{1,0:T(8,128)S(1)} %get-tuple-element.74), channel_id=1, source_target_pairs={{0,1},{1,0},{2,3},{3,2},{4,5},{5,4},{6,7},{7,6},{8,9},{9,8},{10,11... | collective-permute-start | bytes 393224 | tf_op jit(solution)/shard_map/ppermute | solution.py:69
  65.2 0.2 collective-permute-start.18
  65.4 4.2 %collective-permute-done.18.refs_1_ = f32[64,256]{1,0:T(8,128)S(1)} collective-permute-done((f32[64,256]{1,0:T(8,128)S(1)}, f32[64,256]{1,0:T(8,128)S(1)}, u32[]{:S(2)}, u32[]{:S(2)}) %collective-permute-start.18) | collective-permute-done | bytes 65568 | tf_op jit(solution)/shard_map/ppermute | solution.py:87
  69.6 0.6 collective-permute-start.19
  70.2 1.1 %collective-permute-done.13.refs_2_ = f32[128,256]{1,0:T(8,128)S(1)} collective-permute-done((f32[128,256]{1,0:T(8,128)S(1)}, f32[128,256]{1,0:T(8,128)S(1)}, u32[]{:S(2)}, u32[]{:S(2)}) %collective-permute-start.13) | collective-permute-done | bytes 131104 | tf_op jit(solution)/shard_map/ppermute | solution.py:69
  71.3 2.3 %collective-permute-done.19.refs_5_ = f32[32,256]{1,0:T(8,128)S(1)} collective-permute-done((f32[32,256]{1,0:T(8,128)S(1)}, f32[32,256]{1,0:T(8,128)S(1)}, u32[]{:S(2)}, u32[]{:S(2)}) %collective-permute-start.19) | collective-permute-done | bytes 32800 | tf_op jit(solution)/shard_map/ppermute | solution.py:87
  73.6 0.7 last.1
  (17 shorter events, 0.2 us)
Async XLA Ops:
  2.3 7.1 %collective-permute-start = (f32[40,256]{1,0:T(8,128)S(1)}, f32[40,256]{1,0:T(8,128)S(1)}, u32[]{:S(2)}, u32[]{:S(2)}) collective-permute-start(f32[40,256]{1,0:T(8,128)S(1)} %get-tuple-element.49.refs_0_), channel_id=1, source_target_pairs={{0,128},{8,136},{16,144},{24,152},{32,160},{40,168},{48,176},{56,1... | collective-permute-start | bytes 122888 | tf_op jit(solution)/shard_map/ppermute | solution.py:87
  3.9 8.0 %collective-permute-start.2 = (f32[136,256]{1,0:T(8,128)S(1)}, f32[136,256]{1,0:T(8,128)S(1)}, u32[]{:S(2)}, u32[]{:S(2)}) collective-permute-start(f32[136,256]{1,0:T(8,128)S(1)} %get-tuple-element.51.refs_0_), channel_id=1, source_target_pairs={{0,1},{1,0},{2,3},{3,2},{4,5},{5,4},{6,7},{7,6},{8,9},{9,8},{10,11... | collective-permute-start | bytes 417800 | tf_op jit(solution)/shard_map/ppermute | solution.py:69
  9.5 8.3 %collective-permute-start.1 = (f32[72,256]{1,0:T(8,128)S(1)}, f32[72,256]{1,0:T(8,128)S(1)}, u32[]{:S(2)}, u32[]{:S(2)}) collective-permute-start(f32[72,256]{1,0:T(8,128)S(1)} %pair_cols.1.refs_5_.refs_0_), channel_id=1, source_target_pairs={{0,16},{8,24},{16,0},{24,8},{32,48},{40,56},{48,32},{56,40},{64,80... | collective-permute-start | bytes 221192 | tf_op jit(solution)/shard_map/ppermute | solution.py:87
  11.8 21.6 %collective-permute-start.3 = (f32[264,256]{1,0:T(8,128)S(1)}, f32[264,256]{1,0:T(8,128)S(1)}, u32[]{:S(2)}, u32[]{:S(2)}) collective-permute-start(f32[264,256]{1,0:T(8,128)S(1)} %pair_rows.1.refs_2_.refs_0_), channel_id=1, source_target_pairs={{0,2},{1,3},{2,4},{3,5},{4,6},{5,7},{6,0},{7,1},{8,10},{9,11},{10,... | collective-permute-start | bytes 811016 | tf_op jit(solution)/shard_map/ppermute | solution.py:65
  13.5 20.0 %collective-permute-start.4 = (f32[264,256]{1,0:T(8,128)S(1)}, f32[264,256]{1,0:T(8,128)S(1)}, u32[]{:S(2)}, u32[]{:S(2)}) collective-permute-start(f32[264,256]{1,0:T(8,128)S(1)} %pair_rows.1.refs_2_.refs_0_), channel_id=1, source_target_pairs={{0,4},{1,5},{2,6},{3,7},{4,0},{5,1},{6,2},{7,3},{8,12},{9,13},{10,... | collective-permute-start | bytes 811016 | tf_op jit(solution)/shard_map/ppermute | solution.py:65
  16.4 17.1 %collective-permute-start.5 = (f32[264,256]{1,0:T(8,128)S(1)}, f32[264,256]{1,0:T(8,128)S(1)}, u32[]{:S(2)}, u32[]{:S(2)}) collective-permute-start(f32[264,256]{1,0:T(8,128)S(1)} %pair_rows.1.refs_2_.refs_0_), channel_id=1, source_target_pairs={{0,6},{1,7},{2,0},{3,1},{4,2},{5,3},{6,4},{7,5},{8,14},{9,15},{10,... | collective-permute-start | bytes 811016 | tf_op jit(solution)/shard_map/ppermute | solution.py:65
  17.8 9.5 %collective-permute-start.6 = (f32[136,256]{1,0:T(8,128)S(1)}, f32[136,256]{1,0:T(8,128)S(1)}, u32[]{:S(2)}, u32[]{:S(2)}) collective-permute-start(f32[136,256]{1,0:T(8,128)S(1)} %quad_cols.1.refs_5_.refs_0_.refs_11_), channel_id=1, source_target_pairs={{0,8},{8,0},{16,24},{24,16},{32,40},{40,32},{48,56},{56,48},{64,72... | collective-permute-start | bytes 417800 | tf_op jit(solution)/shard_map/ppermute | solution.py:87
  17.9 16.2 %collective-permute-start.8 = (f32[136,256]{1,0:T(8,128)S(1)}, f32[136,256]{1,0:T(8,128)S(1)}, u32[]{:S(2)}, u32[]{:S(2)}) collective-permute-start(f32[136,256]{1,0:T(8,128)S(1)} %quad_cols.1.refs_5_.refs_0_.refs_11_), channel_id=1, source_target_pairs={{0,64},{8,72},{16,80},{24,88},{32,96},{40,104},{48,112},{56,120},{... | collective-permute-start | bytes 417800 | tf_op jit(solution)/shard_map/ppermute | solution.py:73
  27.4 11.9 %collective-permute-start.7 = (f32[272,256]{1,0:T(8,128)S(1)}, f32[272,256]{1,0:T(8,128)S(1)}, u32[]{:S(2)}, u32[]{:S(2)}) collective-permute-start(f32[272,256]{1,0:T(8,128)S(1)} %join.1), channel_id=1, source_target_pairs={{0,32},{8,104},{16,48},{24,120},{32,64},{40,8},{48,80},{56,24},{64... | collective-permute-start | bytes 835592 | tf_op jit(solution)/shard_map/ppermute | solution.py:79
  39.3 2.6 %collective-permute-start.9 = (f32[408,256]{1,0:T(8,128)S(1)}, f32[408,256]{1,0:T(8,128)S(1)}, u32[]{:S(2)}, u32[]{:S(2)}) collective-permute-start(f32[408,256]{1,0:T(8,128)S(1)} %arrived.1), channel_id=1, source_target_pairs={{0,8},{8,0},{16,24},{24,16},{32,40},{40,32},{48,56},{56,48},{64,72... | collective-permute-start | bytes 1253384 | tf_op jit(solution)/shard_map/ppermute | solution.py:87
  44.4 2.4 %collective-permute-start.14 = (f32[512,256]{1,0:T(8,128)S(1)}, f32[512,256]{1,0:T(8,128)S(1)}, u32[]{:S(2)}, u32[]{:S(2)}) collective-permute-start(f32[512,256]{1,0:T(8,128)S(1)} %get-tuple-element.76), channel_id=1, source_target_pairs={{0,8},{8,0},{16,24},{24,16},{32,40},{40,32},{48,56},{56,48},{64,72... | collective-permute-start | bytes 1572872 | tf_op jit(solution)/shard_map/ppermute | solution.py:87
  46.7 26.9 %copy-start = (f32[1,128,256]{2,1,0:T(8,128)S(1)}, f32[1,128,256]{2,1,0:T(8,128)}, u32[]{:S(2)}) copy-start(f32[1,128,256]{2,1,0:T(8,128)} %param.11) | copy-start | bytes 393220
  46.7 26.9 %copy-start.1 = (f32[1,32,256]{2,1,0:T(8,128)S(1)}, f32[1,32,256]{2,1,0:T(8,128)}, u32[]{:S(2)}) copy-start(f32[1,32,256]{2,1,0:T(8,128)} %param.12) | copy-start | bytes 98308
  46.8 11.4 %collective-permute-start.16 = (f32[256,256]{1,0:T(8,128)S(1)}, f32[256,256]{1,0:T(8,128)S(1)}, u32[]{:S(2)}, u32[]{:S(2)}) collective-permute-start(f32[256,256]{1,0:T(8,128)S(1)} %get-tuple-element.79), channel_id=1, source_target_pairs={{0,96},{8,40},{16,112},{24,56},{32,0},{40,72},{48,16},{56,88},{64,... | collective-permute-start | bytes 786440 | tf_op jit(solution)/shard_map/ppermute | solution.py:79
  49.3 9.2 %collective-permute-start.10 = (f32[256,256]{1,0:T(8,128)S(1)}, f32[256,256]{1,0:T(8,128)S(1)}, u32[]{:S(2)}, u32[]{:S(2)}) collective-permute-start(f32[256,256]{1,0:T(8,128)S(1)} %get-tuple-element.70), channel_id=1, source_target_pairs={{0,6},{1,7},{2,0},{3,1},{4,2},{5,3},{6,4},{7,5},{8,14},{9,15},{10,... | collective-permute-start | bytes 786440 | tf_op jit(solution)/shard_map/ppermute | solution.py:65
  49.3 10.8 %collective-permute-start.11 = (f32[256,256]{1,0:T(8,128)S(1)}, f32[256,256]{1,0:T(8,128)S(1)}, u32[]{:S(2)}, u32[]{:S(2)}) collective-permute-start(f32[256,256]{1,0:T(8,128)S(1)} %get-tuple-element.71), channel_id=1, source_target_pairs={{0,4},{1,5},{2,6},{3,7},{4,0},{5,1},{6,2},{7,3},{8,12},{9,13},{10,... | collective-permute-start | bytes 786440 | tf_op jit(solution)/shard_map/ppermute | solution.py:65
  52.0 12.2 %collective-permute-start.12 = (f32[256,256]{1,0:T(8,128)S(1)}, f32[256,256]{1,0:T(8,128)S(1)}, u32[]{:S(2)}, u32[]{:S(2)}) collective-permute-start(f32[256,256]{1,0:T(8,128)S(1)} %get-tuple-element.72), channel_id=1, source_target_pairs={{0,2},{1,3},{2,4},{3,5},{4,6},{5,7},{6,0},{7,1},{8,10},{9,11},{10,... | collective-permute-start | bytes 786440 | tf_op jit(solution)/shard_map/ppermute | solution.py:65
  52.0 13.2 %collective-permute-start.15 = (f32[128,256]{1,0:T(8,128)S(1)}, f32[128,256]{1,0:T(8,128)S(1)}, u32[]{:S(2)}, u32[]{:S(2)}) collective-permute-start(f32[128,256]{1,0:T(8,128)S(1)} %get-tuple-element.78), channel_id=1, source_target_pairs={{0,64},{8,72},{16,80},{24,88},{32,96},{40,104},{48,112},{56,120},{... | collective-permute-start | bytes 393224 | tf_op jit(solution)/shard_map/ppermute | solution.py:73
  58.2 7.0 %collective-permute-start.17 = (f32[128,256]{1,0:T(8,128)S(1)}, f32[128,256]{1,0:T(8,128)S(1)}, u32[]{:S(2)}, u32[]{:S(2)}) collective-permute-start(f32[128,256]{1,0:T(8,128)S(1)} %slice.4), channel_id=1, source_target_pairs={{0,8},{8,0},{16,24},{24,16},{32,40},{40,32},{48,56},{56,48},{64,72... | collective-permute-start | bytes 393224 | tf_op jit(solution)/shard_map/ppermute | solution.py:87
  64.3 7.0 %collective-permute-start.13 = (f32[128,256]{1,0:T(8,128)S(1)}, f32[128,256]{1,0:T(8,128)S(1)}, u32[]{:S(2)}, u32[]{:S(2)}) collective-permute-start(f32[128,256]{1,0:T(8,128)S(1)} %get-tuple-element.74), channel_id=1, source_target_pairs={{0,1},{1,0},{2,3},{3,2},{4,5},{5,4},{6,7},{7,6},{8,9},{9,8},{10,11... | collective-permute-start | bytes 393224 | tf_op jit(solution)/shard_map/ppermute | solution.py:69
  65.2 4.4 %collective-permute-start.18 = (f32[64,256]{1,0:T(8,128)S(1)}, f32[64,256]{1,0:T(8,128)S(1)}, u32[]{:S(2)}, u32[]{:S(2)}) collective-permute-start(f32[64,256]{1,0:T(8,128)S(1)} %get-tuple-element.81), channel_id=1, source_target_pairs={{0,16},{8,24},{16,0},{24,8},{32,48},{40,56},{48,32},{56,40},{64,80... | collective-permute-start | bytes 196616 | tf_op jit(solution)/shard_map/ppermute | solution.py:87
  69.6 4.0 %collective-permute-start.19 = (f32[32,256]{1,0:T(8,128)S(1)}, f32[32,256]{1,0:T(8,128)S(1)}, u32[]{:S(2)}, u32[]{:S(2)}) collective-permute-start(f32[32,256]{1,0:T(8,128)S(1)} %get-tuple-element.83), channel_id=1, source_target_pairs={{0,128},{8,136},{16,144},{24,152},{32,160},{40,168},{48,176},{56,1... | collective-permute-start | bytes 98312 | tf_op jit(solution)/shard_map/ppermute | solution.py:87
